TPU v7x, 32 devices: a whole 2x2x4 slice. The times are simulated.
32 devices in a mesh: grp: 16 (over z, x, core), swap: 2 (over y).
Axes of the slice: x: 2, y: 2, z: 4, core: 2. Of those that a mesh axis runs over, the one named last changes fastest.
Arguments:
- samples: bfloat16 [2, 16, 64, 4, 4096], P('swap', 'grp'), may hold values from 0.049804688 to 4
- tile_list: int32 [2, 16, 64], replicated, may hold values from 0 to 127, as said below
- tile_slot: int32 [128], replicated, may hold values from 0 to 127, as said below
- brick_rank: int32 [2, 128], replicated, may hold values from 0 to 127, each once within a row
Outputs:
- final_image: float32 [16, 8, 4, 4096], P('grp', None, None, 'swap')
Inputs may be any that keep to these rules, and one draw needn't show every extreme that they name: `tile_list`: the 64 tiles of one device are distinct; fragments b * 8 to (b + 1) * 8 - 1 of a device belong to its brick b. With owner(t) = tile_slot[t] // 8, each device has 8 tiles of each of a quarter of the owners of its group, 4 of each of half of them and none of the rest; in every slab one owner has 8 tiles from every device of the group. A permutation: tile t is row tile_slot[t] % 8 of owner tile_slot[t] // 8.
All inputs are finite; a program needn't handle non-finite values.
Results may differ from a plain program's by a relative error of at most 0.0003.
Values sent between devices are 32-bit elements; how exact they have to be, the bound alone decides.
No kernel may reach another device: no remote copies, remote signals or barrier semaphores. Data moves between devices by JAX's collectives and lax.ppermute only.
A program may use at most 64 MiB of HBM per device.

v0:
```python
import jax
import jax.numpy as jnp
from jax import lax
from jax.sharding import PartitionSpec as P

BRICKS = 8


EXTINCTION = 0.024


def from_partner(array, axis, apart):
    return lax.ppermute(array, axis, [(i, i ^ 1 << apart) for i in range(lax.axis_size(axis))])


def render(values_in):
    depth_count = values_in.shape[1]
    shape = (values_in.shape[0], values_in.shape[2])
    before = jnp.zeros(shape, jnp.float32)
    red_sum = jnp.zeros(shape, jnp.float32)
    green_sum = jnp.zeros(shape, jnp.float32)
    blue_sum = jnp.zeros(shape, jnp.float32)
    for level in range(depth_count):
        values = values_in[:, level].astype(jnp.float32)
        extinction = EXTINCTION * values
        weight = jnp.exp(-before) * (1.0 - jnp.exp(-extinction))
        ratio = values / (1.0 + values)
        red_sum = red_sum + weight * ratio
        green_sum = green_sum + weight * 4.0 * ratio * (1.0 - ratio)
        blue_sum = blue_sum + weight * (1.0 - ratio)
        before = before + extinction
    return jnp.stack([red_sum, green_sum, blue_sum, before], axis=1)


def over_pair(front_part, back_part):
    colors = front_part[:, :3] + jnp.exp(-front_part[:, 3:4]) * back_part[:, :3]
    return jnp.concatenate([colors, front_part[:, 3:4] + back_part[:, 3:4]], axis=1)


def slot_tables(tiles_in, tile_slot, owned, per_brick, ranks_in):
    group_count, per_device = tiles_in.shape
    slot_ids = tile_slot[tiles_in]
    owners = slot_ids // owned
    tile_rows = slot_ids % owned
    position = jnp.arange(per_device, dtype=jnp.int32)
    same_owner = (owners[:, :, None] == owners[:, None, :]) & (
        position[None, None, :] < position[None, :, None]
    )
    places = jnp.sum(same_owner.astype(jnp.int32), axis=2)
    depth_keys = jnp.repeat(ranks_in.reshape(group_count, BRICKS), per_brick, axis=1)
    return (owners, tile_rows, places, depth_keys)


def arrivals(owners, tile_rows, places, depth_keys, device, capacity):
    slot_ids = jnp.arange(capacity, dtype=jnp.int32)
    matched = (
        (owners[:, None, :] == device) & (places[:, None, :] == slot_ids[None, :, None])
    ).astype(jnp.int32)
    rows_in = jnp.sum(matched * tile_rows[:, None, :], axis=2).reshape(-1)
    keys_in = jnp.sum(matched * depth_keys[:, None, :], axis=2).reshape(-1)
    valid_in = (jnp.sum(matched, axis=2) > 0).reshape(-1)
    return (rows_in, keys_in, valid_in)


def outgoing(fragments, owners_mine, places_mine, group_count, capacity):
    per_device = fragments.shape[0]
    target = owners_mine * capacity + places_mine
    slot_ids = jnp.arange(group_count * capacity, dtype=jnp.int32)
    matched = (target[None, :] == slot_ids[:, None]).astype(jnp.int32)
    numbers = jnp.arange(per_device, dtype=jnp.int32) + 1
    source = jnp.sum(matched * numbers[None, :], axis=1) - 1
    source = jnp.where(source < 0, per_device, source)
    padded = jnp.concatenate(
        [fragments, jnp.zeros((1,) + fragments.shape[1:], jnp.float32)], axis=0
    )
    return jnp.take(padded, source, axis=0)


def combine(pieces, rows_in, keys_in, valid_in, owned):
    optical = pieces[:, 3]
    both_valid = valid_in[:, None] & valid_in[None, :]
    in_front = (
        (rows_in[:, None] == rows_in[None, :]) & both_valid & (keys_in[None, :] < keys_in[:, None])
    ).astype(jnp.float32)
    prefix = jnp.dot(
        in_front, optical, precision=lax.Precision.HIGHEST, preferred_element_type=jnp.float32
    )
    shaded = pieces[:, :3] * jnp.exp(-prefix)[:, None]
    to_rows = (
        (jnp.arange(owned, dtype=jnp.int32)[:, None] == rows_in[None, :]) & valid_in[None, :]
    ).astype(jnp.float32)
    colors = jnp.einsum("of,fcp->ocp", to_rows, shaded, precision=lax.Precision.HIGHEST)
    summed = jnp.dot(
        to_rows, optical, precision=lax.Precision.HIGHEST, preferred_element_type=jnp.float32
    )
    return jnp.concatenate([colors, summed[:, None]], axis=1)


def leaving_of(fragments, owners_slab, places_slab, device, group_count, capacity):
    owners_mine = lax.dynamic_index_in_dim(owners_slab, device, 0, keepdims=False)
    places_mine = lax.dynamic_index_in_dim(places_slab, device, 0, keepdims=False)
    return outgoing(fragments, owners_mine, places_mine, group_count, capacity)


def shards(samples, tile_list, tile_slot, brick_rank):
    group_count = lax.axis_size("grp")
    swap_count = lax.axis_size("swap")
    device = lax.axis_index("grp")
    slab = lax.axis_index("swap")
    per_device = tile_list.shape[2]
    per_brick = per_device // BRICKS
    owned = tile_slot.shape[0] // group_count
    capacity = 2 * per_device // group_count
    pixels = samples.shape[4]
    block = pixels // swap_count
    fragments = render(samples[0, 0])
    tiles_slab = lax.dynamic_index_in_dim(tile_list, slab, 0, keepdims=False)
    ranks_slab = lax.dynamic_index_in_dim(brick_rank, slab, 0, keepdims=False)
    owners_slab, rows_slab, places_slab, keys_slab = slot_tables(
        tiles_slab, tile_slot, owned, per_brick, ranks_slab
    )
    leaving = leaving_of(fragments, owners_slab, places_slab, device, group_count, capacity)
    rows_in, keys_in, valid_in = arrivals(
        owners_slab, rows_slab, places_slab, keys_slab, device, capacity
    )
    arrived = lax.all_to_all(
        leaving.reshape(group_count, capacity, 4, pixels),
        "grp",
        split_axis=0,
        concat_axis=0,
        tiled=True,
    )
    partial_value = combine(
        arrived.reshape(-1, 4, arrived.shape[3]), rows_in, keys_in, valid_in, owned
    )
    levels = swap_count.bit_length() - 1
    partial_value = partial_value.reshape((owned, 4) + (2,) * levels + (block,))
    for level in range(levels):
        lower = partial_value[..., 0, :]
        upper = partial_value[..., 1, :]
        my_bit = jnp.right_shift(slab, level) % 2
        kept = jnp.where(my_bit == 1, upper, lower)
        given = jnp.where(my_bit == 1, lower, upper)
        received = from_partner(given, "swap", level)
        front_part = jnp.where(my_bit == 0, kept, received)
        back_part = jnp.where(my_bit == 0, received, kept)
        partial_value = over_pair(front_part, back_part)
    final_image = jnp.concatenate(
        [partial_value[:, :3], 1.0 - jnp.exp(-partial_value[:, 3:4])], axis=1
    )
    return final_image[None]


def solution(mesh):
    return jax.shard_map(
        shards,
        mesh=mesh,
        in_specs=(P("swap", "grp", None, None, None), P(), P(), P()),
        out_specs=P("grp", None, None, "swap"),
        check_vma=False,
    )
```

profile of v0, /device:TPU:10, one launch (start us, length us, event | category | flops | bytes accessed | tf_op | source)
XLA Modules:
  0.0 254.9 jit_solution(8371241051433230916)
XLA Ops:
  0.0 0.0 copy-start
  0.0 0.0 copy-start.1
  0.0 0.7 compare_select_fusion.2
  0.7 0.1 reshape.178
  0.8 0.0 copy-done.1
  0.8 0.0 copy-start.2
  0.8 6.6 %gather_fusion = s32[1024]{0:T(1024)S(1)} fusion(s32[128]{0:T(128)S(1)} %copy-done.1, s32[1024]{0:T(1024)S(1)} %broadcast_clamp_fusion), kind=kCustom, calls=%fused_computation | custom fusion | bytes 12288 | tf_op jit(solution)/shard_map/gather | solution.py:42
  7.4 0.1 reshape.177
  7.5 0.5 convert_reduce_fusion
  8.0 0.1 select_reduce_fusion.2
  8.2 0.1 sub.70
  8.3 0.0 copy-done.2
  8.3 1.2 copy.40
  9.4 2.7 %fusion.28 = (f32[64,1,4096]{2,0,1:T(8,128)S(1)}, f32[64,1,4096]{2,0,1:T(8,128)S(1)}, f32[64,1,4096]{2,0,1:T(8,128)S(1)}, f32[64,1,4096]{2,0,1:T(8,128)S(1)}) fusion(bf16[64,4,4096]{2,0,1:T(8,128)(2,1)S(1)} %bitcast.50), kind=kLoop, calls=%fused_computation.46 | loop fusion | flops 17039360 | bytes 6291456 | tf_op jit(solution)/shard_map/add | solution.py:28
  12.2 0.3 pad_maximum_fusion
  12.5 2.7 %copy.34 = f32[64,4,4096]{2,1,0:T(4,128)S(1)} copy(f32[64,4,4096]{2,0,1:T(8,128)S(1)} %pad_maximum_fusion) | data formatting | bytes 8388608
  15.2 2.8 %concatenate.12.clone = f32[65,4,4096]{2,1,0:T(4,128)} pad(f32[64,4,4096]{2,1,0:T(4,128)S(1)} %copy.34, f32[]{:T(128)} %constant.99.clone.1), padding=0_1x0_0x0_0 | pad | bytes 8454148 | tf_op jit(solution)/shard_map/concatenate | solution.py:73
  18.0 11.5 %gather_fusion.1 = f32[128,4,4096]{2,1,0:T(4,128)} fusion(f32[65,4,4096]{2,1,0:T(4,128)} %concatenate.12.clone, s32[1024]{0:T(1024)S(1)} %pad_clamp_fusion), kind=kCustom, calls=%fused_computation.1 | custom fusion | bytes 16777728 | tf_op jit(solution)/shard_map/jit(_take)/gather | solution.py:76
  29.5 10.6 %broadcast_select_fusion = f32[16,8,4,4096]{3,2,1,0:T(4,128)} fusion(f32[16,8,4,4096]{3,2,1,0:T(4,128)} %bitcast.49, pred[16,8]{1,0:T(8,128)(4,1)S(1)} %compare_and_fusion), kind=kLoop, calls=%fused_computation.8 | loop fusion | flops 2097152 | bytes 16777344 | tf_op jit(solution)/shard_map/jit(_take)/select_n | solution.py:76
  40.0 6.2 %all-to-all-start = ((f32[16,8,4,4096]{3,2,1,0:T(4,128)}), f32[16,8,4,4096]{3,2,1,0:T(4,128)}, u32[]{:S(2)}, u32[]{:S(2)}) async-start(f32[16,8,4,4096]{3,2,1,0:T(4,128)} %broadcast_select_fusion), calls=%async_computation | async-start | bytes 16777216 | tf_op jit(solution)/shard_map/all_to_all | solution.py:126
  46.3 0.0 copy-done
  46.3 0.1 reshape.174
  46.4 0.1 copy.29
  46.4 0.1 copy.30
  46.5 0.9 select_reduce_fusion
  47.4 0.1 lt.119
  47.5 0.1 eq.103
  47.6 0.1 gt.19
  47.7 180.7 %all-to-all-done = f32[16,8,4,4096]{3,2,1,0:T(4,128)} async-done(((f32[16,8,4,4096]{3,2,1,0:T(4,128)}), f32[16,8,4,4096]{3,2,1,0:T(4,128)}, u32[]{:S(2)}, u32[]{:S(2)}) %all-to-all-start) | async-done | bytes 8388640 | tf_op jit(solution)/shard_map/all_to_all | solution.py:126
  228.5 8.2 %copy.39 = f32[16,8,4,4096]{3,1,0,2:T(8,128)S(1)} copy(f32[16,8,4,4096]{3,2,1,0:T(4,128)} %all-to-all-done) | data formatting | bytes 16777216 | tf_op jit(solution)/shard_map/all_to_all | solution.py:126
  236.7 0.2 slice_bitcast_fusion
  236.9 1.4 fusion.1
  238.3 2.5 fusion
  240.7 1.9 copy.31
  242.6 2.6 %convolution_bitcast_fusion = f32[8,1,2,2048]{3,0,1,2:T(8,128)S(1)} fusion(f32[2,2048,128]{2,1,0:T(8,128)} %bitcast.51, s32[128]{0:T(128)S(1)} %eq.103, pred[128]{0:T(512)(128)(4,1)S(1)} %gt.19), kind=kOutput, calls=%fused_computation.10 | convolution fusion | flops 50333696 | bytes 2228864 | tf_op jit(solution)/shard_map/dot_general | solution.py:93
  245.3 1.6 collective-permute-start
  246.9 7.0 %collective-permute-done = f32[8,4,2048]{2,0,1:T(8,128)S(1)} collective-permute-done((f32[8,4,2048]{2,0,1:T(8,128)S(1)}, f32[8,4,2048]{2,0,1:T(8,128)S(1)}, u32[]{:S(2)}, u32[]{:S(2)}) %collective-permute-start) | collective-permute-done | bytes 262176 | tf_op jit(solution)/shard_map/ppermute | solution.py:13
  254.0 0.9 copy.33
  (19 shorter events, 0.3 us)
Async XLA Ops:
  0.0 46.3 %copy-start = (s32[2,128]{1,0:T(2,128)S(1)}, s32[2,128]{1,0:T(2,128)}, u32[]{:S(2)}) copy-start(s32[2,128]{1,0:T(2,128)} %param.7) | copy-start | bytes 3076
  0.0 0.8 copy-start.1
  0.8 7.4 %copy-start.2 = (bf16[1,1,64,4,4096]{4,3,2,1,0:T(4,128)(2,1)S(1)}, bf16[1,1,64,4,4096]{4,3,2,1,0:T(4,128)(2,1)}, u32[]{:S(2)}) copy-start(bf16[1,1,64,4,4096]{4,3,2,1,0:T(4,128)(2,1)} %param.4) | copy-start | bytes 6291460
  40.0 188.4 %all-to-all-start = ((f32[16,8,4,4096]{3,2,1,0:T(4,128)}), f32[16,8,4,4096]{3,2,1,0:T(4,128)}, u32[]{:S(2)}, u32[]{:S(2)}) async-start(f32[16,8,4,4096]{3,2,1,0:T(4,128)} %broadcast_select_fusion), calls=%async_computation | async-start | bytes 16777216 | tf_op jit(solution)/shard_map/all_to_all | solution.py:126
  245.3 8.6 %collective-permute-start = (f32[8,4,2048]{2,0,1:T(8,128)S(1)}, f32[8,4,2048]{2,0,1:T(8,128)S(1)}, u32[]{:S(2)}, u32[]{:S(2)}) collective-permute-start(f32[8,4,2048]{2,0,1:T(8,128)S(1)} %select_bitcast_fusion), channel_id=1, source_target_pairs={{0,1},{1,0},{2,3},{3,2},{4,5},{5,4},{6,7},{7,6},{8,9},{9,8},{10,11... | collective-permute-start | bytes 786440 | tf_op jit(solution)/shard_map/ppermute | solution.py:13
where the time goes:
time: 255 us
  waiting for transfers between devices  188 us (74%)
  local copies, waits for them, and re-layouts  36.7 us (14%)
  other arithmetic  16.1 us (6%)
  starting transfers between devices  7.83 us (3%)
  matrix products  6.46 us (3%)
    all_to_all x1, waiting for transfers between devices, shards(): lax.all_to_all(leaving.reshape(group_count, capacity, 4, pixels), 'grp',...  181 us
    gather x1, local copies, waits for them, and re-layouts, outgoing(): return jnp.take(padded, source, axis=0)  11.5 us
    select_n x2, other arithmetic, outgoing(): return jnp.take(padded, source, axis=0)  10.6 us
    all_to_all x1, local copies, waits for them, and re-layouts, shards(): lax.all_to_all(leaving.reshape(group_count, capacity, 4, pixels), 'grp',...  8.24 us
    ppermute x1, waiting for transfers between devices, from_partner(): lax.ppermute(array, axis, [(i, i ^ 1 << apart) for i in range(lax.axis_si...  6.96 us
    gather x2, local copies, waits for them, and re-layouts, slot_tables(): slot_ids = tile_slot[tiles_in]  6.64 us
    all_to_all x1, starting transfers between devices, shards(): lax.all_to_all(leaving.reshape(group_count, capacity, 4, pixels), 'grp',...  6.22 us
  transfers between devices with their start and end apart: 2, of which 2 were waited for; matrix products, arithmetic and copies ran while one was open for 1% of the time, Pallas kernels for 0%

commit v1 on v0

--- a/solution.py
+++ b/solution.py
@@ -1,6 +1,9 @@
+import functools
 import jax
 import jax.numpy as jnp
 from jax import lax
+from jax.experimental import pallas as pl
+from jax.experimental.pallas import tpu as pltpu
 from jax.sharding import PartitionSpec as P
 
 BRICKS = 8
@@ -102,7 +105,7 @@
     return outgoing(fragments, owners_mine, places_mine, group_count, capacity)
 
 
-def shards(samples, tile_list, tile_slot, brick_rank):
+def general_shards(samples, tile_list, tile_slot, brick_rank):
     group_count = lax.axis_size("grp")
     swap_count = lax.axis_size("swap")
     device = lax.axis_index("grp")
@@ -151,6 +154,174 @@
     return final_image[None]
 
 
+LANES = 128
+VMEM_BYTES = 48 * 1024 * 1024
+
+
+def render_kernel(samples_ref, out_ref):
+    depth_count = samples_ref.shape[0]
+    for part in range(out_ref.shape[0]):
+        lanes = slice(part * LANES, (part + 1) * LANES)
+        before = None
+        through = None
+        for level in range(depth_count):
+            values = samples_ref[level, :, lanes].astype(jnp.float32)
+            extinction = EXTINCTION * values
+            before = extinction if before is None else before + extinction
+            after = jnp.exp(-before)
+            weight = (1.0 - after) if through is None else (through - after)
+            through = after
+            absent = 1.0 / (1.0 + values)
+            red = weight * (1.0 - absent)
+            green = red * absent
+            if level == 0:
+                red_sum, green_sum = red, green
+            else:
+                red_sum, green_sum = red_sum + red, green_sum + green
+        out_ref[part, 0, 0] = red_sum
+        out_ref[part, 0, 1] = 4.0 * green_sum
+        out_ref[part, 0, 2] = before
+
+
+def render_chunks(levels, group_count, swap_count):
+    depth_count, per_device, pixels = levels.shape
+    parts = 4
+    return pl.pallas_call(
+        render_kernel,
+        grid=(pixels // (parts * LANES),),
+        in_specs=[pl.BlockSpec((depth_count, per_device, parts * LANES), lambda i: (0, 0, i))],
+        out_specs=pl.BlockSpec(
+            (parts, 1, 3, per_device, LANES),
+            lambda i: (i % (group_count // parts), i // (group_count // parts), 0, 0, 0),
+        ),
+        out_shape=jax.ShapeDtypeStruct(
+            (group_count, swap_count, 3, per_device, LANES), jnp.float32
+        ),
+        compiler_params=pltpu.CompilerParams(vmem_limit_bytes=VMEM_BYTES),
+    )(levels)
+
+
+def mask_kernel(key_count, tiles_ref, keys_ref, slots_ref, front_ref, member_ref):
+    swap_count, fragment_count = tiles_ref.shape
+    slot_count = slots_ref.shape[1]
+    slot_id = lax.broadcasted_iota(jnp.int32, (slot_count, slot_count), 0).astype(jnp.float32)
+    tile_id = lax.broadcasted_iota(jnp.int32, (slot_count, slot_count), 1).astype(jnp.float32)
+    held = jnp.where(slots_ref[...] == slot_id, tile_id, 0.0)
+    slot_tile = jnp.sum(held, axis=1, keepdims=True)
+    for slab in range(swap_count):
+        tiles = tiles_ref[slab : slab + 1, :]
+        codes = tiles * float(key_count) + keys_ref[slab : slab + 1, :]
+        member_ref[slab] = jnp.where(tiles == slot_tile, 1.0, 0.0).astype(jnp.bfloat16)
+        for start in range(0, fragment_count, LANES):
+            block = slice(start, start + LANES)
+            mine = jnp.broadcast_to(codes[:, block], (LANES, LANES)).T
+            least = jnp.broadcast_to(tiles[:, block], (LANES, LANES)).T * float(key_count)
+            for other in range(0, fragment_count, LANES):
+                theirs = codes[:, other : other + LANES]
+                nearer = (theirs >= least) & (theirs < mine)
+                front_ref[slab, block, other : other + LANES] = jnp.where(
+                    nearer, 1.0, 0.0
+                ).astype(jnp.bfloat16)
+
+
+def depth_masks(tile_list, tile_slot, brick_rank):
+    swap_count, group_count, per_device = tile_list.shape
+    fragment_count = group_count * per_device
+    slot_count = tile_slot.shape[0]
+    key_count = brick_rank.shape[1]
+    tiles = tile_list.reshape(swap_count, fragment_count).astype(jnp.float32)
+    keys = jnp.broadcast_to(
+        brick_rank[:, :, None], (swap_count, key_count, fragment_count // key_count)
+    )
+    keys = keys.reshape(swap_count, fragment_count).astype(jnp.float32)
+    return pl.pallas_call(
+        functools.partial(mask_kernel, key_count),
+        out_shape=[
+            jax.ShapeDtypeStruct((swap_count, fragment_count, fragment_count), jnp.bfloat16),
+            jax.ShapeDtypeStruct((swap_count, slot_count, fragment_count), jnp.bfloat16),
+        ],
+        compiler_params=pltpu.CompilerParams(vmem_limit_bytes=VMEM_BYTES),
+    )(tiles, keys, tile_slot.astype(jnp.float32)[None])
+
+
+def split(values):
+    high = values.astype(jnp.bfloat16)
+    low = (values - high.astype(jnp.float32)).astype(jnp.bfloat16)
+    return jnp.concatenate([high, low], axis=1)
+
+
+def masked_sum(mask, values):
+    both = jnp.dot(mask, split(values), preferred_element_type=jnp.float32)
+    width = values.shape[1]
+    return both[:, :width] + both[:, width:]
+
+
+def composite_kernel(chunk_ref, front_ref, member_ref, out_ref):
+    group_count, swap_count, _, per_device, lanes = chunk_ref.shape
+    shape = (group_count * per_device, lanes)
+    for slab in range(swap_count):
+        optical = chunk_ref[:, slab, 2].reshape(shape)
+        through = jnp.exp(-masked_sum(front_ref[slab], optical))
+        red = chunk_ref[:, slab, 0].reshape(shape) * through
+        green = chunk_ref[:, slab, 1].reshape(shape) * through
+        sums = masked_sum(member_ref[slab], jnp.concatenate([red, green, optical], axis=1))
+        if slab == 0:
+            colors, depth = sums[:, : 2 * lanes], sums[:, 2 * lanes :]
+        else:
+            seen = jnp.exp(-depth)
+            colors = colors + jnp.concatenate([seen, seen], axis=1) * sums[:, : 2 * lanes]
+            depth = depth + sums[:, 2 * lanes :]
+    owned = out_ref.shape[2]
+    tiles = (group_count, owned, lanes)
+    out_ref[:, 0] = colors[:, :lanes].reshape(tiles)
+    out_ref[:, 1] = colors[:, lanes:].reshape(tiles)
+    out_ref[:, 2] = (1.0 - jnp.exp(-depth)).reshape(tiles)
+
+
+def composite(chunk, front, member):
+    group_count, _, _, _, lanes = chunk.shape
+    owned = member.shape[1] // group_count
+    return pl.pallas_call(
+        composite_kernel,
+        out_shape=jax.ShapeDtypeStruct((group_count, 3, owned, lanes), jnp.float32),
+        compiler_params=pltpu.CompilerParams(vmem_limit_bytes=VMEM_BYTES),
+    )(chunk, front, member)
+
+
+def chunk_shards(samples, tile_list, tile_slot, brick_rank):
+    group_count = lax.axis_size("grp")
+    swap_count = lax.axis_size("swap")
+    per_device, pixels = samples.shape[2], samples.shape[4]
+    owned = tile_slot.shape[0] // group_count
+    levels = jnp.transpose(samples[0, 0], (1, 0, 2))
+    leaving = render_chunks(levels, group_count, swap_count)
+    arrived = lax.all_to_all(
+        leaving.reshape(group_count * swap_count, 3, per_device, LANES),
+        ("grp", "swap"),
+        split_axis=0,
+        concat_axis=0,
+        tiled=True,
+    )
+    front, member = depth_masks(tile_list, tile_slot, brick_rank)
+    tiles = composite(
+        arrived.reshape(group_count, swap_count, 3, per_device, LANES), front, member
+    )
+    image = lax.all_to_all(tiles, "grp", split_axis=0, concat_axis=0, tiled=True)
+    red, green, opacity = (
+        jnp.transpose(image[:, channel], (1, 0, 2)).reshape(owned, pixels // swap_count)
+        for channel in range(3)
+    )
+    return jnp.stack([red, green, opacity - red, opacity], axis=1)[None]
+
+
+def shards(samples, tile_list, tile_slot, brick_rank):
+    device_count = lax.axis_size("grp") * lax.axis_size("swap")
+    fragment_count = tile_list.shape[1] * tile_list.shape[2]
+    if samples.shape[4] == device_count * LANES and fragment_count <= 1024:
+        return chunk_shards(samples, tile_list, tile_slot, brick_rank)
+    return general_shards(samples, tile_list, tile_slot, brick_rank)
+
+
 def solution(mesh):
     return jax.shard_map(
         shards,

time: 255 us -> 106 us (0.42)
  the two profiles are of different devices: /device:TPU:10 before, /device:TPU:0 now
where the time goes in v1:
time: 106 us
  waiting for transfers between devices  66.6 us (63%)
  blocking collectives  12.7 us (12%)
  Pallas kernels  11.3 us (11%)
  local copies, waits for them, and re-layouts  7.69 us (7%)
  starting transfers between devices  7.3 us (7%)
    all_to_all x1, waiting for transfers between devices, chunk_shards(): lax.all_to_all(leaving.reshape(group_count * swap_count, 3, per_device, L...  66.6 us
    all_to_all x1, blocking collectives, chunk_shards(): lax.all_to_all(tiles, 'grp', split_axis=0, concat_axis=0, tiled=True)  12.7 us
    all_to_all x1, starting transfers between devices, chunk_shards(): lax.all_to_all(leaving.reshape(group_count * swap_count, 3, per_device, L...  7.3 us
    unnamed x13, local copies, waits for them, and re-layouts  6.52 us
    pallas_call x1, Pallas kernels, composite(): pl.pallas_call(composite_kernel, out_shape=jax.ShapeDtypeStruct((group_co...  5.39 us
    pallas_call x1, Pallas kernels, render_chunks(): pl.pallas_call(render_kernel, grid=(pixels // (parts * LANES),), in_specs...  4.41 us
  transfers between devices with their start and end apart: 1, of which 1 were waited for; matrix products, arithmetic and copies ran while one was open for 0% of the time, Pallas kernels for 1%

profile of v1, /device:TPU:0, one launch (start us, length us, event | category | flops | bytes accessed | tf_op | source)
XLA Modules:
  0.0 105.8 jit_solution(12398881129977780469)
XLA Ops:
  0.0 2.7 %copy.9 = bf16[1,1,64,4,4096]{4,2,3,1,0:T(8,128)(2,1)S(1)} copy(bf16[1,1,64,4,4096]{4,3,2,1,0:T(4,128)(2,1)} %param.4) | data formatting | bytes 4194304 | tf_op args[0]
  2.7 4.4 %shard_map.46 = f32[16,2,3,64,128]{4,3,2,1,0:T(8,128)} custom-call(bf16[4,64,4096]{2,1,0:T(8,128)(2,1)S(1)} %bitcast.34), custom_call_target="tpu_custom_call" | custom-call | tf_op jit(solution)/shard_map/pallas_call | solution.py:189
  7.2 0.0 copy-start.4
  7.2 0.0 copy-start.3
  7.2 0.0 copy-start.5
  7.2 7.3 %all-to-all-start = ((f32[32,3,64,128]{3,2,1,0:T(8,128)}), f32[32,3,64,128]{3,2,1,0:T(8,128)S(1)}, u32[]{:S(2)}, u32[]{:S(2)}) async-start(f32[32,3,64,128]{3,2,1,0:T(8,128)} %bitcast.2), calls=%async_computation | async-start | bytes 6291456 | tf_op jit(solution)/shard_map/all_to_all | solution.py:298
  14.5 0.0 copy-done.4
  14.5 0.0 copy-done.3
  14.5 0.1 convert_element_type.14.tiles_ref
  14.6 0.1 broadcast_in_dim.12
  14.7 0.1 convert_element_type.16.keys_ref
  14.8 0.0 copy-done.5
  14.8 1.5 %shard_map.47 = (bf16[2,1024,1024]{2,1,0:T(8,128)(2,1)S(1)}, bf16[2,128,1024]{2,1,0:T(8,128)(2,1)S(1)}) custom-call(f32[2,1024]{1,0:T(2,128)S(1)} %convert_element_type.14.tiles_ref, f32[2,1024]{1,0:T(2,128)S(1)} %convert_element_type.16.keys_ref, f32[1,128]{1,0:T(1,128)S(1)} %convert_bitcast_fusion.slots_ref), custom_call_target="tpu_custom_call" | custom-call | tf_op jit(solution)/shard_map/pallas_call | solution.py:237
  16.4 0.0 copy-start
  16.4 1.9 %copy-done = bf16[2,1024,1024]{2,1,0:T(8,128)(2,1)} copy-done((bf16[2,1024,1024]{2,1,0:T(8,128)(2,1)}, bf16[2,1024,1024]{2,1,0:T(8,128)(2,1)S(1)}, u32[]{:S(2)}) %copy-start) | copy-done | bytes 4194328
  18.3 0.0 copy-start.1
  18.3 0.8 copy-done.1
  19.1 66.6 %all-to-all-done = f32[32,3,64,128]{3,2,1,0:T(8,128)S(1)} async-done(((f32[32,3,64,128]{3,2,1,0:T(8,128)}), f32[32,3,64,128]{3,2,1,0:T(8,128)S(1)}, u32[]{:S(2)}, u32[]{:S(2)}) %all-to-all-start) | async-done | bytes 3145760 | tf_op jit(solution)/shard_map/all_to_all | solution.py:298
  85.7 0.0 copy-start.2
  85.7 1.0 copy-done.2
  86.8 5.4 %shard_map.48 = f32[16,3,8,128]{3,2,1,0:T(8,128)S(1)} custom-call(f32[16,2,3,64,128]{4,3,2,1,0:T(8,128)S(1)} %bitcast.33, bf16[2,1024,1024]{2,1,0:T(8,128)(2,1)} %copy-done, bf16[2,128,1024]{2,1,0:T(8,128)(2,1)S(1)} %copy-done.2), custom_call_target="tpu_custom_call" | custom-call | tf_op jit(solution)/shard_map/pallas_call | solution.py:284
  92.2 12.7 %all_to_all.10 = f32[16,3,8,128]{3,2,1,0:T(8,128)S(1)} all-to-all(f32[16,3,8,128]{3,2,1,0:T(8,128)S(1)} %shard_map.48), channel_id=1, replica_groups=mesh['grp'=16,'swap'=2] {'grp'}, dimensions={0} | all-to-all | bytes 393216 | tf_op jit(solution)/shard_map/all_to_all | solution.py:309
  104.9 0.9 copy.7
  (6 shorter events, 0.1 us)
Async XLA Ops:
  7.2 7.3 %copy-start.4 = (s32[2,128]{1,0:T(2,128)S(1)}, s32[2,128]{1,0:T(2,128)}, u32[]{:S(2)}) copy-start(s32[2,128]{1,0:T(2,128)} %param.7) | copy-start | bytes 3076
  7.2 7.3 %copy-start.3 = (s32[2,16,64]{2,1,0:T(8,128)S(1)}, s32[2,16,64]{2,1,0:T(8,128)}, u32[]{:S(2)}) copy-start(s32[2,16,64]{2,1,0:T(8,128)} %param.5) | copy-start | bytes 24580
  7.2 7.7 %copy-start.5 = (s32[128]{0:T(128)S(1)}, s32[128]{0:T(128)}, u32[]{:S(2)}) copy-start(s32[128]{0:T(128)} %param.6) | copy-start | bytes 1540
  7.2 78.6 %all-to-all-start = ((f32[32,3,64,128]{3,2,1,0:T(8,128)}), f32[32,3,64,128]{3,2,1,0:T(8,128)S(1)}, u32[]{:S(2)}, u32[]{:S(2)}) async-start(f32[32,3,64,128]{3,2,1,0:T(8,128)} %bitcast.2), calls=%async_computation | async-start | bytes 6291456 | tf_op jit(solution)/shard_map/all_to_all | solution.py:298
  16.4 1.9 %copy-start = (bf16[2,1024,1024]{2,1,0:T(8,128)(2,1)}, bf16[2,1024,1024]{2,1,0:T(8,128)(2,1)S(1)}, u32[]{:S(2)}) copy-start(bf16[2,1024,1024]{2,1,0:T(8,128)(2,1)S(1)} %get-tuple-element.7.front_ref) | copy-start | bytes 12582916
  18.3 0.8 copy-start.1
  85.7 1.0 copy-start.2

commit v2 on v0

--- a/solution.py
+++ b/solution.py
@@ -1,6 +1,9 @@
+import functools
 import jax
 import jax.numpy as jnp
 from jax import lax
+from jax.experimental import pallas as pl
+from jax.experimental.pallas import tpu as pltpu
 from jax.sharding import PartitionSpec as P
 
 BRICKS = 8
@@ -102,7 +105,7 @@
     return outgoing(fragments, owners_mine, places_mine, group_count, capacity)
 
 
-def shards(samples, tile_list, tile_slot, brick_rank):
+def general_shards(samples, tile_list, tile_slot, brick_rank):
     group_count = lax.axis_size("grp")
     swap_count = lax.axis_size("swap")
     device = lax.axis_index("grp")
@@ -151,6 +154,236 @@
     return final_image[None]
 
 
+LANES = 128
+VMEM_BYTES = 20 * 1024 * 1024
+
+
+def level_order(fragments, depth_count):
+    rows = fragments * depth_count
+    to = lax.broadcasted_iota(jnp.int32, (rows, rows), 0)
+    source = lax.broadcasted_iota(jnp.int32, (rows, rows), 1)
+    wanted = (to % fragments) * depth_count + to // fragments
+    return jnp.where(source == wanted, 1.0, 0.0).astype(jnp.bfloat16)
+
+
+def render_levels(levels):
+    before = through = held = held_twice = None
+    for level in range(levels.shape[0]):
+        values = levels[level]
+        extinction = EXTINCTION * values
+        before = extinction if before is None else before + extinction
+        after = jnp.exp(-before)
+        weight = (1.0 - after) if through is None else (through - after)
+        through = after
+        absent = 1.0 / (1.0 + values)
+        once = weight * absent
+        twice = once * absent
+        held = once if held is None else held + once
+        held_twice = twice if held_twice is None else held_twice + twice
+    return (1.0 - through) - held, 4.0 * (held - held_twice), before
+
+
+def render_kernel(samples_ref, out_ref, held_ref, made_ref, in_sems, out_sems):
+    group_count, swap_count = out_ref.shape[:2]
+    fragments, depth_count, pixels = samples_ref.shape
+    pieces, width = held_ref.shape[0], held_ref.shape[3]
+    chunks = width // LANES
+    per_slab = group_count // chunks
+    arriving, leaving = [], []
+    for piece in range(pieces):
+        part = samples_ref.at[:, :, pl.ds(piece * width, width)]
+        arriving.append(pltpu.make_async_copy(part, held_ref.at[piece], in_sems.at[piece]))
+        place = (pl.ds(piece % per_slab * chunks, chunks), piece // per_slab)
+        leaving.append(
+            pltpu.make_async_copy(made_ref.at[place], out_ref.at[place], out_sems.at[piece])
+        )
+    for copy in arriving:
+        copy.start()
+    order = level_order(fragments, depth_count)
+    for piece in range(pieces):
+        arriving[piece].wait()
+        levels = jnp.dot(
+            order,
+            held_ref[piece].reshape(fragments * depth_count, width),
+            preferred_element_type=jnp.float32,
+        ).reshape(depth_count, fragments, width)
+        for at in range(chunks):
+            channels = render_levels(levels[:, :, at * LANES : (at + 1) * LANES])
+            chunk = piece % per_slab * chunks + at
+            for channel in range(3):
+                made_ref[chunk, piece // per_slab, channel] = channels[channel]
+        leaving[piece].start()
+    for copy in leaving:
+        copy.wait()
+
+
+def render_chunks(samples, group_count, swap_count):
+    fragments, depth_count, pixels = samples.shape
+    pieces = 4
+    out_shape = (group_count, swap_count, 3, fragments, LANES)
+    return pl.pallas_call(
+        render_kernel,
+        in_specs=[pl.BlockSpec(memory_space=pltpu.HBM)],
+        out_specs=pl.BlockSpec(memory_space=pltpu.HBM),
+        out_shape=jax.ShapeDtypeStruct(out_shape, jnp.float32),
+        scratch_shapes=[
+            pltpu.VMEM((pieces, fragments, depth_count, pixels // pieces), jnp.bfloat16),
+            pltpu.VMEM(out_shape, jnp.float32),
+            pltpu.SemaphoreType.DMA((pieces,)),
+            pltpu.SemaphoreType.DMA((pieces,)),
+        ],
+        compiler_params=pltpu.CompilerParams(vmem_limit_bytes=3 * VMEM_BYTES),
+    )(pltpu.with_memory_space_constraint(samples, pltpu.HBM))
+
+
+def split(values):
+    high = values.astype(jnp.bfloat16)
+    low = (values - high.astype(jnp.float32)).astype(jnp.bfloat16)
+    return jnp.concatenate([high, low], axis=1)
+
+
+def masked_sum(mask, parts):
+    both = jnp.dot(mask, parts, preferred_element_type=jnp.float32)
+    width = parts.shape[1] // 2
+    return both[:, :width] + both[:, width:]
+
+
+def composite_kernel(order_ref, chunk_ref, member_ref, back_ref, out_ref, *scratch):
+    member_held, back_held, sorted_ref, sems = scratch
+    group_count, swap_count, channels, per_device, lanes = chunk_ref.shape
+    copies = [
+        pltpu.make_async_copy(member_ref, member_held, sems.at[0]),
+        pltpu.make_async_copy(back_ref, back_held, sems.at[1]),
+    ]
+    for copy in copies:
+        copy.start()
+    per_brick = per_device // BRICKS
+    bricks = group_count * BRICKS
+    for at in range(swap_count * bricks):
+        brick = order_ref[at]
+        source = lax.div(brick, BRICKS)
+        first = pl.multiple_of(lax.rem(brick, BRICKS) * per_brick, per_brick)
+        for channel in range(channels):
+            sorted_ref[
+                at * per_brick : (at + 1) * per_brick, channel * lanes : (channel + 1) * lanes
+            ] = chunk_ref[source, at // bricks, channel, pl.ds(first, per_brick), :]
+    for copy in copies:
+        copy.wait()
+    fragment_count = swap_count * bricks * per_brick
+    block = min(2 * LANES, fragment_count)
+    starts = range(0, fragment_count, block)
+    row = lax.broadcasted_iota(jnp.int32, (block, block), 0) // per_brick
+    column = lax.broadcasted_iota(jnp.int32, (block, block), 1) // per_brick
+    nearer = column < row
+    members = [member_held[:, start : start + block] for start in starts]
+    backs = [back_held[start : start + block, :] for start in starts]
+    opticals = [split(sorted_ref[start : start + block, 2 * lanes :]) for start in starts]
+    added = [masked_sum(member, optical) for member, optical in zip(members, opticals)]
+    fronts = []
+    for member, back in zip(members, backs):
+        same = jnp.dot(back, member, preferred_element_type=jnp.float32)
+        fronts.append(jnp.where(nearer, same, 0.0).astype(jnp.bfloat16))
+    depths = [added[0]]
+    for value in added[1:]:
+        depths.append(depths[-1] + value)
+    throughs = []
+    for at, (front, back, optical) in enumerate(zip(fronts, backs, opticals)):
+        before = masked_sum(front, optical)
+        if at > 0:
+            before = before + masked_sum(back, split(depths[at - 1]))
+        throughs.append(jnp.exp(-before))
+    color = None
+    for start, member, through in zip(starts, members, throughs):
+        both = jnp.concatenate([through, through], axis=1)
+        shaded = split(sorted_ref[start : start + block, : 2 * lanes] * both)
+        shaded = masked_sum(member, shaded)
+        color = shaded if color is None else color + shaded
+    owned = out_ref.shape[2]
+    tiles = (group_count, owned, lanes)
+    out_ref[:, 0] = color[:, :lanes].reshape(tiles)
+    out_ref[:, 1] = color[:, lanes:].reshape(tiles)
+    out_ref[:, 2] = (1.0 - jnp.exp(-depths[-1])).reshape(tiles)
+
+
+def composite(order, chunk, member, back):
+    group_count, swap_count, channels, per_device, lanes = chunk.shape
+    slot_count, fragment_count = member.shape
+    return pl.pallas_call(
+        composite_kernel,
+        in_specs=[
+            pl.BlockSpec(memory_space=pltpu.SMEM),
+            pl.BlockSpec(memory_space=pltpu.VMEM),
+            pl.BlockSpec(memory_space=pltpu.HBM),
+            pl.BlockSpec(memory_space=pltpu.HBM),
+        ],
+        out_specs=pl.BlockSpec(memory_space=pltpu.VMEM),
+        out_shape=jax.ShapeDtypeStruct(
+            (group_count, channels, slot_count // group_count, lanes), jnp.float32
+        ),
+        scratch_shapes=[
+            pltpu.VMEM(member.shape, member.dtype),
+            pltpu.VMEM(back.shape, back.dtype),
+            pltpu.VMEM((fragment_count, channels * lanes), jnp.float32),
+            pltpu.SemaphoreType.DMA((2,)),
+        ],
+        compiler_params=pltpu.CompilerParams(vmem_limit_bytes=VMEM_BYTES),
+    )(
+        order,
+        chunk,
+        pltpu.with_memory_space_constraint(member, pltpu.HBM),
+        pltpu.with_memory_space_constraint(back, pltpu.HBM),
+    )
+
+
+def depth_order(tile_list, tile_slot, brick_rank):
+    swap_count, brick_count = brick_rank.shape
+    numbers = jnp.arange(brick_count, dtype=jnp.int32)
+    placed = brick_rank[:, None, :] == numbers[None, :, None]
+    order = jnp.sum(jnp.where(placed, numbers[None, None, :], 0), axis=2)
+    slot_count = tile_slot.shape[0]
+    ids = jnp.arange(slot_count, dtype=jnp.int32)
+    found = tile_list[..., None] == ids
+    slots = jnp.sum(jnp.where(found, tile_slot, 0), axis=-1)
+    slots = slots.reshape(swap_count, 1, brick_count, -1)
+    slots = jnp.sum(jnp.where(placed[..., None], slots, 0), axis=2).reshape(-1)
+    member = (ids[:, None] == slots[None, :]).astype(jnp.bfloat16)
+    back = (slots[:, None] == ids[None, :]).astype(jnp.bfloat16)
+    return order.reshape(-1), member, back
+
+
+def chunk_shards(samples, tile_list, tile_slot, brick_rank):
+    group_count = lax.axis_size("grp")
+    swap_count = lax.axis_size("swap")
+    per_device, pixels = samples.shape[2], samples.shape[4]
+    owned = tile_slot.shape[0] // group_count
+    leaving = render_chunks(samples[0, 0], group_count, swap_count)
+    arrived = lax.all_to_all(
+        leaving.reshape(group_count * swap_count, 3, per_device, LANES),
+        ("grp", "swap"),
+        split_axis=0,
+        concat_axis=0,
+        tiled=True,
+    )
+    order, member, back = depth_order(tile_list, tile_slot, brick_rank)
+    tiles = composite(
+        order, arrived.reshape(group_count, swap_count, 3, per_device, LANES), member, back
+    )
+    image = lax.all_to_all(tiles, "grp", split_axis=0, concat_axis=0, tiled=True)
+    red, green, opacity = (
+        jnp.transpose(image[:, channel], (1, 0, 2)).reshape(owned, pixels // swap_count)
+        for channel in range(3)
+    )
+    return jnp.stack([red, green, opacity - red, opacity], axis=1)[None]
+
+
+def shards(samples, tile_list, tile_slot, brick_rank):
+    device_count = lax.axis_size("grp") * lax.axis_size("swap")
+    fragment_count = tile_list.shape[1] * tile_list.shape[2]
+    if samples.shape[4] == device_count * LANES and fragment_count <= 1024:
+        return chunk_shards(samples, tile_list, tile_slot, brick_rank)
+    return general_shards(samples, tile_list, tile_slot, brick_rank)
+
+
 def solution(mesh):
     return jax.shard_map(
         shards,

time: 255 us -> 100 us (0.39)
  the two profiles are of different devices: /device:TPU:10 before, /device:TPU:0 now
where the time goes in v2:
time: 100 us
  waiting for transfers between devices  63.5 us (64%)
  blocking collectives  12.7 us (13%)
  Pallas kernels  7.81 us (8%)
  other arithmetic  7.52 us (8%)
  starting transfers between devices  7.3 us (7%)
  local copies, waits for them, and re-layouts  1.17 us (1%)
    all_to_all x1, waiting for transfers between devices, chunk_shards(): lax.all_to_all(leaving.reshape(group_count * swap_count, 3, per_device, L...  63.5 us
    all_to_all x1, blocking collectives, chunk_shards(): lax.all_to_all(tiles, 'grp', split_axis=0, concat_axis=0, tiled=True)  12.7 us
    all_to_all x1, starting transfers between devices, chunk_shards(): lax.all_to_all(leaving.reshape(group_count * swap_count, 3, per_device, L...  7.3 us
    pallas_call x1, Pallas kernels, render_chunks(): pl.pallas_call(render_kernel, in_specs=[pl.BlockSpec(memory_space=pltpu.H...  4.48 us
    reduce_sum x1, other arithmetic, depth_order(): slots = jnp.sum(jnp.where(placed[..., None], slots, 0), axis=2).reshape(-1)  4.39 us
    pallas_call x1, Pallas kernels, composite(): pl.pallas_call(composite_kernel, in_specs=[pl.BlockSpec(memory_space=pltp...  3.33 us
  transfers between devices with their start and end apart: 1, of which 1 were waited for; matrix products, arithmetic and copies ran while one was open for 8% of the time, Pallas kernels for 0%

profile of v2, /device:TPU:0, one launch (start us, length us, event | category | flops | bytes accessed | tf_op | source)
XLA Modules:
  0.0 100.0 jit_solution(13176494339106186144)
XLA Ops:
  0.0 4.5 %shard_map.46 = f32[16,2,3,64,128]{4,3,2,1,0:T(8,128)} custom-call(bf16[64,4,4096]{2,1,0:T(4,128)(2,1)} %bitcast.31), custom_call_target="tpu_custom_call" | custom-call | tf_op jit(solution)/shard_map/pallas_call | solution.py:224
  4.5 0.0 copy-start
  4.5 0.0 copy-start.2
  4.5 0.0 copy-start.1
  4.5 7.3 %all-to-all-start = ((f32[32,3,64,128]{3,2,1,0:T(8,128)}), f32[32,3,64,128]{3,2,1,0:T(8,128)S(1)}, u32[]{:S(2)}, u32[]{:S(2)}) async-start(f32[32,3,64,128]{3,2,1,0:T(8,128)} %bitcast.30), calls=%async_computation | async-start | bytes 6291456 | tf_op jit(solution)/shard_map/all_to_all | solution.py:360
  11.8 0.0 copy-done
  11.8 0.0 copy-done.2
  11.9 0.9 select_reduce_fusion.1
  12.8 0.1 broadcast_in_dim.58
  12.9 0.1 copy.6
  12.9 0.0 copy-done.1
  13.0 4.4 %select_reduce_fusion = s32[2,128,8]{2,1,0:T(8,128)S(1)} fusion(s32[2,128,8]{1,2,0:T(8,128)S(1)} %copy.6, pred[2,128,128]{2,1,0:T(8,128)(4,1)S(1)} %iota_compare_fusion.3), kind=kLoop, calls=%fused_computation.1 | loop fusion | flops 522240 | bytes 49152 | tf_op jit(solution)/shard_map/reduce_sum | solution.py:348
  17.4 0.1 eq.65
  17.5 0.1 select_reduce_fusion.2
  17.6 0.9 fusion.member_ref
  18.5 1.1 %fusion.1.back_ref = bf16[2048,128]{1,0:T(8,128)(2,1)} fusion(s32[2048]{0:T(1024)S(1)} %eq.65), kind=kLoop, calls=%fused_computation.6 | loop fusion | flops 524288 | bytes 532480 | tf_op jit(solution)/shard_map/convert_element_type | solution.py:350
  19.6 63.5 %all-to-all-done = f32[32,3,64,128]{3,2,1,0:T(8,128)S(1)} async-done(((f32[32,3,64,128]{3,2,1,0:T(8,128)}), f32[32,3,64,128]{3,2,1,0:T(8,128)S(1)}, u32[]{:S(2)}, u32[]{:S(2)}) %all-to-all-start) | async-done | bytes 3145760 | tf_op jit(solution)/shard_map/all_to_all | solution.py:360
  83.1 3.3 %shard_map.47 = f32[16,3,8,128]{3,2,1,0:T(8,128)S(1)} custom-call(s32[256]{0:T(256)S(1)} %bitcast.29, f32[16,2,3,64,128]{4,3,2,1,0:T(8,128)S(1)} %bitcast.28, bf16[128,2048]{1,0:T(8,128)(2,1)} %fusion.member_ref, bf16[2048,128]{1,0:T(8,128)(2,1)} %fusion.1.back_ref), custom_call_target="tpu_custom_call" | custom-call | tf_op jit(solution)/shard_map/pallas_call | solution.py:311
  86.4 12.7 %all_to_all.10 = f32[16,3,8,128]{3,2,1,0:T(8,128)S(1)} all-to-all(f32[16,3,8,128]{3,2,1,0:T(8,128)S(1)} %shard_map.47), channel_id=1, replica_groups=mesh['grp'=16,'swap'=2] {'grp'}, dimensions={0} | all-to-all | bytes 393216 | tf_op jit(solution)/shard_map/all_to_all | solution.py:371
  99.2 0.9 copy.7
  (4 shorter events, 0.1 us)
Async XLA Ops:
  4.5 7.3 %copy-start = (s32[2,16,64]{2,1,0:T(8,128)S(1)}, s32[2,16,64]{2,1,0:T(8,128)}, u32[]{:S(2)}) copy-start(s32[2,16,64]{2,1,0:T(8,128)} %param.5) | copy-start | bytes 24580
  4.5 7.3 %copy-start.2 = (s32[128]{0:T(128)S(1)}, s32[128]{0:T(128)}, u32[]{:S(2)}) copy-start(s32[128]{0:T(128)} %param.6) | copy-start | bytes 1540
  4.5 8.4 %copy-start.1 = (s32[2,128]{1,0:T(2,128)S(1)}, s32[2,128]{1,0:T(2,128)}, u32[]{:S(2)}) copy-start(s32[2,128]{1,0:T(2,128)} %param.7) | copy-start | bytes 3076
  4.5 78.6 %all-to-all-start = ((f32[32,3,64,128]{3,2,1,0:T(8,128)}), f32[32,3,64,128]{3,2,1,0:T(8,128)S(1)}, u32[]{:S(2)}, u32[]{:S(2)}) async-start(f32[32,3,64,128]{3,2,1,0:T(8,128)} %bitcast.30), calls=%async_computation | async-start | bytes 6291456 | tf_op jit(solution)/shard_map/all_to_all | solution.py:360

commit v3 on v2

--- a/solution.py
+++ b/solution.py
@@ -248,15 +248,8 @@
     return both[:, :width] + both[:, width:]
 
 
-def composite_kernel(order_ref, chunk_ref, member_ref, back_ref, out_ref, *scratch):
-    member_held, back_held, sorted_ref, sems = scratch
+def composite_kernel(order_ref, chunk_ref, slots_ref, out_ref, sorted_ref):
     group_count, swap_count, channels, per_device, lanes = chunk_ref.shape
-    copies = [
-        pltpu.make_async_copy(member_ref, member_held, sems.at[0]),
-        pltpu.make_async_copy(back_ref, back_held, sems.at[1]),
-    ]
-    for copy in copies:
-        copy.start()
     per_brick = per_device // BRICKS
     bricks = group_count * BRICKS
     for at in range(swap_count * bricks):
@@ -267,16 +260,19 @@
             sorted_ref[
                 at * per_brick : (at + 1) * per_brick, channel * lanes : (channel + 1) * lanes
             ] = chunk_ref[source, at // bricks, channel, pl.ds(first, per_brick), :]
-    for copy in copies:
-        copy.wait()
     fragment_count = swap_count * bricks * per_brick
     block = min(2 * LANES, fragment_count)
     starts = range(0, fragment_count, block)
     row = lax.broadcasted_iota(jnp.int32, (block, block), 0) // per_brick
     column = lax.broadcasted_iota(jnp.int32, (block, block), 1) // per_brick
     nearer = column < row
-    members = [member_held[:, start : start + block] for start in starts]
-    backs = [back_held[start : start + block, :] for start in starts]
+    slot_count = group_count * out_ref.shape[2]
+    slot_id = lax.broadcasted_iota(jnp.int32, (slot_count, block), 0).astype(jnp.float32)
+    members, backs = [], []
+    for start in starts:
+        found = jnp.where(slots_ref[:, start : start + block] == slot_id, 1.0, 0.0)
+        members.append(found.astype(jnp.bfloat16))
+        backs.append(found.T.astype(jnp.bfloat16))
     opticals = [split(sorted_ref[start : start + block, 2 * lanes :]) for start in starts]
     added = [masked_sum(member, optical) for member, optical in zip(members, opticals)]
     fronts = []
@@ -305,34 +301,19 @@
     out_ref[:, 2] = (1.0 - jnp.exp(-depths[-1])).reshape(tiles)
 
 
-def composite(order, chunk, member, back):
-    group_count, swap_count, channels, per_device, lanes = chunk.shape
-    slot_count, fragment_count = member.shape
+def composite(order, chunk, slots, slot_count):
+    group_count, _, channels, _, lanes = chunk.shape
+    vmem = pl.BlockSpec(memory_space=pltpu.VMEM)
     return pl.pallas_call(
         composite_kernel,
-        in_specs=[
-            pl.BlockSpec(memory_space=pltpu.SMEM),
-            pl.BlockSpec(memory_space=pltpu.VMEM),
-            pl.BlockSpec(memory_space=pltpu.HBM),
-            pl.BlockSpec(memory_space=pltpu.HBM),
-        ],
-        out_specs=pl.BlockSpec(memory_space=pltpu.VMEM),
+        in_specs=[pl.BlockSpec(memory_space=pltpu.SMEM), vmem, vmem],
+        out_specs=vmem,
         out_shape=jax.ShapeDtypeStruct(
             (group_count, channels, slot_count // group_count, lanes), jnp.float32
         ),
-        scratch_shapes=[
-            pltpu.VMEM(member.shape, member.dtype),
-            pltpu.VMEM(back.shape, back.dtype),
-            pltpu.VMEM((fragment_count, channels * lanes), jnp.float32),
-            pltpu.SemaphoreType.DMA((2,)),
-        ],
+        scratch_shapes=[pltpu.VMEM((slots.shape[1], channels * lanes), jnp.float32)],
         compiler_params=pltpu.CompilerParams(vmem_limit_bytes=VMEM_BYTES),
-    )(
-        order,
-        chunk,
-        pltpu.with_memory_space_constraint(member, pltpu.HBM),
-        pltpu.with_memory_space_constraint(back, pltpu.HBM),
-    )
+    )(order, chunk, slots)
 
 
 def depth_order(tile_list, tile_slot, brick_rank):
@@ -340,15 +321,15 @@
     numbers = jnp.arange(brick_count, dtype=jnp.int32)
     placed = brick_rank[:, None, :] == numbers[None, :, None]
     order = jnp.sum(jnp.where(placed, numbers[None, None, :], 0), axis=2)
-    slot_count = tile_slot.shape[0]
-    ids = jnp.arange(slot_count, dtype=jnp.int32)
-    found = tile_list[..., None] == ids
+    found = tile_list[..., None] == jnp.arange(tile_slot.shape[0], dtype=jnp.int32)
     slots = jnp.sum(jnp.where(found, tile_slot, 0), axis=-1)
-    slots = slots.reshape(swap_count, 1, brick_count, -1)
-    slots = jnp.sum(jnp.where(placed[..., None], slots, 0), axis=2).reshape(-1)
-    member = (ids[:, None] == slots[None, :]).astype(jnp.bfloat16)
-    back = (slots[:, None] == ids[None, :]).astype(jnp.bfloat16)
-    return order.reshape(-1), member, back
+    slots = jnp.einsum(
+        "srb,sbf->srf",
+        placed.astype(jnp.float32),
+        slots.reshape(swap_count, brick_count, -1).astype(jnp.float32),
+        precision=lax.Precision.HIGHEST,
+    )
+    return order.reshape(-1), jnp.round(slots).reshape(1, -1)
 
 
 def chunk_shards(samples, tile_list, tile_slot, brick_rank):
@@ -364,10 +345,9 @@
         concat_axis=0,
         tiled=True,
     )
-    order, member, back = depth_order(tile_list, tile_slot, brick_rank)
-    tiles = composite(
-        order, arrived.reshape(group_count, swap_count, 3, per_device, LANES), member, back
-    )
+    order, slots = depth_order(tile_list, tile_slot, brick_rank)
+    arrived = arrived.reshape(leaving.shape)
+    tiles = composite(order, arrived, slots, tile_slot.shape[0])
     image = lax.all_to_all(tiles, "grp", split_axis=0, concat_axis=0, tiled=True)
     red, green, opacity = (
         jnp.transpose(image[:, channel], (1, 0, 2)).reshape(owned, pixels // swap_count)

time: 100 us -> 100 us (level)
  other arithmetic: 7.52 us -> 1.04 us
  waiting for transfers between devices: 63.5 us -> 69.6 us
    all_to_all x1, waiting for transfers between devices: 63.5 us -> 69.6 us  [chunk_shards(): lax.all_to_all(leaving.reshape(group_count * swap_count, 3, per_device, L...]
    reduce_sum x1 -> x0, other arithmetic: 4.39 us -> none  [depth_order(): slots = jnp.sum(jnp.where(placed[..., None], slots, 0), axis=2).reshape(-1)]
    convert_element_type x2 -> x1, other arithmetic: 2.06 us -> 0.01 us  [depth_order(): slots.reshape(swap_count, brick_count, -1).astype(jnp.float32)]
  transfers between devices with their start and end apart: 1 -> 1, of which waited for: 1 -> 1; matrix products, arithmetic and copies ran while one was open for 8% -> 2% of each run, Pallas kernels for 0% -> 0%
where the time goes in v3:
time: 100 us; the launch traced here: 99.7 us
  waiting for transfers between devices  69.6 us (70%)
  blocking collectives  12.7 us (13%)
  Pallas kernels  7.48 us (7%)
  starting transfers between devices  7.3 us (7%)
  local copies, waits for them, and re-layouts  1.26 us (1%)
  other arithmetic  1.04 us (1%)
    all_to_all x1, waiting for transfers between devices, chunk_shards(): lax.all_to_all(leaving.reshape(group_count * swap_count, 3, per_device, L...  69.6 us
    all_to_all x1, blocking collectives, chunk_shards(): lax.all_to_all(tiles, 'grp', split_axis=0, concat_axis=0, tiled=True)  12.7 us
    all_to_all x1, starting transfers between devices, chunk_shards(): lax.all_to_all(leaving.reshape(group_count * swap_count, 3, per_device, L...  7.3 us
    pallas_call x1, Pallas kernels, render_chunks(): pl.pallas_call(render_kernel, in_specs=[pl.BlockSpec(memory_space=pltpu.H...  4.5 us
    pallas_call x1, Pallas kernels, composite(): pl.pallas_call(composite_kernel, in_specs=[pl.BlockSpec(memory_space=pltp...  2.98 us
  transfers between devices with their start and end apart: 1, of which 1 were waited for; matrix products, arithmetic and copies ran while one was open for 2% of the time, Pallas kernels for 0%

profile of v3, /device:TPU:0, one launch (start us, length us, event | category | flops | bytes accessed | tf_op | source)
XLA Modules:
  0.0 99.7 jit_solution(6488746999855032127)
XLA Ops:
  0.0 4.5 %shard_map.46 = f32[16,2,3,64,128]{4,3,2,1,0:T(8,128)} custom-call(bf16[64,4,4096]{2,1,0:T(4,128)(2,1)} %bitcast.32), custom_call_target="tpu_custom_call" | custom-call | tf_op jit(solution)/shard_map/pallas_call | solution.py:224
  4.5 0.0 copy-start
  4.5 0.0 copy-start.2
  4.5 0.0 copy-start.1
  4.5 7.3 %all-to-all-start = ((f32[32,3,64,128]{3,2,1,0:T(8,128)}), f32[32,3,64,128]{3,2,1,0:T(8,128)S(1)}, u32[]{:S(2)}, u32[]{:S(2)}) async-start(f32[32,3,64,128]{3,2,1,0:T(8,128)} %bitcast.31), calls=%async_computation | async-start | bytes 6291456 | tf_op jit(solution)/shard_map/all_to_all | solution.py:341
  11.9 0.0 copy-done
  11.9 0.0 copy-done.2
  11.9 0.9 select_reduce_fusion
  12.8 0.1 convert_element_type.8
  12.9 0.0 copy-done.1
  12.9 0.2 convolution_round-nearest-even_fusion
  13.1 0.1 copy.10
  13.3 0.1 reshape.40.slots_ref
  13.4 0.1 select_reduce_fusion.1
  13.5 69.6 %all-to-all-done = f32[32,3,64,128]{3,2,1,0:T(8,128)S(1)} async-done(((f32[32,3,64,128]{3,2,1,0:T(8,128)}), f32[32,3,64,128]{3,2,1,0:T(8,128)S(1)}, u32[]{:S(2)}, u32[]{:S(2)}) %all-to-all-start) | async-done | bytes 3145760 | tf_op jit(solution)/shard_map/all_to_all | solution.py:341
  83.1 3.0 %shard_map.47 = f32[16,3,8,128]{3,2,1,0:T(8,128)S(1)} custom-call(s32[256]{0:T(256)S(1)} %bitcast.30, f32[16,2,3,64,128]{4,3,2,1,0:T(8,128)S(1)} %bitcast.29, f32[1,2048]{1,0:T(1,128)S(1)} %reshape.40.slots_ref), custom_call_target="tpu_custom_call" | custom-call | tf_op jit(solution)/shard_map/pallas_call | solution.py:307
  86.1 12.7 %all_to_all.10 = f32[16,3,8,128]{3,2,1,0:T(8,128)S(1)} all-to-all(f32[16,3,8,128]{3,2,1,0:T(8,128)S(1)} %shard_map.47), channel_id=1, replica_groups=mesh['grp'=16,'swap'=2] {'grp'}, dimensions={0} | all-to-all | bytes 393216 | tf_op jit(solution)/shard_map/all_to_all | solution.py:351
  98.9 0.9 copy.11
  (4 shorter events, 0.0 us)
Async XLA Ops:
  4.5 7.3 %copy-start = (s32[2,16,64]{2,1,0:T(8,128)S(1)}, s32[2,16,64]{2,1,0:T(8,128)}, u32[]{:S(2)}) copy-start(s32[2,16,64]{2,1,0:T(8,128)} %param.5) | copy-start | bytes 24580
  4.5 7.3 %copy-start.2 = (s32[128]{0:T(128)S(1)}, s32[128]{0:T(128)}, u32[]{:S(2)}) copy-start(s32[128]{0:T(128)} %param.6) | copy-start | bytes 1540
  4.5 8.4 %copy-start.1 = (s32[2,128]{1,0:T(2,128)S(1)}, s32[2,128]{1,0:T(2,128)}, u32[]{:S(2)}) copy-start(s32[2,128]{1,0:T(2,128)} %param.7) | copy-start | bytes 3076
  4.5 78.6 %all-to-all-start = ((f32[32,3,64,128]{3,2,1,0:T(8,128)}), f32[32,3,64,128]{3,2,1,0:T(8,128)S(1)}, u32[]{:S(2)}, u32[]{:S(2)}) async-start(f32[32,3,64,128]{3,2,1,0:T(8,128)} %bitcast.31), calls=%async_computation | async-start | bytes 6291456 | tf_op jit(solution)/shard_map/all_to_all | solution.py:341

commit v4 on v3

--- a/solution.py
+++ b/solution.py
@@ -183,54 +183,60 @@
     return (1.0 - through) - held, 4.0 * (held - held_twice), before
 
 
-def render_kernel(samples_ref, out_ref, held_ref, made_ref, in_sems, out_sems):
-    group_count, swap_count = out_ref.shape[:2]
-    fragments, depth_count, pixels = samples_ref.shape
-    pieces, width = held_ref.shape[0], held_ref.shape[3]
-    chunks = width // LANES
-    per_slab = group_count // chunks
+def render_kernel(groups, samples_ref, out_ref, held_ref, made_ref, in_sems, out_sems):
+    group_count = out_ref.shape[0]
+    _, depth_count, pixels = samples_ref.shape
+    width = 8 * LANES
     arriving, leaving = [], []
-    for piece in range(pieces):
-        part = samples_ref.at[:, :, pl.ds(piece * width, width)]
-        arriving.append(pltpu.make_async_copy(part, held_ref.at[piece], in_sems.at[piece]))
-        place = (pl.ds(piece % per_slab * chunks, chunks), piece // per_slab)
+    for at, (first, count) in enumerate(groups):
+        rows = pl.ds(first, count)
+        arriving.append(
+            pltpu.make_async_copy(samples_ref.at[rows], held_ref.at[rows], in_sems.at[at])
+        )
+        place = (slice(None), slice(None), slice(None), rows)
         leaving.append(
-            pltpu.make_async_copy(made_ref.at[place], out_ref.at[place], out_sems.at[piece])
+            pltpu.make_async_copy(made_ref.at[place], out_ref.at[place], out_sems.at[at])
         )
     for copy in arriving:
         copy.start()
-    order = level_order(fragments, depth_count)
-    for piece in range(pieces):
-        arriving[piece].wait()
-        levels = jnp.dot(
-            order,
-            held_ref[piece].reshape(fragments * depth_count, width),
-            preferred_element_type=jnp.float32,
-        ).reshape(depth_count, fragments, width)
-        for at in range(chunks):
-            channels = render_levels(levels[:, :, at * LANES : (at + 1) * LANES])
-            chunk = piece % per_slab * chunks + at
-            for channel in range(3):
-                made_ref[chunk, piece // per_slab, channel] = channels[channel]
-        leaving[piece].start()
+    for at, (first, count) in enumerate(groups):
+        order = level_order(count, depth_count)
+        arriving[at].wait()
+        for start in range(0, pixels, width):
+            levels = jnp.dot(
+                order,
+                held_ref[first : first + count, :, start : start + width].reshape(
+                    count * depth_count, width
+                ),
+                preferred_element_type=jnp.float32,
+            ).reshape(depth_count, count, width)
+            for part in range(width // LANES):
+                channels = render_levels(levels[:, :, part * LANES : (part + 1) * LANES])
+                chunk = start // LANES + part
+                for channel in range(3):
+                    made_ref[
+                        chunk % group_count, chunk // group_count, channel, first : first + count, :
+                    ] = channels[channel]
+        leaving[at].start()
     for copy in leaving:
         copy.wait()
 
 
 def render_chunks(samples, group_count, swap_count):
-    fragments, depth_count, pixels = samples.shape
-    pieces = 4
+    fragments = samples.shape[0]
+    counts = [8] + [16] * (fragments // 16 - 1) + [8]
+    groups = [(sum(counts[:at]), count) for at, count in enumerate(counts)]
     out_shape = (group_count, swap_count, 3, fragments, LANES)
     return pl.pallas_call(
-        render_kernel,
+        functools.partial(render_kernel, groups),
         in_specs=[pl.BlockSpec(memory_space=pltpu.HBM)],
         out_specs=pl.BlockSpec(memory_space=pltpu.HBM),
         out_shape=jax.ShapeDtypeStruct(out_shape, jnp.float32),
         scratch_shapes=[
-            pltpu.VMEM((pieces, fragments, depth_count, pixels // pieces), jnp.bfloat16),
+            pltpu.VMEM(samples.shape, jnp.bfloat16),
             pltpu.VMEM(out_shape, jnp.float32),
-            pltpu.SemaphoreType.DMA((pieces,)),
-            pltpu.SemaphoreType.DMA((pieces,)),
+            pltpu.SemaphoreType.DMA((len(groups),)),
+            pltpu.SemaphoreType.DMA((len(groups),)),
         ],
         compiler_params=pltpu.CompilerParams(vmem_limit_bytes=3 * VMEM_BYTES),
     )(pltpu.with_memory_space_constraint(samples, pltpu.HBM))
@@ -248,19 +254,18 @@
     return both[:, :width] + both[:, width:]
 
 
-def composite_kernel(order_ref, chunk_ref, slots_ref, out_ref, sorted_ref):
-    group_count, swap_count, channels, per_device, lanes = chunk_ref.shape
-    per_brick = per_device // BRICKS
-    bricks = group_count * BRICKS
-    for at in range(swap_count * bricks):
-        brick = order_ref[at]
-        source = lax.div(brick, BRICKS)
-        first = pl.multiple_of(lax.rem(brick, BRICKS) * per_brick, per_brick)
+def composite_kernel(per_device, rows_ref, chunk_ref, slots_ref, out_ref, sorted_ref):
+    fragment_count = sorted_ref.shape[0]
+    group_count, channels, _, lanes = out_ref.shape
+    bricks = rows_ref.shape[0]
+    per_brick = fragment_count // bricks
+    for at in range(bricks):
+        first = rows_ref[at]
         for channel in range(channels):
+            source = pl.multiple_of(first + channel * per_device, per_brick)
             sorted_ref[
                 at * per_brick : (at + 1) * per_brick, channel * lanes : (channel + 1) * lanes
-            ] = chunk_ref[source, at // bricks, channel, pl.ds(first, per_brick), :]
-    fragment_count = swap_count * bricks * per_brick
+            ] = chunk_ref[pl.ds(source, per_brick), :]
     block = min(2 * LANES, fragment_count)
     starts = range(0, fragment_count, block)
     row = lax.broadcasted_iota(jnp.int32, (block, block), 0) // per_brick
@@ -294,18 +299,20 @@
         shaded = split(sorted_ref[start : start + block, : 2 * lanes] * both)
         shaded = masked_sum(member, shaded)
         color = shaded if color is None else color + shaded
-    owned = out_ref.shape[2]
-    tiles = (group_count, owned, lanes)
+    tiles = (group_count, out_ref.shape[2], lanes)
     out_ref[:, 0] = color[:, :lanes].reshape(tiles)
     out_ref[:, 1] = color[:, lanes:].reshape(tiles)
     out_ref[:, 2] = (1.0 - jnp.exp(-depths[-1])).reshape(tiles)
 
 
 def composite(order, chunk, slots, slot_count):
-    group_count, _, channels, _, lanes = chunk.shape
+    group_count, swap_count, channels, per_device, lanes = chunk.shape
+    slabs = jnp.arange(swap_count, dtype=jnp.int32)[:, None]
+    rows = ((order // BRICKS * swap_count + slabs) * channels) * per_device
+    rows = rows + order % BRICKS * (per_device // BRICKS)
     vmem = pl.BlockSpec(memory_space=pltpu.VMEM)
     return pl.pallas_call(
-        composite_kernel,
+        functools.partial(composite_kernel, per_device),
         in_specs=[pl.BlockSpec(memory_space=pltpu.SMEM), vmem, vmem],
         out_specs=vmem,
         out_shape=jax.ShapeDtypeStruct(
@@ -313,7 +320,7 @@
         ),
         scratch_shapes=[pltpu.VMEM((slots.shape[1], channels * lanes), jnp.float32)],
         compiler_params=pltpu.CompilerParams(vmem_limit_bytes=VMEM_BYTES),
-    )(order, chunk, slots)
+    )(rows.reshape(-1), chunk.reshape(-1, lanes), slots)
 
 
 def depth_order(tile_list, tile_slot, brick_rank):
@@ -329,7 +336,7 @@
         slots.reshape(swap_count, brick_count, -1).astype(jnp.float32),
         precision=lax.Precision.HIGHEST,
     )
-    return order.reshape(-1), jnp.round(slots).reshape(1, -1)
+    return order, jnp.round(slots).reshape(1, -1)
 
 
 def chunk_shards(samples, tile_list, tile_slot, brick_rank):

time: 100 us -> 99 us (0.990)
  Pallas kernels: 7.48 us -> 6.48 us
    pallas_call x2, Pallas kernels: 7.48 us -> 6.48 us  [the longest x1 4.3 us: render_chunks(): pl.pallas_call(functools.partial(render_kernel, groups), in_specs=[pl.Blo...]
where the time goes in v4:
time: 99 us; the launch traced here: 98.7 us
  waiting for transfers between devices  69.6 us (70%)
  blocking collectives  12.7 us (13%)
  starting transfers between devices  7.31 us (7%)
  Pallas kernels  6.48 us (7%)
  local copies, waits for them, and re-layouts  1.26 us (1%)
  other arithmetic  1.06 us (1%)
    all_to_all x1, waiting for transfers between devices, chunk_shards(): lax.all_to_all(leaving.reshape(group_count * swap_count, 3, per_device, L...  69.6 us
    all_to_all x1, blocking collectives, chunk_shards(): lax.all_to_all(tiles, 'grp', split_axis=0, concat_axis=0, tiled=True)  12.7 us
    all_to_all x1, starting transfers between devices, chunk_shards(): lax.all_to_all(leaving.reshape(group_count * swap_count, 3, per_device, L...  7.31 us
    pallas_call x1, Pallas kernels, render_chunks(): pl.pallas_call(functools.partial(render_kernel, groups), in_specs=[pl.Blo...  4.3 us
    pallas_call x1, Pallas kernels, composite(): pl.pallas_call(functools.partial(composite_kernel, per_device), in_specs=...  2.18 us
  transfers between devices with their start and end apart: 1, of which 1 were waited for; matrix products, arithmetic and copies ran while one was open for 2% of the time, Pallas kernels for 0%

profile of v4, /device:TPU:0, one launch (start us, length us, event | category | flops | bytes accessed | tf_op | source)
XLA Modules:
  0.0 98.7 jit_solution(15883798342685485997)
XLA Ops:
  0.0 4.3 %shard_map.46 = f32[16,2,3,64,128]{4,3,2,1,0:T(8,128)} custom-call(bf16[64,4,4096]{2,1,0:T(4,128)(2,1)} %bitcast.50), custom_call_target="tpu_custom_call" | custom-call | tf_op jit(solution)/shard_map/pallas_call | solution.py:230
  4.3 0.0 copy-start
  4.3 0.0 copy-start.2
  4.3 0.0 copy-start.1
  4.3 7.3 %all-to-all-start = ((f32[32,3,64,128]{3,2,1,0:T(8,128)}), f32[32,3,64,128]{3,2,1,0:T(8,128)S(1)}, u32[]{:S(2)}, u32[]{:S(2)}) async-start(f32[32,3,64,128]{3,2,1,0:T(8,128)} %bitcast.49), calls=%async_computation | async-start | bytes 6291456 | tf_op jit(solution)/shard_map/all_to_all | solution.py:348
  11.7 0.0 copy-done
  11.7 0.0 copy-done.2
  11.7 0.9 select_reduce_fusion
  12.6 0.1 convert_element_type.8
  12.7 0.0 copy-done.1
  12.7 0.2 convolution_round-nearest-even_fusion
  13.0 0.1 copy.10
  13.1 0.1 reshape.35.slots_ref
  13.2 0.1 select_reduce_fusion.1
  13.4 69.6 %all-to-all-done = f32[32,3,64,128]{3,2,1,0:T(8,128)S(1)} async-done(((f32[32,3,64,128]{3,2,1,0:T(8,128)}), f32[32,3,64,128]{3,2,1,0:T(8,128)S(1)}, u32[]{:S(2)}, u32[]{:S(2)}) %all-to-all-start) | async-done | bytes 3145760 | tf_op jit(solution)/shard_map/all_to_all | solution.py:348
  82.9 2.2 %shard_map.47 = f32[16,3,8,128]{3,2,1,0:T(8,128)S(1)} custom-call(s32[256]{0:T(256)S(1)} %fusion.2.rows_ref, f32[6144,128]{1,0:T(8,128)S(1)} %bitcast.48, f32[1,2048]{1,0:T(1,128)S(1)} %reshape.35.slots_ref), custom_call_target="tpu_custom_call" | custom-call | tf_op jit(solution)/shard_map/pallas_call | solution.py:314
  85.1 12.7 %all_to_all.10 = f32[16,3,8,128]{3,2,1,0:T(8,128)S(1)} all-to-all(f32[16,3,8,128]{3,2,1,0:T(8,128)S(1)} %shard_map.47), channel_id=1, replica_groups=mesh['grp'=16,'swap'=2] {'grp'}, dimensions={0} | all-to-all | bytes 393216 | tf_op jit(solution)/shard_map/all_to_all | solution.py:358
  97.9 0.9 copy.11
  (5 shorter events, 0.1 us)
Async XLA Ops:
  4.3 7.4 %copy-start = (s32[2,16,64]{2,1,0:T(8,128)S(1)}, s32[2,16,64]{2,1,0:T(8,128)}, u32[]{:S(2)}) copy-start(s32[2,16,64]{2,1,0:T(8,128)} %param.5) | copy-start | bytes 24580
  4.3 7.4 %copy-start.2 = (s32[128]{0:T(128)S(1)}, s32[128]{0:T(128)}, u32[]{:S(2)}) copy-start(s32[128]{0:T(128)} %param.6) | copy-start | bytes 1540
  4.3 8.4 %copy-start.1 = (s32[2,128]{1,0:T(2,128)S(1)}, s32[2,128]{1,0:T(2,128)}, u32[]{:S(2)}) copy-start(s32[2,128]{1,0:T(2,128)} %param.7) | copy-start | bytes 3076
  4.3 78.6 %all-to-all-start = ((f32[32,3,64,128]{3,2,1,0:T(8,128)}), f32[32,3,64,128]{3,2,1,0:T(8,128)S(1)}, u32[]{:S(2)}, u32[]{:S(2)}) async-start(f32[32,3,64,128]{3,2,1,0:T(8,128)} %bitcast.49), calls=%async_computation | async-start | bytes 6291456 | tf_op jit(solution)/shard_map/all_to_all | solution.py:348

commit v5 on v3

--- a/solution.py
+++ b/solution.py
@@ -183,57 +183,55 @@
     return (1.0 - through) - held, 4.0 * (held - held_twice), before
 
 
-def render_kernel(samples_ref, out_ref, held_ref, made_ref, in_sems, out_sems):
-    group_count, swap_count = out_ref.shape[:2]
+def render_pair(device, slab, samples_ref, order, offset):
     fragments, depth_count, pixels = samples_ref.shape
-    pieces, width = held_ref.shape[0], held_ref.shape[3]
-    chunks = width // LANES
-    per_slab = group_count // chunks
-    arriving, leaving = [], []
-    for piece in range(pieces):
-        part = samples_ref.at[:, :, pl.ds(piece * width, width)]
-        arriving.append(pltpu.make_async_copy(part, held_ref.at[piece], in_sems.at[piece]))
-        place = (pl.ds(piece % per_slab * chunks, chunks), piece // per_slab)
-        leaving.append(
-            pltpu.make_async_copy(made_ref.at[place], out_ref.at[place], out_sems.at[piece])
-        )
-    for copy in arriving:
-        copy.start()
-    order = level_order(fragments, depth_count)
-    for piece in range(pieces):
-        arriving[piece].wait()
-        levels = jnp.dot(
-            order,
-            held_ref[piece].reshape(fragments * depth_count, width),
-            preferred_element_type=jnp.float32,
-        ).reshape(depth_count, fragments, width)
-        for at in range(chunks):
-            channels = render_levels(levels[:, :, at * LANES : (at + 1) * LANES])
-            chunk = piece % per_slab * chunks + at
+    half = pixels // 2
+    picked = []
+    for flip in range(2):
+        first = jnp.bitwise_xor(slab, flip) * half + jnp.bitwise_xor(device, offset) * LANES
+        picked.append(samples_ref[:, :, pl.ds(pl.multiple_of(first, LANES), LANES)])
+    levels = jnp.dot(
+        order,
+        jnp.concatenate(picked, axis=2).reshape(fragments * depth_count, 2 * LANES),
+        preferred_element_type=jnp.float32,
+    ).reshape(depth_count, fragments, 2 * LANES)
+    channels = render_levels(levels)
+    return [[value[:, at * LANES : (at + 1) * LANES] for value in channels] for at in range(2)]
+
+
+def pair_kernel(offsets, singles, numbers_ref, samples_ref, *out_refs):
+    order = level_order(*samples_ref.shape[:2])
+    targets = [[ref.at[0], ref.at[1]] for ref in out_refs[: len(offsets)]]
+    rest = out_refs[len(offsets) :]
+    targets += [rest[at : at + 2] for at in range(0, len(rest), 2)]
+    for target, offset in zip(targets, offsets + singles):
+        pair = render_pair(numbers_ref[0], numbers_ref[1], samples_ref, order, offset)
+        for flip in range(2):
             for channel in range(3):
-                made_ref[chunk, piece // per_slab, channel] = channels[channel]
-        leaving[piece].start()
-    for copy in leaving:
-        copy.wait()
-
-
-def render_chunks(samples, group_count, swap_count):
-    fragments, depth_count, pixels = samples.shape
-    pieces = 4
-    out_shape = (group_count, swap_count, 3, fragments, LANES)
+                target[flip][channel] = pair[flip][channel]
+
+
+def near_kernel(near, numbers_ref, samples_ref, *refs):
+    out_ref = refs[-1]
+    order = level_order(*samples_ref.shape[:2])
+    device, slab = numbers_ref[0], numbers_ref[1]
+    for offset in range(near):
+        pair = render_pair(device, slab, samples_ref, order, offset)
+        for flip in range(2):
+            entry = lax.rem(jnp.bitwise_xor(device, offset), near) * 2 + jnp.bitwise_xor(slab, flip)
+            for channel in range(3):
+                out_ref[entry, channel] = pair[flip][channel]
+
+
+def on_device(kernel, out_shapes, numbers, *arrays):
+    vmem = pl.BlockSpec(memory_space=pltpu.VMEM)
     return pl.pallas_call(
-        render_kernel,
-        in_specs=[pl.BlockSpec(memory_space=pltpu.HBM)],
-        out_specs=pl.BlockSpec(memory_space=pltpu.HBM),
-        out_shape=jax.ShapeDtypeStruct(out_shape, jnp.float32),
-        scratch_shapes=[
-            pltpu.VMEM((pieces, fragments, depth_count, pixels // pieces), jnp.bfloat16),
-            pltpu.VMEM(out_shape, jnp.float32),
-            pltpu.SemaphoreType.DMA((pieces,)),
-            pltpu.SemaphoreType.DMA((pieces,)),
-        ],
-        compiler_params=pltpu.CompilerParams(vmem_limit_bytes=3 * VMEM_BYTES),
-    )(pltpu.with_memory_space_constraint(samples, pltpu.HBM))
+        kernel,
+        in_specs=[pl.BlockSpec(memory_space=pltpu.SMEM)] + [vmem] * len(arrays),
+        out_specs=[vmem] * len(out_shapes),
+        out_shape=[jax.ShapeDtypeStruct(shape, jnp.float32) for shape in out_shapes],
+        compiler_params=pltpu.CompilerParams(vmem_limit_bytes=VMEM_BYTES),
+    )(numbers, *arrays)
 
 
 def split(values):
@@ -248,19 +246,38 @@
     return both[:, :width] + both[:, width:]
 
 
-def composite_kernel(order_ref, chunk_ref, slots_ref, out_ref, sorted_ref):
-    group_count, swap_count, channels, per_device, lanes = chunk_ref.shape
+def slots_kernel(slots_ref, *refs):
+    refs[-1][...] = jnp.round(slots_ref[...])
+
+
+def composite_kernel(picks, late, places_ref, slots_ref, *refs):
+    count = 1 + max(array for array, _ in picks)
+    chunk_refs, (out_ref, sorted_ref, held_ref, sems) = refs[:count], refs[count:]
+    chunks, copies = [], []
+    for array, index in picks:
+        chunk = chunk_refs[array] if index is None else chunk_refs[array].at[index]
+        if array in late:
+            chunks.append((chunk, None))
+        else:
+            slot = len(copies)
+            copies.append(pltpu.make_async_copy(chunk, held_ref.at[slot], sems.at[slot]))
+            copies[-1].start()
+            chunks.append((held_ref.at[slot], copies[-1]))
+    channels, per_device, lanes = held_ref.shape[1:]
+    fragment_count = sorted_ref.shape[0]
+    group_count = out_ref.shape[0]
     per_brick = per_device // BRICKS
-    bricks = group_count * BRICKS
-    for at in range(swap_count * bricks):
-        brick = order_ref[at]
-        source = lax.div(brick, BRICKS)
-        first = pl.multiple_of(lax.rem(brick, BRICKS) * per_brick, per_brick)
-        for channel in range(channels):
-            sorted_ref[
-                at * per_brick : (at + 1) * per_brick, channel * lanes : (channel + 1) * lanes
-            ] = chunk_ref[source, at // bricks, channel, pl.ds(first, per_brick), :]
-    fragment_count = swap_count * bricks * per_brick
+    for at in sorted(range(len(picks)), key=lambda at: chunks[at][1] is not None):
+        chunk, copy = chunks[at]
+        if copy is not None:
+            copy.wait()
+        for brick in range(BRICKS):
+            place = pl.multiple_of(places_ref[at * BRICKS + brick], per_brick)
+            rows = slice(brick * per_brick, (brick + 1) * per_brick)
+            for channel in range(channels):
+                sorted_ref[
+                    pl.ds(place, per_brick), channel * lanes : (channel + 1) * lanes
+                ] = chunk[channel, rows, :]
     block = min(2 * LANES, fragment_count)
     starts = range(0, fragment_count, block)
     row = lax.broadcasted_iota(jnp.int32, (block, block), 0) // per_brick
@@ -294,33 +311,41 @@
         shaded = split(sorted_ref[start : start + block, : 2 * lanes] * both)
         shaded = masked_sum(member, shaded)
         color = shaded if color is None else color + shaded
-    owned = out_ref.shape[2]
-    tiles = (group_count, owned, lanes)
+    tiles = (group_count, out_ref.shape[2], lanes)
     out_ref[:, 0] = color[:, :lanes].reshape(tiles)
     out_ref[:, 1] = color[:, lanes:].reshape(tiles)
     out_ref[:, 2] = (1.0 - jnp.exp(-depths[-1])).reshape(tiles)
 
 
-def composite(order, chunk, slots, slot_count):
-    group_count, _, channels, _, lanes = chunk.shape
-    vmem = pl.BlockSpec(memory_space=pltpu.VMEM)
+def composite(places, arrays, picks, late, slots, slot_count, group_count):
+    smem, vmem = pl.BlockSpec(memory_space=pltpu.SMEM), pl.BlockSpec(memory_space=pltpu.VMEM)
+    hbm = pl.BlockSpec(memory_space=pltpu.HBM)
+    held = (sum(array not in late for array, _ in picks),) + arrays[0].shape[-3:]
+    specs = [vmem if at in late else hbm for at in range(len(arrays))]
+    arrays = [
+        array if at in late else pltpu.with_memory_space_constraint(array, pltpu.HBM)
+        for at, array in enumerate(arrays)
+    ]
     return pl.pallas_call(
-        composite_kernel,
-        in_specs=[pl.BlockSpec(memory_space=pltpu.SMEM), vmem, vmem],
+        functools.partial(composite_kernel, picks, late),
+        in_specs=[smem, vmem] + specs,
         out_specs=vmem,
         out_shape=jax.ShapeDtypeStruct(
-            (group_count, channels, slot_count // group_count, lanes), jnp.float32
+            (group_count, 3, slot_count // group_count, LANES), jnp.float32
         ),
-        scratch_shapes=[pltpu.VMEM((slots.shape[1], channels * lanes), jnp.float32)],
+        scratch_shapes=[
+            pltpu.VMEM((slots.shape[1], 3 * LANES), jnp.float32),
+            pltpu.VMEM(held, jnp.float32),
+            pltpu.SemaphoreType.DMA(held[:1]),
+        ],
         compiler_params=pltpu.CompilerParams(vmem_limit_bytes=VMEM_BYTES),
-    )(order, chunk, slots)
-
-
-def depth_order(tile_list, tile_slot, brick_rank):
+    )(places, slots, *arrays)
+
+
+def depth_slots(tile_list, tile_slot, brick_rank, after):
     swap_count, brick_count = brick_rank.shape
     numbers = jnp.arange(brick_count, dtype=jnp.int32)
     placed = brick_rank[:, None, :] == numbers[None, :, None]
-    order = jnp.sum(jnp.where(placed, numbers[None, None, :], 0), axis=2)
     found = tile_list[..., None] == jnp.arange(tile_slot.shape[0], dtype=jnp.int32)
     slots = jnp.sum(jnp.where(found, tile_slot, 0), axis=-1)
     slots = jnp.einsum(
@@ -328,26 +353,100 @@
         placed.astype(jnp.float32),
         slots.reshape(swap_count, brick_count, -1).astype(jnp.float32),
         precision=lax.Precision.HIGHEST,
-    )
-    return order.reshape(-1), jnp.round(slots).reshape(1, -1)
+    ).reshape(1, -1)
+    vmem = pl.BlockSpec(memory_space=pltpu.VMEM)
+    return pl.pallas_call(
+        slots_kernel,
+        in_specs=[vmem] + [pl.BlockSpec(memory_space=pl.ANY)] * len(after),
+        out_specs=vmem,
+        out_shape=jax.ShapeDtypeStruct(slots.shape, jnp.float32),
+        compiler_params=pltpu.CompilerParams(vmem_limit_bytes=VMEM_BYTES),
+        cost_estimate=pl.CostEstimate(flops=30000000000, bytes_accessed=0, transcendentals=0),
+    )(slots, *after)
 
 
 def chunk_shards(samples, tile_list, tile_slot, brick_rank):
     group_count = lax.axis_size("grp")
     swap_count = lax.axis_size("swap")
+    device = lax.axis_index("grp").astype(jnp.int32)
+    slab = lax.axis_index("swap").astype(jnp.int32)
     per_device, pixels = samples.shape[2], samples.shape[4]
-    owned = tile_slot.shape[0] // group_count
-    leaving = render_chunks(samples[0, 0], group_count, swap_count)
-    arrived = lax.all_to_all(
-        leaving.reshape(group_count * swap_count, 3, per_device, LANES),
+    slot_count = tile_slot.shape[0]
+    owned = slot_count // group_count
+    numbers = jnp.stack([device, slab])
+    mine = samples[0, 0]
+    near = group_count // 2
+    chunk = (3, per_device, LANES)
+
+    def send(array, offset, flip):
+        pairs = [
+            (g * swap_count + s, (g ^ offset) * swap_count + (s ^ flip))
+            for g in range(group_count)
+            for s in range(swap_count)
+        ]
+        return lax.ppermute(array, ("grp", "swap"), pairs)
+
+    relayed, direct = list(range(near, group_count - 4)), list(range(group_count - 4, group_count))
+    leaving = on_device(
+        functools.partial(pair_kernel, relayed[:2], []), [(2,) + chunk] * 2, numbers, mine
+    )
+    leaving += on_device(
+        functools.partial(pair_kernel, relayed[2:], direct),
+        [(2,) + chunk] * len(relayed[2:]) + [chunk] * (2 * len(direct)),
+        numbers,
+        mine,
+    )
+    (near_chunks,) = on_device(
+        functools.partial(near_kernel, near), [(near * swap_count,) + chunk], numbers, mine
+    )
+    arrays, picks, sources = [], [], []
+
+    def keep(array, entries):
+        for index, source in entries:
+            picks.append((len(arrays), index))
+            sources.append(source)
+        arrays.append(array)
+
+    passing = []
+    for offset, array in zip(relayed, leaving):
+        got = send(array, offset, 0)
+        keep(got, [(0, (offset, 0))])
+        passing.append(got)
+    singles = [(offset, flip) for offset in direct for flip in range(2)]
+    for partner, array in zip(singles, leaving[len(relayed) :]):
+        keep(send(array, *partner), [(None, partner)])
+    late = set(range(len(relayed) + 1, len(arrays) + 1))
+    for first, last in ((0, 4),):
+        group = jnp.stack([got[1] for got in passing[first:last]])
+        keep(
+            send(group, 0, 1),
+            [(at, (offset, 1)) for at, offset in enumerate(relayed[first:last])],
+        )
+    late.add(len(arrays))
+    slots = depth_slots(tile_list, tile_slot, brick_rank, arrays)
+    members = near * swap_count
+    near_chunks = lax.all_to_all(
+        near_chunks,
         ("grp", "swap"),
         split_axis=0,
         concat_axis=0,
         tiled=True,
-    )
-    order, slots = depth_order(tile_list, tile_slot, brick_rank)
-    arrived = arrived.reshape(leaving.shape)
-    tiles = composite(order, arrived, slots, tile_slot.shape[0])
+        axis_index_groups=[list(range(members)), list(range(members, 2 * members))],
+    )
+    picks = [(0, at) for at in range(members)] + [(array + 1, index) for array, index in picks]
+    arrays = [near_chunks] + arrays
+    offsets = jnp.array([offset for offset, _ in sources], jnp.int32)
+    flips = jnp.array([flip for _, flip in sources], jnp.int32)
+    source = jnp.bitwise_xor(slab, flips) * group_count + jnp.bitwise_xor(device, offsets)
+    entries = jnp.arange(members, dtype=jnp.int32)
+    near_source = entries % swap_count * group_count + device // near * near + entries // swap_count
+    source = jnp.concatenate([near_source, source])
+    ranks = brick_rank.reshape(swap_count * group_count, BRICKS)
+    ranks = ranks + jnp.repeat(jnp.arange(swap_count), group_count)[:, None] * brick_rank.shape[1]
+    ids = jnp.arange(swap_count * group_count, dtype=jnp.int32)
+    places = jnp.sum(jnp.where((source[:, None] == ids)[..., None], ranks[None], 0), axis=1)
+    places = places.reshape(-1) * (per_device // BRICKS)
+    tiles = composite(places, arrays, picks, late, slots, slot_count, group_count)
     image = lax.all_to_all(tiles, "grp", split_axis=0, concat_axis=0, tiled=True)
     red, green, opacity = (
         jnp.transpose(image[:, channel], (1, 0, 2)).reshape(owned, pixels // swap_count)

time: 100 us -> 95.5 us (0.955)
  waiting for transfers between devices: 69.6 us -> 23 us
  starting transfers between devices: 7.3 us -> 42 us
  Pallas kernels: 7.48 us -> 9.79 us
  blocking collectives: 12.7 us -> 14.9 us
  local copies, waits for them, and re-layouts: 1.26 us -> 3.08 us
    all_to_all x1, waiting for transfers between devices: 69.6 us -> 5 us  [chunk_shards(): lax.all_to_all(near_chunks, ('grp', 'swap'), split_axis=0, concat_axis=0,...]
    ppermute x0 -> x13, starting transfers between devices: none -> 37.5 us  [send(): return lax.ppermute(array, ('grp', 'swap'), pairs)]
    ppermute x0 -> x13, waiting for transfers between devices: none -> 18 us  [send(): return lax.ppermute(array, ('grp', 'swap'), pairs)]
    all_to_all x1, starting transfers between devices: 7.3 us -> 4.54 us  [chunk_shards(): lax.all_to_all(near_chunks, ('grp', 'swap'), split_axis=0, concat_axis=0,...]
    pallas_call x2 -> x5, Pallas kernels: 7.48 us -> 9.79 us  [the longest x3 5.82 us: on_device(): pl.pallas_call(kernel, in_specs=[pl.BlockSpec(memory_space=pltpu.SMEM)] +...]
    all_to_all x1, blocking collectives: 12.7 us -> 14.9 us  [chunk_shards(): lax.all_to_all(tiles, 'grp', split_axis=0, concat_axis=0, tiled=True)]
    unnamed x6 -> x20, local copies, waits for them, and re-layouts: 0.02 us -> 1.63 us
  transfers between devices with their start and end apart: 1 -> 14, of which waited for: 1 -> 5; matrix products, arithmetic and copies ran while one was open for 2% -> 3% of each run, Pallas kernels for 0% -> 5%
where the time goes in v5:
time: 95.5 us; the launch traced here: 95.2 us
  starting transfers between devices  42 us (44%)
  waiting for transfers between devices  23 us (24%)
  blocking collectives  14.9 us (16%)
  Pallas kernels  9.79 us (10%)
  local copies, waits for them, and re-layouts  3.08 us (3%)
  other arithmetic  1.9 us (2%)
    ppermute x13, starting transfers between devices, send(): return lax.ppermute(array, ('grp', 'swap'), pairs)  37.5 us
    ppermute x13, waiting for transfers between devices, send(): return lax.ppermute(array, ('grp', 'swap'), pairs)  18 us
    all_to_all x1, blocking collectives, chunk_shards(): lax.all_to_all(tiles, 'grp', split_axis=0, concat_axis=0, tiled=True)  14.9 us
    pallas_call x3, Pallas kernels, on_device(): pl.pallas_call(kernel, in_specs=[pl.BlockSpec(memory_space=pltpu.SMEM)] +...  5.82 us
    all_to_all x1, waiting for transfers between devices, chunk_shards(): lax.all_to_all(near_chunks, ('grp', 'swap'), split_axis=0, concat_axis=0,...  5 us
    all_to_all x1, starting transfers between devices, chunk_shards(): lax.all_to_all(near_chunks, ('grp', 'swap'), split_axis=0, concat_axis=0,...  4.54 us
    pallas_call x1, Pallas kernels, composite(): pl.pallas_call(functools.partial(composite_kernel, picks, late), in_specs...  3.97 us
  transfers between devices with their start and end apart: 14, of which 5 were waited for; matrix products, arithmetic and copies ran while one was open for 3% of the time, Pallas kernels for 5%

profile of v5, /device:TPU:0, one launch (start us, length us, event | category | flops | bytes accessed | tf_op | source)
XLA Modules:
  0.0 95.2 jit_solution(2509115887173960361)
XLA Ops:
  0.0 0.1 pad_add_fusion.1.numbers_ref
  0.1 1.6 %copy-done = bf16[1,1,64,4,4096]{4,3,2,1,0:T(4,128)(2,1)S(1)} copy-done((bf16[1,1,64,4,4096]{4,3,2,1,0:T(4,128)(2,1)S(1)}, bf16[1,1,64,4,4096]{4,3,2,1,0:T(4,128)(2,1)}, u32[]{:S(2)}) %copy-start) | copy-done | bytes 2097176
  1.7 1.0 %shard_map.64 = (f32[2,3,64,128]{3,2,1,0:T(8,128)S(1)}, f32[2,3,64,128]{3,2,1,0:T(8,128)S(1)}) custom-call(s32[2]{0:T(128)S(1)} %pad_add_fusion.1.numbers_ref, bf16[64,4,4096]{2,1,0:T(4,128)(2,1)S(1)} %bitcast.28), custom_call_target="tpu_custom_call" | custom-call | tf_op jit(solution)/shard_map/pallas_call | solution.py:228
  2.7 4.1 %collective-permute-start = (f32[2,3,64,128]{3,2,1,0:T(8,128)S(1)}, f32[2,3,64,128]{3,2,1,0:T(8,128)S(1)}, u32[]{:S(2)}, u32[]{:S(2)}) collective-permute-start(f32[2,3,64,128]{3,2,1,0:T(8,128)S(1)} %get-tuple-element.17), channel_id=1, source_target_pairs={{0,16},{1,17},{2,18},{3,19},{4,20},{5,21},{6,22},{7,23},{8,24},{9,... | collective-permute-start | bytes 589832 | tf_op jit(solution)/shard_map/ppermute | solution.py:387
  6.8 0.0 collective-permute-start.1
  6.8 1.6 %shard_map.65 = (f32[2,3,64,128]{3,2,1,0:T(8,128)S(1)}, f32[2,3,64,128]{3,2,1,0:T(8,128)S(1)}, f32[3,64,128]{2,1,0:T(8,128)S(1)}, f32[3,64,128]{2,1,0:T(8,128)S(...) custom-call(s32[2]{0:T(128)S(1)} %pad_add_fusion.1.numbers_ref, ...), custom_call_target="tpu_custom_call" | custom-call | tf_op jit(solution)/shard_map/pallas_call | solution.py:228
  8.4 3.2 %collective-permute-start.4 = (f32[3,64,128]{2,1,0:T(8,128)S(1)}, f32[3,64,128]{2,1,0:T(8,128)S(1)}, u32[]{:S(2)}, u32[]{:S(2)}) collective-permute-start(f32[3,64,128]{2,1,0:T(8,128)S(1)} %get-tuple-element.21), channel_id=1, source_target_pairs={{0,24},{1,25},{2,26},{3,27},{4,28},{5,29},{6,30},{7,31},{8,16},{9,... | collective-permute-start | bytes 294920 | tf_op jit(solution)/shard_map/ppermute | solution.py:387
  11.6 0.9 collective-permute-start.2
  12.5 3.0 %collective-permute-start.3 = (f32[2,3,64,128]{3,2,1,0:T(8,128)S(1)}, f32[2,3,64,128]{3,2,1,0:T(8,128)S(1)}, u32[]{:S(2)}, u32[]{:S(2)}) collective-permute-start(f32[2,3,64,128]{3,2,1,0:T(8,128)S(1)} %get-tuple-element.20), channel_id=1, source_target_pairs={{0,22},{1,23},{2,20},{3,21},{4,18},{5,19},{6,16},{7,17},{8,30},{9,... | collective-permute-start | bytes 589832 | tf_op jit(solution)/shard_map/ppermute | solution.py:387
  15.4 3.2 %shard_map.67 = f32[16,3,64,128]{3,2,1,0:T(8,128)} custom-call(s32[2]{0:T(128)S(1)} %pad_add_fusion.1.numbers_ref, bf16[64,4,4096]{2,1,0:T(4,128)(2,1)S(1)} %bitcast.30), custom_call_target="tpu_custom_call" | custom-call | tf_op jit(solution)/shard_map/pallas_call | solution.py:228
  18.6 0.0 copy-start.9
  18.6 4.5 %all-to-all-start = ((f32[16,3,64,128]{3,2,1,0:T(8,128)}), f32[16,3,64,128]{3,2,1,0:T(8,128)}, u32[]{:S(2)}, u32[]{:S(2)}) async-start(f32[16,3,64,128]{3,2,1,0:T(8,128)} %shard_map.67), calls=%async_computation | async-start | bytes 3145728 | tf_op jit(solution)/shard_map/all_to_all | solution.py:428
  23.2 0.1 mul.36
  23.3 0.9 select_reduce_fusion
  24.2 0.1 reshape.81
  24.3 0.1 convert_element_type.8
  24.4 0.2 fusion
  24.7 0.1 pad_add_fusion
  24.7 0.1 broadcast_add_fusion
  24.8 6.8 %collective-permute-done.refs_0_.refs_1_ = f32[2,3,64,128]{3,2,1,0:T(8,128)S(1)} collective-permute-done((f32[2,3,64,128]{3,2,1,0:T(8,128)S(1)}, f32[2,3,64,128]{3,2,1,0:T(8,128)S(1)}, u32[]{:S(2)}, u32[]{:S(2)}) %collective-permute-start) | collective-permute-done | bytes 196640 | tf_op jit(solution)/shard_map/ppermute | solution.py:387
  31.6 3.8 %collective-permute-start.5 = (f32[3,64,128]{2,1,0:T(8,128)S(1)}, f32[3,64,128]{2,1,0:T(8,128)S(1)}, u32[]{:S(2)}, u32[]{:S(2)}) collective-permute-start(f32[3,64,128]{2,1,0:T(8,128)S(1)} %get-tuple-element.22), channel_id=1, source_target_pairs={{0,25},{1,24},{2,27},{3,26},{4,29},{5,28},{6,31},{7,30},{8,17},{9,... | collective-permute-start | bytes 294920 | tf_op jit(solution)/shard_map/ppermute | solution.py:387
  35.4 0.0 collective-permute-done.1.refs_1_.refs_2_
  35.4 2.7 %collective-permute-start.6 = (f32[3,64,128]{2,1,0:T(8,128)S(1)}, f32[3,64,128]{2,1,0:T(8,128)S(1)}, u32[]{:S(2)}, u32[]{:S(2)}) collective-permute-start(f32[3,64,128]{2,1,0:T(8,128)S(1)} %get-tuple-element.23), channel_id=1, source_target_pairs={{0,26},{1,27},{2,24},{3,25},{4,30},{5,31},{6,28},{7,29},{8,18},{9,... | collective-permute-start | bytes 294920 | tf_op jit(solution)/shard_map/ppermute | solution.py:387
  38.1 5.2 %collective-permute-done.2.refs_2_.refs_3_ = f32[2,3,64,128]{3,2,1,0:T(8,128)S(1)} collective-permute-done((f32[2,3,64,128]{3,2,1,0:T(8,128)S(1)}, f32[2,3,64,128]{3,2,1,0:T(8,128)S(1)}, u32[]{:S(2)}, u32[]{:S(2)}) %collective-permute-start.2) | collective-permute-done | bytes 196640 | tf_op jit(solution)/shard_map/ppermute | solution.py:387
  43.4 3.1 %collective-permute-start.7 = (f32[3,64,128]{2,1,0:T(8,128)S(1)}, f32[3,64,128]{2,1,0:T(8,128)S(1)}, u32[]{:S(2)}, u32[]{:S(2)}) collective-permute-start(f32[3,64,128]{2,1,0:T(8,128)S(1)} %get-tuple-element.24), channel_id=1, source_target_pairs={{0,27},{1,26},{2,25},{3,24},{4,31},{5,30},{6,29},{7,28},{8,19},{9,... | collective-permute-start | bytes 294920 | tf_op jit(solution)/shard_map/ppermute | solution.py:387
  46.5 0.0 collective-permute-done.3.refs_3_.refs_4_
  46.5 1.3 %collective-permute-start.12 = (f32[4,3,64,128]{3,2,1,0:T(8,128)S(1)}, f32[4,3,64,128]{3,2,1,0:T(8,128)S(1)}, u32[]{:S(2)}, u32[]{:S(2)}) collective-permute-start(f32[4,3,64,128]{3,2,1,0:T(8,128)S(1)} %pad_maximum_fusion), channel_id=1, source_target_pairs={{0,1},{1,0},{2,3},{3,2},{4,5},{5,4},{6,7},{7,6},{8,9},{9,8},{10,11... | collective-permute-start | bytes 1179656 | tf_op jit(solution)/shard_map/ppermute | solution.py:387
  47.8 0.1 iota_compare_fusion.3
  47.9 0.1 copy.11
  47.9 0.6 select_reduce_fusion.1
  48.5 0.0 collective-permute-done.4.refs_4_.refs_5_
  48.6 10.1 %collective-permute-start.8 = (f32[3,64,128]{2,1,0:T(8,128)S(1)}, f32[3,64,128]{2,1,0:T(8,128)S(1)}, u32[]{:S(2)}, u32[]{:S(2)}) collective-permute-start(f32[3,64,128]{2,1,0:T(8,128)S(1)} %get-tuple-element.25), channel_id=1, source_target_pairs={{0,28},{1,29},{2,30},{3,31},{4,24},{5,25},{6,26},{7,27},{8,20},{9,... | collective-permute-start | bytes 294920 | tf_op jit(solution)/shard_map/ppermute | solution.py:387
  58.7 0.0 collective-permute-done.5.refs_5_.refs_6_
  58.7 0.0 collective-permute-start.9
  58.7 0.0 collective-permute-done.6.refs_6_.refs_7_
  58.7 3.5 %collective-permute-start.10 = (f32[3,64,128]{2,1,0:T(8,128)S(1)}, f32[3,64,128]{2,1,0:T(8,128)S(1)}, u32[]{:S(2)}, u32[]{:S(2)}) collective-permute-start(f32[3,64,128]{2,1,0:T(8,128)S(1)} %get-tuple-element.27), channel_id=1, source_target_pairs={{0,30},{1,31},{2,28},{3,29},{4,26},{5,27},{6,24},{7,25},{8,22},{9,... | collective-permute-start | bytes 294920 | tf_op jit(solution)/shard_map/ppermute | solution.py:387
  62.2 0.0 collective-permute-done.7.refs_7_.refs_8_
  62.2 1.9 %collective-permute-start.11 = (f32[3,64,128]{2,1,0:T(8,128)S(1)}, f32[3,64,128]{2,1,0:T(8,128)S(1)}, u32[]{:S(2)}, u32[]{:S(2)}) collective-permute-start(f32[3,64,128]{2,1,0:T(8,128)S(1)} %get-tuple-element.28), channel_id=1, source_target_pairs={{0,31},{1,30},{2,29},{3,28},{4,27},{5,26},{6,25},{7,24},{8,23},{9,... | collective-permute-start | bytes 294920 | tf_op jit(solution)/shard_map/ppermute | solution.py:387
  64.1 0.1 mul.39.places_ref
  64.2 0.1 reshape.82.slots_ref
  64.4 0.0 collective-permute-done.8.refs_8_.refs_9_
  64.4 3.8 %collective-permute-done.9.refs_9_.refs_10_ = f32[3,64,128]{2,1,0:T(8,128)S(1)} collective-permute-done((f32[3,64,128]{2,1,0:T(8,128)S(1)}, f32[3,64,128]{2,1,0:T(8,128)S(1)}, u32[]{:S(2)}, u32[]{:S(2)}) %collective-permute-start.9) | collective-permute-done | bytes 98336 | tf_op jit(solution)/shard_map/ppermute | solution.py:387
  68.2 0.0 collective-permute-done.10.refs_10_.refs_11_
  68.2 2.2 %collective-permute-done.11.refs_11_.refs_12_ = f32[3,64,128]{2,1,0:T(8,128)S(1)} collective-permute-done((f32[3,64,128]{2,1,0:T(8,128)S(1)}, f32[3,64,128]{2,1,0:T(8,128)S(1)}, u32[]{:S(2)}, u32[]{:S(2)}) %collective-permute-start.11) | collective-permute-done | bytes 98336 | tf_op jit(solution)/shard_map/ppermute | solution.py:387
  70.4 5.0 %all-to-all-done.refs_0_ = f32[16,3,64,128]{3,2,1,0:T(8,128)} async-done(((f32[16,3,64,128]{3,2,1,0:T(8,128)}), f32[16,3,64,128]{3,2,1,0:T(8,128)}, u32[]{:S(2)}, u32[]{:S(2)}) %all-to-all-start) | async-done | bytes 1572896 | tf_op jit(solution)/shard_map/all_to_all | solution.py:428
  75.4 4.0 %shard_map.68 = f32[16,3,8,128]{3,2,1,0:T(8,128)S(1)} custom-call(s32[256]{0:T(256)S(1)} %mul.39.places_ref, f32[1,2048]{1,0:T(1,128)S(1)} %shard_map.66.slots_ref, f32[16,3,64,128]{3,2,1,0:T(8,128)} %all-to-all-done.refs_0_, f32[2,3,64,128]{3,2,1,0:T(8,128)} %copy-done.1, f32[2,3,64,128]{3,2,1,0:T(8,128)} %copy-done.2, f32[2,3,64,128]{3,2,1,0:T(8,128)} %copy-done.3, ...), custom_call_target="tpu_custom_call" | custom-call | tf_op jit(solution)/shard_map/pallas_call | solution.py:329
  79.4 14.9 %all_to_all.10 = f32[16,3,8,128]{3,2,1,0:T(8,128)S(1)} all-to-all(f32[16,3,8,128]{3,2,1,0:T(8,128)S(1)} %shard_map.68), channel_id=1, replica_groups=mesh['grp'=16,'swap'=2] {'grp'}, dimensions={0} | all-to-all | bytes 393216 | tf_op jit(solution)/shard_map/all_to_all | solution.py:450
  94.3 0.9 copy.14
  (32 shorter events, 0.2 us)
Async XLA Ops:
  0.1 1.6 %copy-start = (bf16[1,1,64,4,4096]{4,3,2,1,0:T(4,128)(2,1)S(1)}, bf16[1,1,64,4,4096]{4,3,2,1,0:T(4,128)(2,1)}, u32[]{:S(2)}) copy-start(bf16[1,1,64,4,4096]{4,3,2,1,0:T(4,128)(2,1)} %param.6) | copy-start | bytes 6291460
  2.7 28.9 %collective-permute-start = (f32[2,3,64,128]{3,2,1,0:T(8,128)S(1)}, f32[2,3,64,128]{3,2,1,0:T(8,128)S(1)}, u32[]{:S(2)}, u32[]{:S(2)}) collective-permute-start(f32[2,3,64,128]{3,2,1,0:T(8,128)S(1)} %get-tuple-element.17), channel_id=1, source_target_pairs={{0,16},{1,17},{2,18},{3,19},{4,20},{5,21},{6,22},{7,23},{8,24},{9,... | collective-permute-start | bytes 589832 | tf_op jit(solution)/shard_map/ppermute | solution.py:387
  6.8 28.6 %collective-permute-start.1 = (f32[2,3,64,128]{3,2,1,0:T(8,128)S(1)}, f32[2,3,64,128]{3,2,1,0:T(8,128)S(1)}, u32[]{:S(2)}, u32[]{:S(2)}) collective-permute-start(f32[2,3,64,128]{3,2,1,0:T(8,128)S(1)} %get-tuple-element.18), channel_id=1, source_target_pairs={{0,18},{1,19},{2,16},{3,17},{4,22},{5,23},{6,20},{7,21},{8,26},{9,... | collective-permute-start | bytes 589832 | tf_op jit(solution)/shard_map/ppermute | solution.py:387
  8.4 40.1 %collective-permute-start.4 = (f32[3,64,128]{2,1,0:T(8,128)S(1)}, f32[3,64,128]{2,1,0:T(8,128)S(1)}, u32[]{:S(2)}, u32[]{:S(2)}) collective-permute-start(f32[3,64,128]{2,1,0:T(8,128)S(1)} %get-tuple-element.21), channel_id=1, source_target_pairs={{0,24},{1,25},{2,26},{3,27},{4,28},{5,29},{6,30},{7,31},{8,16},{9,... | collective-permute-start | bytes 294920 | tf_op jit(solution)/shard_map/ppermute | solution.py:387
  11.6 31.7 %collective-permute-start.2 = (f32[2,3,64,128]{3,2,1,0:T(8,128)S(1)}, f32[2,3,64,128]{3,2,1,0:T(8,128)S(1)}, u32[]{:S(2)}, u32[]{:S(2)}) collective-permute-start(f32[2,3,64,128]{3,2,1,0:T(8,128)S(1)} %get-tuple-element.19), channel_id=1, source_target_pairs={{0,20},{1,21},{2,22},{3,23},{4,16},{5,17},{6,18},{7,19},{8,28},{9,... | collective-permute-start | bytes 589832 | tf_op jit(solution)/shard_map/ppermute | solution.py:387
  12.5 34.0 %collective-permute-start.3 = (f32[2,3,64,128]{3,2,1,0:T(8,128)S(1)}, f32[2,3,64,128]{3,2,1,0:T(8,128)S(1)}, u32[]{:S(2)}, u32[]{:S(2)}) collective-permute-start(f32[2,3,64,128]{3,2,1,0:T(8,128)S(1)} %get-tuple-element.20), channel_id=1, source_target_pairs={{0,22},{1,23},{2,20},{3,21},{4,18},{5,19},{6,16},{7,17},{8,30},{9,... | collective-permute-start | bytes 589832 | tf_op jit(solution)/shard_map/ppermute | solution.py:387
  18.6 4.7 %copy-start.5 = (s32[2,16,64]{2,1,0:T(8,128)S(1)}, s32[2,16,64]{2,1,0:T(8,128)}, u32[]{:S(2)}) copy-start(s32[2,16,64]{2,1,0:T(8,128)} %param.7) | copy-start | bytes 24580
  18.6 4.7 %copy-start.7 = (s32[128]{0:T(128)S(1)}, s32[128]{0:T(128)}, u32[]{:S(2)}) copy-start(s32[128]{0:T(128)} %param.8) | copy-start | bytes 1540
  18.6 5.6 %copy-start.6 = (s32[2,128]{1,0:T(2,128)S(1)}, s32[2,128]{1,0:T(2,128)}, u32[]{:S(2)}) copy-start(s32[2,128]{1,0:T(2,128)} %param.9) | copy-start | bytes 3076
  18.6 6.0 %copy-start.8 = (s32[16]{0:T(128)S(1)}, s32[16]{0:T(128)}, u32[]{:S(2)}) copy-start(s32[16]{0:T(128)} %constant.62.clone) | copy-start | bytes 196
  18.6 6.0 %copy-start.9 = (s32[16]{0:T(128)S(1)}, s32[16]{0:T(128)}, u32[]{:S(2)}) copy-start(s32[16]{0:T(128)} %constant.61.clone) | copy-start | bytes 196
  18.6 56.8 %all-to-all-start = ((f32[16,3,64,128]{3,2,1,0:T(8,128)}), f32[16,3,64,128]{3,2,1,0:T(8,128)}, u32[]{:S(2)}, u32[]{:S(2)}) async-start(f32[16,3,64,128]{3,2,1,0:T(8,128)} %shard_map.67), calls=%async_computation | async-start | bytes 3145728 | tf_op jit(solution)/shard_map/all_to_all | solution.py:428
  31.6 38.8 %copy-start.1 = (f32[2,3,64,128]{3,2,1,0:T(8,128)}, f32[2,3,64,128]{3,2,1,0:T(8,128)S(1)}, u32[]{:S(2)}) copy-start(f32[2,3,64,128]{3,2,1,0:T(8,128)S(1)} %collective-permute-done.refs_0_.refs_1_) | copy-start | bytes 589828
  31.6 27.1 %collective-permute-start.5 = (f32[3,64,128]{2,1,0:T(8,128)S(1)}, f32[3,64,128]{2,1,0:T(8,128)S(1)}, u32[]{:S(2)}, u32[]{:S(2)}) collective-permute-start(f32[3,64,128]{2,1,0:T(8,128)S(1)} %get-tuple-element.22), channel_id=1, source_target_pairs={{0,25},{1,24},{2,27},{3,26},{4,29},{5,28},{6,31},{7,30},{8,17},{9,... | collective-permute-start | bytes 294920 | tf_op jit(solution)/shard_map/ppermute | solution.py:387
  35.4 35.0 %copy-start.2 = (f32[2,3,64,128]{3,2,1,0:T(8,128)}, f32[2,3,64,128]{3,2,1,0:T(8,128)S(1)}, u32[]{:S(2)}) copy-start(f32[2,3,64,128]{3,2,1,0:T(8,128)S(1)} %collective-permute-done.1.refs_1_.refs_2_) | copy-start | bytes 589828
  35.4 23.4 %collective-permute-start.6 = (f32[3,64,128]{2,1,0:T(8,128)S(1)}, f32[3,64,128]{2,1,0:T(8,128)S(1)}, u32[]{:S(2)}, u32[]{:S(2)}) collective-permute-start(f32[3,64,128]{2,1,0:T(8,128)S(1)} %get-tuple-element.23), channel_id=1, source_target_pairs={{0,26},{1,27},{2,24},{3,25},{4,30},{5,31},{6,28},{7,29},{8,18},{9,... | collective-permute-start | bytes 294920 | tf_op jit(solution)/shard_map/ppermute | solution.py:387
  43.4 27.0 %copy-start.3 = (f32[2,3,64,128]{3,2,1,0:T(8,128)}, f32[2,3,64,128]{3,2,1,0:T(8,128)S(1)}, u32[]{:S(2)}) copy-start(f32[2,3,64,128]{3,2,1,0:T(8,128)S(1)} %collective-permute-done.2.refs_2_.refs_3_) | copy-start | bytes 589828
  43.4 18.9 %collective-permute-start.7 = (f32[3,64,128]{2,1,0:T(8,128)S(1)}, f32[3,64,128]{2,1,0:T(8,128)S(1)}, u32[]{:S(2)}, u32[]{:S(2)}) collective-permute-start(f32[3,64,128]{2,1,0:T(8,128)S(1)} %get-tuple-element.24), channel_id=1, source_target_pairs={{0,27},{1,26},{2,25},{3,24},{4,31},{5,30},{6,29},{7,28},{8,19},{9,... | collective-permute-start | bytes 294920 | tf_op jit(solution)/shard_map/ppermute | solution.py:387
  46.5 23.9 %copy-start.4 = (f32[2,3,64,128]{3,2,1,0:T(8,128)}, f32[2,3,64,128]{3,2,1,0:T(8,128)S(1)}, u32[]{:S(2)}) copy-start(f32[2,3,64,128]{3,2,1,0:T(8,128)S(1)} %collective-permute-done.3.refs_3_.refs_4_) | copy-start | bytes 589828
  46.5 23.8 %collective-permute-start.12 = (f32[4,3,64,128]{3,2,1,0:T(8,128)S(1)}, f32[4,3,64,128]{3,2,1,0:T(8,128)S(1)}, u32[]{:S(2)}, u32[]{:S(2)}) collective-permute-start(f32[4,3,64,128]{3,2,1,0:T(8,128)S(1)} %pad_maximum_fusion), channel_id=1, source_target_pairs={{0,1},{1,0},{2,3},{3,2},{4,5},{5,4},{6,7},{7,6},{8,9},{9,8},{10,11... | collective-permute-start | bytes 1179656 | tf_op jit(solution)/shard_map/ppermute | solution.py:387
  48.6 15.8 %collective-permute-start.8 = (f32[3,64,128]{2,1,0:T(8,128)S(1)}, f32[3,64,128]{2,1,0:T(8,128)S(1)}, u32[]{:S(2)}, u32[]{:S(2)}) collective-permute-start(f32[3,64,128]{2,1,0:T(8,128)S(1)} %get-tuple-element.25), channel_id=1, source_target_pairs={{0,28},{1,29},{2,30},{3,31},{4,24},{5,25},{6,26},{7,27},{8,20},{9,... | collective-permute-start | bytes 294920 | tf_op jit(solution)/shard_map/ppermute | solution.py:387
  58.7 9.5 %collective-permute-start.9 = (f32[3,64,128]{2,1,0:T(8,128)S(1)}, f32[3,64,128]{2,1,0:T(8,128)S(1)}, u32[]{:S(2)}, u32[]{:S(2)}) collective-permute-start(f32[3,64,128]{2,1,0:T(8,128)S(1)} %get-tuple-element.26), channel_id=1, source_target_pairs={{0,29},{1,28},{2,31},{3,30},{4,25},{5,24},{6,27},{7,26},{8,21},{9,... | collective-permute-start | bytes 294920 | tf_op jit(solution)/shard_map/ppermute | solution.py:387
  58.7 9.4 %collective-permute-start.10 = (f32[3,64,128]{2,1,0:T(8,128)S(1)}, f32[3,64,128]{2,1,0:T(8,128)S(1)}, u32[]{:S(2)}, u32[]{:S(2)}) collective-permute-start(f32[3,64,128]{2,1,0:T(8,128)S(1)} %get-tuple-element.27), channel_id=1, source_target_pairs={{0,30},{1,31},{2,28},{3,29},{4,26},{5,27},{6,24},{7,25},{8,22},{9,... | collective-permute-start | bytes 294920 | tf_op jit(solution)/shard_map/ppermute | solution.py:387
  62.2 8.1 %collective-permute-start.11 = (f32[3,64,128]{2,1,0:T(8,128)S(1)}, f32[3,64,128]{2,1,0:T(8,128)S(1)}, u32[]{:S(2)}, u32[]{:S(2)}) collective-permute-start(f32[3,64,128]{2,1,0:T(8,128)S(1)} %get-tuple-element.28), channel_id=1, source_target_pairs={{0,31},{1,30},{2,29},{3,28},{4,27},{5,26},{6,25},{7,24},{8,23},{9,... | collective-permute-start | bytes 294920 | tf_op jit(solution)/shard_map/ppermute | solution.py:387

commit v6 on v5

--- a/solution.py
+++ b/solution.py
@@ -155,7 +155,7 @@
 
 
 LANES = 128
-VMEM_BYTES = 20 * 1024 * 1024
+VMEM_BYTES = 16 * 1024 * 1024
 
 
 def level_order(fragments, depth_count):
@@ -230,7 +230,7 @@
         in_specs=[pl.BlockSpec(memory_space=pltpu.SMEM)] + [vmem] * len(arrays),
         out_specs=[vmem] * len(out_shapes),
         out_shape=[jax.ShapeDtypeStruct(shape, jnp.float32) for shape in out_shapes],
-        compiler_params=pltpu.CompilerParams(vmem_limit_bytes=VMEM_BYTES),
+        compiler_params=pltpu.CompilerParams(vmem_limit_bytes=VMEM_BYTES // 2),
     )(numbers, *arrays)
 
 
@@ -360,7 +360,7 @@
         in_specs=[vmem] + [pl.BlockSpec(memory_space=pl.ANY)] * len(after),
         out_specs=vmem,
         out_shape=jax.ShapeDtypeStruct(slots.shape, jnp.float32),
-        compiler_params=pltpu.CompilerParams(vmem_limit_bytes=VMEM_BYTES),
+        compiler_params=pltpu.CompilerParams(vmem_limit_bytes=VMEM_BYTES // 4),
         cost_estimate=pl.CostEstimate(flops=30000000000, bytes_accessed=0, transcendentals=0),
     )(slots, *after)
 
@@ -415,7 +415,7 @@
     singles = [(offset, flip) for offset in direct for flip in range(2)]
     for partner, array in zip(singles, leaving[len(relayed) :]):
         keep(send(array, *partner), [(None, partner)])
-    late = set(range(len(relayed) + 1, len(arrays) + 1))
+    late = set(range(1, len(arrays) + 1))
     for first, last in ((0, 4),):
         group = jnp.stack([got[1] for got in passing[first:last]])
         keep(

time: 95.5 us -> 95.4 us (level)
  no operation moved by 1% of the time
where the time goes in v6:
time: 95.4 us; the launch traced here: 95 us
  starting transfers between devices  42 us (44%)
  waiting for transfers between devices  23.1 us (24%)
  blocking collectives  14.9 us (16%)
  Pallas kernels  9.68 us (10%)
  local copies, waits for them, and re-layouts  3.06 us (3%)
  other arithmetic  1.9 us (2%)
    ppermute x13, starting transfers between devices, send(): return lax.ppermute(array, ('grp', 'swap'), pairs)  37.5 us
    ppermute x13, waiting for transfers between devices, send(): return lax.ppermute(array, ('grp', 'swap'), pairs)  18 us
    all_to_all x1, blocking collectives, chunk_shards(): lax.all_to_all(tiles, 'grp', split_axis=0, concat_axis=0, tiled=True)  14.9 us
    pallas_call x3, Pallas kernels, on_device(): pl.pallas_call(kernel, in_specs=[pl.BlockSpec(memory_space=pltpu.SMEM)] +...  5.81 us
    all_to_all x1, waiting for transfers between devices, chunk_shards(): lax.all_to_all(near_chunks, ('grp', 'swap'), split_axis=0, concat_axis=0,...  5.04 us
    all_to_all x1, starting transfers between devices, chunk_shards(): lax.all_to_all(near_chunks, ('grp', 'swap'), split_axis=0, concat_axis=0,...  4.55 us
    pallas_call x1, Pallas kernels, composite(): pl.pallas_call(functools.partial(composite_kernel, picks, late), in_specs...  3.86 us
  transfers between devices with their start and end apart: 14, of which 5 were waited for; matrix products, arithmetic and copies ran while one was open for 3% of the time, Pallas kernels for 5%

profile of v6, /device:TPU:0, one launch (start us, length us, event | category | flops | bytes accessed | tf_op | source)
XLA Modules:
  0.0 95.0 jit_solution(13255970340292692302)
XLA Ops:
  0.0 0.1 pad_add_fusion.1.numbers_ref
  0.1 1.6 %copy-done = bf16[1,1,64,4,4096]{4,3,2,1,0:T(4,128)(2,1)S(1)} copy-done((bf16[1,1,64,4,4096]{4,3,2,1,0:T(4,128)(2,1)S(1)}, bf16[1,1,64,4,4096]{4,3,2,1,0:T(4,128)(2,1)}, u32[]{:S(2)}) %copy-start) | copy-done | bytes 2097176
  1.7 1.0 %shard_map.64 = (f32[2,3,64,128]{3,2,1,0:T(8,128)S(1)}, f32[2,3,64,128]{3,2,1,0:T(8,128)S(1)}) custom-call(s32[2]{0:T(128)S(1)} %pad_add_fusion.1.numbers_ref, bf16[64,4,4096]{2,1,0:T(4,128)(2,1)S(1)} %bitcast.28), custom_call_target="tpu_custom_call" | custom-call | tf_op jit(solution)/shard_map/pallas_call | solution.py:228
  2.7 4.1 %collective-permute-start = (f32[2,3,64,128]{3,2,1,0:T(8,128)S(1)}, f32[2,3,64,128]{3,2,1,0:T(8,128)S(1)}, u32[]{:S(2)}, u32[]{:S(2)}) collective-permute-start(f32[2,3,64,128]{3,2,1,0:T(8,128)S(1)} %get-tuple-element.17), channel_id=1, source_target_pairs={{0,16},{1,17},{2,18},{3,19},{4,20},{5,21},{6,22},{7,23},{8,24},{9,... | collective-permute-start | bytes 589832 | tf_op jit(solution)/shard_map/ppermute | solution.py:387
  6.8 0.0 collective-permute-start.1
  6.8 1.6 %shard_map.65 = (f32[2,3,64,128]{3,2,1,0:T(8,128)S(1)}, f32[2,3,64,128]{3,2,1,0:T(8,128)S(1)}, f32[3,64,128]{2,1,0:T(8,128)S(1)}, f32[3,64,128]{2,1,0:T(8,128)S(...) custom-call(s32[2]{0:T(128)S(1)} %pad_add_fusion.1.numbers_ref, ...), custom_call_target="tpu_custom_call" | custom-call | tf_op jit(solution)/shard_map/pallas_call | solution.py:228
  8.4 3.2 %collective-permute-start.4 = (f32[3,64,128]{2,1,0:T(8,128)S(1)}, f32[3,64,128]{2,1,0:T(8,128)S(1)}, u32[]{:S(2)}, u32[]{:S(2)}) collective-permute-start(f32[3,64,128]{2,1,0:T(8,128)S(1)} %get-tuple-element.21), channel_id=1, source_target_pairs={{0,24},{1,25},{2,26},{3,27},{4,28},{5,29},{6,30},{7,31},{8,16},{9,... | collective-permute-start | bytes 294920 | tf_op jit(solution)/shard_map/ppermute | solution.py:387
  11.6 0.9 collective-permute-start.2
  12.5 3.0 %collective-permute-start.3 = (f32[2,3,64,128]{3,2,1,0:T(8,128)S(1)}, f32[2,3,64,128]{3,2,1,0:T(8,128)S(1)}, u32[]{:S(2)}, u32[]{:S(2)}) collective-permute-start(f32[2,3,64,128]{3,2,1,0:T(8,128)S(1)} %get-tuple-element.20), channel_id=1, source_target_pairs={{0,22},{1,23},{2,20},{3,21},{4,18},{5,19},{6,16},{7,17},{8,30},{9,... | collective-permute-start | bytes 589832 | tf_op jit(solution)/shard_map/ppermute | solution.py:387
  15.4 3.2 %shard_map.67 = f32[16,3,64,128]{3,2,1,0:T(8,128)} custom-call(s32[2]{0:T(128)S(1)} %pad_add_fusion.1.numbers_ref, bf16[64,4,4096]{2,1,0:T(4,128)(2,1)S(1)} %bitcast.30), custom_call_target="tpu_custom_call" | custom-call | tf_op jit(solution)/shard_map/pallas_call | solution.py:228
  18.6 0.0 copy-start.5
  18.6 4.5 %all-to-all-start = ((f32[16,3,64,128]{3,2,1,0:T(8,128)}), f32[16,3,64,128]{3,2,1,0:T(8,128)}, u32[]{:S(2)}, u32[]{:S(2)}) async-start(f32[16,3,64,128]{3,2,1,0:T(8,128)} %shard_map.67), calls=%async_computation | async-start | bytes 3145728 | tf_op jit(solution)/shard_map/all_to_all | solution.py:428
  23.2 0.1 mul.36
  23.3 0.9 select_reduce_fusion
  24.2 0.1 reshape.81
  24.3 0.1 convert_element_type.8
  24.4 0.2 fusion
  24.7 0.1 pad_add_fusion
  24.7 0.1 broadcast_add_fusion
  24.8 6.8 %collective-permute-done.refs_0_.refs_1_ = f32[2,3,64,128]{3,2,1,0:T(8,128)S(1)} collective-permute-done((f32[2,3,64,128]{3,2,1,0:T(8,128)S(1)}, f32[2,3,64,128]{3,2,1,0:T(8,128)S(1)}, u32[]{:S(2)}, u32[]{:S(2)}) %collective-permute-start) | collective-permute-done | bytes 196640 | tf_op jit(solution)/shard_map/ppermute | solution.py:387
  31.6 3.8 %collective-permute-start.5 = (f32[3,64,128]{2,1,0:T(8,128)S(1)}, f32[3,64,128]{2,1,0:T(8,128)S(1)}, u32[]{:S(2)}, u32[]{:S(2)}) collective-permute-start(f32[3,64,128]{2,1,0:T(8,128)S(1)} %get-tuple-element.22), channel_id=1, source_target_pairs={{0,25},{1,24},{2,27},{3,26},{4,29},{5,28},{6,31},{7,30},{8,17},{9,... | collective-permute-start | bytes 294920 | tf_op jit(solution)/shard_map/ppermute | solution.py:387
  35.4 0.0 collective-permute-done.1.refs_1_.refs_2_
  35.4 2.7 %collective-permute-start.6 = (f32[3,64,128]{2,1,0:T(8,128)S(1)}, f32[3,64,128]{2,1,0:T(8,128)S(1)}, u32[]{:S(2)}, u32[]{:S(2)}) collective-permute-start(f32[3,64,128]{2,1,0:T(8,128)S(1)} %get-tuple-element.23), channel_id=1, source_target_pairs={{0,26},{1,27},{2,24},{3,25},{4,30},{5,31},{6,28},{7,29},{8,18},{9,... | collective-permute-start | bytes 294920 | tf_op jit(solution)/shard_map/ppermute | solution.py:387
  38.1 5.2 %collective-permute-done.2.refs_2_.refs_3_ = f32[2,3,64,128]{3,2,1,0:T(8,128)S(1)} collective-permute-done((f32[2,3,64,128]{3,2,1,0:T(8,128)S(1)}, f32[2,3,64,128]{3,2,1,0:T(8,128)S(1)}, u32[]{:S(2)}, u32[]{:S(2)}) %collective-permute-start.2) | collective-permute-done | bytes 196640 | tf_op jit(solution)/shard_map/ppermute | solution.py:387
  43.3 3.1 %collective-permute-start.7 = (f32[3,64,128]{2,1,0:T(8,128)S(1)}, f32[3,64,128]{2,1,0:T(8,128)S(1)}, u32[]{:S(2)}, u32[]{:S(2)}) collective-permute-start(f32[3,64,128]{2,1,0:T(8,128)S(1)} %get-tuple-element.24), channel_id=1, source_target_pairs={{0,27},{1,26},{2,25},{3,24},{4,31},{5,30},{6,29},{7,28},{8,19},{9,... | collective-permute-start | bytes 294920 | tf_op jit(solution)/shard_map/ppermute | solution.py:387
  46.4 0.0 collective-permute-done.3.refs_3_.refs_4_
  46.5 1.3 %collective-permute-start.12 = (f32[4,3,64,128]{3,2,1,0:T(8,128)S(1)}, f32[4,3,64,128]{3,2,1,0:T(8,128)S(1)}, u32[]{:S(2)}, u32[]{:S(2)}) collective-permute-start(f32[4,3,64,128]{3,2,1,0:T(8,128)S(1)} %pad_maximum_fusion), channel_id=1, source_target_pairs={{0,1},{1,0},{2,3},{3,2},{4,5},{5,4},{6,7},{7,6},{8,9},{9,8},{10,11... | collective-permute-start | bytes 1179656 | tf_op jit(solution)/shard_map/ppermute | solution.py:387
  47.8 0.1 iota_compare_fusion.3
  47.8 0.1 copy.11
  47.9 0.6 select_reduce_fusion.1
  48.5 0.0 collective-permute-done.4.refs_4_.refs_5_
  48.6 10.1 %collective-permute-start.8 = (f32[3,64,128]{2,1,0:T(8,128)S(1)}, f32[3,64,128]{2,1,0:T(8,128)S(1)}, u32[]{:S(2)}, u32[]{:S(2)}) collective-permute-start(f32[3,64,128]{2,1,0:T(8,128)S(1)} %get-tuple-element.25), channel_id=1, source_target_pairs={{0,28},{1,29},{2,30},{3,31},{4,24},{5,25},{6,26},{7,27},{8,20},{9,... | collective-permute-start | bytes 294920 | tf_op jit(solution)/shard_map/ppermute | solution.py:387
  58.7 0.0 collective-permute-done.5.refs_5_.refs_6_
  58.7 0.0 collective-permute-start.9
  58.7 0.0 collective-permute-done.6.refs_6_.refs_7_
  58.7 3.5 %collective-permute-start.10 = (f32[3,64,128]{2,1,0:T(8,128)S(1)}, f32[3,64,128]{2,1,0:T(8,128)S(1)}, u32[]{:S(2)}, u32[]{:S(2)}) collective-permute-start(f32[3,64,128]{2,1,0:T(8,128)S(1)} %get-tuple-element.27), channel_id=1, source_target_pairs={{0,30},{1,31},{2,28},{3,29},{4,26},{5,27},{6,24},{7,25},{8,22},{9,... | collective-permute-start | bytes 294920 | tf_op jit(solution)/shard_map/ppermute | solution.py:387
  62.2 0.0 collective-permute-done.7.refs_7_.refs_8_
  62.2 1.9 %collective-permute-start.11 = (f32[3,64,128]{2,1,0:T(8,128)S(1)}, f32[3,64,128]{2,1,0:T(8,128)S(1)}, u32[]{:S(2)}, u32[]{:S(2)}) collective-permute-start(f32[3,64,128]{2,1,0:T(8,128)S(1)} %get-tuple-element.28), channel_id=1, source_target_pairs={{0,31},{1,30},{2,29},{3,28},{4,27},{5,26},{6,25},{7,24},{8,23},{9,... | collective-permute-start | bytes 294920 | tf_op jit(solution)/shard_map/ppermute | solution.py:387
  64.1 0.1 mul.39.places_ref
  64.2 0.1 reshape.82.slots_ref
  64.4 0.0 collective-permute-done.8.refs_8_.refs_9_
  64.4 3.8 %collective-permute-done.9.refs_9_.refs_10_ = f32[3,64,128]{2,1,0:T(8,128)S(1)} collective-permute-done((f32[3,64,128]{2,1,0:T(8,128)S(1)}, f32[3,64,128]{2,1,0:T(8,128)S(1)}, u32[]{:S(2)}, u32[]{:S(2)}) %collective-permute-start.9) | collective-permute-done | bytes 98336 | tf_op jit(solution)/shard_map/ppermute | solution.py:387
  68.2 0.0 collective-permute-done.10.refs_10_.refs_11_
  68.2 2.2 %collective-permute-done.11.refs_11_.refs_12_ = f32[3,64,128]{2,1,0:T(8,128)S(1)} collective-permute-done((f32[3,64,128]{2,1,0:T(8,128)S(1)}, f32[3,64,128]{2,1,0:T(8,128)S(1)}, u32[]{:S(2)}, u32[]{:S(2)}) %collective-permute-start.11) | collective-permute-done | bytes 98336 | tf_op jit(solution)/shard_map/ppermute | solution.py:387
  70.3 5.0 %all-to-all-done.refs_0_ = f32[16,3,64,128]{3,2,1,0:T(8,128)} async-done(((f32[16,3,64,128]{3,2,1,0:T(8,128)}), f32[16,3,64,128]{3,2,1,0:T(8,128)}, u32[]{:S(2)}, u32[]{:S(2)}) %all-to-all-start) | async-done | bytes 1572896 | tf_op jit(solution)/shard_map/all_to_all | solution.py:428
  75.4 3.9 %shard_map.68 = f32[16,3,8,128]{3,2,1,0:T(8,128)S(1)} custom-call(s32[256]{0:T(256)S(1)} %mul.39.places_ref, f32[1,2048]{1,0:T(1,128)S(1)} %shard_map.66.slots_ref, f32[16,3,64,128]{3,2,1,0:T(8,128)} %all-to-all-done.refs_0_, f32[2,3,64,128]{3,2,1,0:T(8,128)S(1)} %collective-permute-done.refs_0_.refs_1_, ...), custom_call_target="tpu_custom_call" | custom-call | tf_op jit(solution)/shard_map/pallas_call | solution.py:329
  79.2 14.9 %all_to_all.10 = f32[16,3,8,128]{3,2,1,0:T(8,128)S(1)} all-to-all(f32[16,3,8,128]{3,2,1,0:T(8,128)S(1)} %shard_map.68), channel_id=1, replica_groups=mesh['grp'=16,'swap'=2] {'grp'}, dimensions={0} | all-to-all | bytes 393216 | tf_op jit(solution)/shard_map/all_to_all | solution.py:450
  94.2 0.9 copy.14
  (24 shorter events, 0.1 us)
Async XLA Ops:
  0.1 1.6 %copy-start = (bf16[1,1,64,4,4096]{4,3,2,1,0:T(4,128)(2,1)S(1)}, bf16[1,1,64,4,4096]{4,3,2,1,0:T(4,128)(2,1)}, u32[]{:S(2)}) copy-start(bf16[1,1,64,4,4096]{4,3,2,1,0:T(4,128)(2,1)} %param.6) | copy-start | bytes 6291460
  2.7 28.9 %collective-permute-start = (f32[2,3,64,128]{3,2,1,0:T(8,128)S(1)}, f32[2,3,64,128]{3,2,1,0:T(8,128)S(1)}, u32[]{:S(2)}, u32[]{:S(2)}) collective-permute-start(f32[2,3,64,128]{3,2,1,0:T(8,128)S(1)} %get-tuple-element.17), channel_id=1, source_target_pairs={{0,16},{1,17},{2,18},{3,19},{4,20},{5,21},{6,22},{7,23},{8,24},{9,... | collective-permute-start | bytes 589832 | tf_op jit(solution)/shard_map/ppermute | solution.py:387
  6.8 28.6 %collective-permute-start.1 = (f32[2,3,64,128]{3,2,1,0:T(8,128)S(1)}, f32[2,3,64,128]{3,2,1,0:T(8,128)S(1)}, u32[]{:S(2)}, u32[]{:S(2)}) collective-permute-start(f32[2,3,64,128]{3,2,1,0:T(8,128)S(1)} %get-tuple-element.18), channel_id=1, source_target_pairs={{0,18},{1,19},{2,16},{3,17},{4,22},{5,23},{6,20},{7,21},{8,26},{9,... | collective-permute-start | bytes 589832 | tf_op jit(solution)/shard_map/ppermute | solution.py:387
  8.4 40.1 %collective-permute-start.4 = (f32[3,64,128]{2,1,0:T(8,128)S(1)}, f32[3,64,128]{2,1,0:T(8,128)S(1)}, u32[]{:S(2)}, u32[]{:S(2)}) collective-permute-start(f32[3,64,128]{2,1,0:T(8,128)S(1)} %get-tuple-element.21), channel_id=1, source_target_pairs={{0,24},{1,25},{2,26},{3,27},{4,28},{5,29},{6,30},{7,31},{8,16},{9,... | collective-permute-start | bytes 294920 | tf_op jit(solution)/shard_map/ppermute | solution.py:387
  11.6 31.7 %collective-permute-start.2 = (f32[2,3,64,128]{3,2,1,0:T(8,128)S(1)}, f32[2,3,64,128]{3,2,1,0:T(8,128)S(1)}, u32[]{:S(2)}, u32[]{:S(2)}) collective-permute-start(f32[2,3,64,128]{3,2,1,0:T(8,128)S(1)} %get-tuple-element.19), channel_id=1, source_target_pairs={{0,20},{1,21},{2,22},{3,23},{4,16},{5,17},{6,18},{7,19},{8,28},{9,... | collective-permute-start | bytes 589832 | tf_op jit(solution)/shard_map/ppermute | solution.py:387
  12.5 34.0 %collective-permute-start.3 = (f32[2,3,64,128]{3,2,1,0:T(8,128)S(1)}, f32[2,3,64,128]{3,2,1,0:T(8,128)S(1)}, u32[]{:S(2)}, u32[]{:S(2)}) collective-permute-start(f32[2,3,64,128]{3,2,1,0:T(8,128)S(1)} %get-tuple-element.20), channel_id=1, source_target_pairs={{0,22},{1,23},{2,20},{3,21},{4,18},{5,19},{6,16},{7,17},{8,30},{9,... | collective-permute-start | bytes 589832 | tf_op jit(solution)/shard_map/ppermute | solution.py:387
  18.6 4.7 %copy-start.1 = (s32[2,16,64]{2,1,0:T(8,128)S(1)}, s32[2,16,64]{2,1,0:T(8,128)}, u32[]{:S(2)}) copy-start(s32[2,16,64]{2,1,0:T(8,128)} %param.7) | copy-start | bytes 24580
  18.6 4.7 %copy-start.3 = (s32[128]{0:T(128)S(1)}, s32[128]{0:T(128)}, u32[]{:S(2)}) copy-start(s32[128]{0:T(128)} %param.8) | copy-start | bytes 1540
  18.6 5.6 %copy-start.2 = (s32[2,128]{1,0:T(2,128)S(1)}, s32[2,128]{1,0:T(2,128)}, u32[]{:S(2)}) copy-start(s32[2,128]{1,0:T(2,128)} %param.9) | copy-start | bytes 3076
  18.6 6.0 %copy-start.4 = (s32[16]{0:T(128)S(1)}, s32[16]{0:T(128)}, u32[]{:S(2)}) copy-start(s32[16]{0:T(128)} %constant.62.clone) | copy-start | bytes 196
  18.6 6.0 %copy-start.5 = (s32[16]{0:T(128)S(1)}, s32[16]{0:T(128)}, u32[]{:S(2)}) copy-start(s32[16]{0:T(128)} %constant.61.clone) | copy-start | bytes 196
  18.6 56.8 %all-to-all-start = ((f32[16,3,64,128]{3,2,1,0:T(8,128)}), f32[16,3,64,128]{3,2,1,0:T(8,128)}, u32[]{:S(2)}, u32[]{:S(2)}) async-start(f32[16,3,64,128]{3,2,1,0:T(8,128)} %shard_map.67), calls=%async_computation | async-start | bytes 3145728 | tf_op jit(solution)/shard_map/all_to_all | solution.py:428
  31.6 27.1 %collective-permute-start.5 = (f32[3,64,128]{2,1,0:T(8,128)S(1)}, f32[3,64,128]{2,1,0:T(8,128)S(1)}, u32[]{:S(2)}, u32[]{:S(2)}) collective-permute-start(f32[3,64,128]{2,1,0:T(8,128)S(1)} %get-tuple-element.22), channel_id=1, source_target_pairs={{0,25},{1,24},{2,27},{3,26},{4,29},{5,28},{6,31},{7,30},{8,17},{9,... | collective-permute-start | bytes 294920 | tf_op jit(solution)/shard_map/ppermute | solution.py:387
  35.4 23.4 %collective-permute-start.6 = (f32[3,64,128]{2,1,0:T(8,128)S(1)}, f32[3,64,128]{2,1,0:T(8,128)S(1)}, u32[]{:S(2)}, u32[]{:S(2)}) collective-permute-start(f32[3,64,128]{2,1,0:T(8,128)S(1)} %get-tuple-element.23), channel_id=1, source_target_pairs={{0,26},{1,27},{2,24},{3,25},{4,30},{5,31},{6,28},{7,29},{8,18},{9,... | collective-permute-start | bytes 294920 | tf_op jit(solution)/shard_map/ppermute | solution.py:387
  43.3 18.9 %collective-permute-start.7 = (f32[3,64,128]{2,1,0:T(8,128)S(1)}, f32[3,64,128]{2,1,0:T(8,128)S(1)}, u32[]{:S(2)}, u32[]{:S(2)}) collective-permute-start(f32[3,64,128]{2,1,0:T(8,128)S(1)} %get-tuple-element.24), channel_id=1, source_target_pairs={{0,27},{1,26},{2,25},{3,24},{4,31},{5,30},{6,29},{7,28},{8,19},{9,... | collective-permute-start | bytes 294920 | tf_op jit(solution)/shard_map/ppermute | solution.py:387
  46.5 23.8 %collective-permute-start.12 = (f32[4,3,64,128]{3,2,1,0:T(8,128)S(1)}, f32[4,3,64,128]{3,2,1,0:T(8,128)S(1)}, u32[]{:S(2)}, u32[]{:S(2)}) collective-permute-start(f32[4,3,64,128]{3,2,1,0:T(8,128)S(1)} %pad_maximum_fusion), channel_id=1, source_target_pairs={{0,1},{1,0},{2,3},{3,2},{4,5},{5,4},{6,7},{7,6},{8,9},{9,8},{10,11... | collective-permute-start | bytes 1179656 | tf_op jit(solution)/shard_map/ppermute | solution.py:387
  48.6 15.8 %collective-permute-start.8 = (f32[3,64,128]{2,1,0:T(8,128)S(1)}, f32[3,64,128]{2,1,0:T(8,128)S(1)}, u32[]{:S(2)}, u32[]{:S(2)}) collective-permute-start(f32[3,64,128]{2,1,0:T(8,128)S(1)} %get-tuple-element.25), channel_id=1, source_target_pairs={{0,28},{1,29},{2,30},{3,31},{4,24},{5,25},{6,26},{7,27},{8,20},{9,... | collective-permute-start | bytes 294920 | tf_op jit(solution)/shard_map/ppermute | solution.py:387
  58.7 9.5 %collective-permute-start.9 = (f32[3,64,128]{2,1,0:T(8,128)S(1)}, f32[3,64,128]{2,1,0:T(8,128)S(1)}, u32[]{:S(2)}, u32[]{:S(2)}) collective-permute-start(f32[3,64,128]{2,1,0:T(8,128)S(1)} %get-tuple-element.26), channel_id=1, source_target_pairs={{0,29},{1,28},{2,31},{3,30},{4,25},{5,24},{6,27},{7,26},{8,21},{9,... | collective-permute-start | bytes 294920 | tf_op jit(solution)/shard_map/ppermute | solution.py:387
  58.7 9.4 %collective-permute-start.10 = (f32[3,64,128]{2,1,0:T(8,128)S(1)}, f32[3,64,128]{2,1,0:T(8,128)S(1)}, u32[]{:S(2)}, u32[]{:S(2)}) collective-permute-start(f32[3,64,128]{2,1,0:T(8,128)S(1)} %get-tuple-element.27), channel_id=1, source_target_pairs={{0,30},{1,31},{2,28},{3,29},{4,26},{5,27},{6,24},{7,25},{8,22},{9,... | collective-permute-start | bytes 294920 | tf_op jit(solution)/shard_map/ppermute | solution.py:387
  62.2 8.1 %collective-permute-start.11 = (f32[3,64,128]{2,1,0:T(8,128)S(1)}, f32[3,64,128]{2,1,0:T(8,128)S(1)}, u32[]{:S(2)}, u32[]{:S(2)}) collective-permute-start(f32[3,64,128]{2,1,0:T(8,128)S(1)} %get-tuple-element.28), channel_id=1, source_target_pairs={{0,31},{1,30},{2,29},{3,28},{4,27},{5,26},{6,25},{7,24},{8,23},{9,... | collective-permute-start | bytes 294920 | tf_op jit(solution)/shard_map/ppermute | solution.py:387

commit v7 on v5

--- a/solution.py
+++ b/solution.py
@@ -423,7 +423,10 @@
             [(at, (offset, 1)) for at, offset in enumerate(relayed[first:last])],
         )
     late.add(len(arrays))
-    slots = depth_slots(tile_list, tile_slot, brick_rank, arrays)
+    low = group_count // 4
+    owner, row = tile_slot // owned, tile_slot % owned
+    exchange_slot = (owner % low * 4 + owner // low) * owned + row
+    slots = depth_slots(tile_list, exchange_slot, brick_rank, arrays)
     members = near * swap_count
     near_chunks = lax.all_to_all(
         near_chunks,
@@ -447,7 +450,15 @@
     places = jnp.sum(jnp.where((source[:, None] == ids)[..., None], ranks[None], 0), axis=1)
     places = places.reshape(-1) * (per_device // BRICKS)
     tiles = composite(places, arrays, picks, late, slots, slot_count, group_count)
-    image = lax.all_to_all(tiles, "grp", split_axis=0, concat_axis=0, tiled=True)
+    image = lax.all_to_all(
+        tiles,
+        "grp",
+        split_axis=0,
+        concat_axis=0,
+        tiled=True,
+        axis_index_groups=[[z * low + rest for rest in range(low) for z in range(4)]],
+    )
+    image = jnp.swapaxes(image.reshape((low, 4) + image.shape[1:]), 0, 1).reshape(image.shape)
     red, green, opacity = (
         jnp.transpose(image[:, channel], (1, 0, 2)).reshape(owned, pixels // swap_count)
         for channel in range(3)

time: 95.5 us -> 94.7 us (level)
  no operation moved by 1% of the time
where the time goes in v7:
time: 94.7 us; the launch traced here: 94.4 us
  starting transfers between devices  42 us (44%)
  waiting for transfers between devices  23 us (24%)
  blocking collectives  14 us (15%)
  Pallas kernels  9.8 us (10%)
  local copies, waits for them, and re-layouts  3.09 us (3%)
  other arithmetic  1.93 us (2%)
    ppermute x13, starting transfers between devices, send(): return lax.ppermute(array, ('grp', 'swap'), pairs)  37.5 us
    ppermute x13, waiting for transfers between devices, send(): return lax.ppermute(array, ('grp', 'swap'), pairs)  18 us
    all_to_all x1, blocking collectives, chunk_shards(): lax.all_to_all(tiles, 'grp', split_axis=0, concat_axis=0, tiled=True, axi...  14 us
    pallas_call x3, Pallas kernels, on_device(): pl.pallas_call(kernel, in_specs=[pl.BlockSpec(memory_space=pltpu.SMEM)] +...  5.82 us
    all_to_all x1, waiting for transfers between devices, chunk_shards(): lax.all_to_all(near_chunks, ('grp', 'swap'), split_axis=0, concat_axis=0,...  5 us
    all_to_all x1, starting transfers between devices, chunk_shards(): lax.all_to_all(near_chunks, ('grp', 'swap'), split_axis=0, concat_axis=0,...  4.54 us
    pallas_call x1, Pallas kernels, composite(): pl.pallas_call(functools.partial(composite_kernel, picks, late), in_specs...  3.98 us
  transfers between devices with their start and end apart: 14, of which 5 were waited for; matrix products, arithmetic and copies ran while one was open for 3% of the time, Pallas kernels for 5%

profile of v7, /device:TPU:0, one launch (start us, length us, event | category | flops | bytes accessed | tf_op | source)
XLA Modules:
  0.0 94.4 jit_solution(13008403979700653928)
XLA Ops:
  0.0 0.1 pad_add_fusion.1.numbers_ref
  0.1 1.6 %copy-done = bf16[1,1,64,4,4096]{4,3,2,1,0:T(4,128)(2,1)S(1)} copy-done((bf16[1,1,64,4,4096]{4,3,2,1,0:T(4,128)(2,1)S(1)}, bf16[1,1,64,4,4096]{4,3,2,1,0:T(4,128)(2,1)}, u32[]{:S(2)}) %copy-start) | copy-done | bytes 2097176
  1.7 1.0 %shard_map.64 = (f32[2,3,64,128]{3,2,1,0:T(8,128)S(1)}, f32[2,3,64,128]{3,2,1,0:T(8,128)S(1)}) custom-call(s32[2]{0:T(128)S(1)} %pad_add_fusion.1.numbers_ref, bf16[64,4,4096]{2,1,0:T(4,128)(2,1)S(1)} %bitcast.32), custom_call_target="tpu_custom_call" | custom-call | tf_op jit(solution)/shard_map/pallas_call | solution.py:228
  2.7 4.1 %collective-permute-start = (f32[2,3,64,128]{3,2,1,0:T(8,128)S(1)}, f32[2,3,64,128]{3,2,1,0:T(8,128)S(1)}, u32[]{:S(2)}, u32[]{:S(2)}) collective-permute-start(f32[2,3,64,128]{3,2,1,0:T(8,128)S(1)} %get-tuple-element.17), channel_id=1, source_target_pairs={{0,16},{1,17},{2,18},{3,19},{4,20},{5,21},{6,22},{7,23},{8,24},{9,... | collective-permute-start | bytes 589832 | tf_op jit(solution)/shard_map/ppermute | solution.py:387
  6.8 0.0 collective-permute-start.1
  6.8 1.6 %shard_map.65 = (f32[2,3,64,128]{3,2,1,0:T(8,128)S(1)}, f32[2,3,64,128]{3,2,1,0:T(8,128)S(1)}, f32[3,64,128]{2,1,0:T(8,128)S(1)}, f32[3,64,128]{2,1,0:T(8,128)S(...) custom-call(s32[2]{0:T(128)S(1)} %pad_add_fusion.1.numbers_ref, ...), custom_call_target="tpu_custom_call" | custom-call | tf_op jit(solution)/shard_map/pallas_call | solution.py:228
  8.4 3.2 %collective-permute-start.4 = (f32[3,64,128]{2,1,0:T(8,128)S(1)}, f32[3,64,128]{2,1,0:T(8,128)S(1)}, u32[]{:S(2)}, u32[]{:S(2)}) collective-permute-start(f32[3,64,128]{2,1,0:T(8,128)S(1)} %get-tuple-element.21), channel_id=1, source_target_pairs={{0,24},{1,25},{2,26},{3,27},{4,28},{5,29},{6,30},{7,31},{8,16},{9,... | collective-permute-start | bytes 294920 | tf_op jit(solution)/shard_map/ppermute | solution.py:387
  11.6 0.9 collective-permute-start.2
  12.5 3.0 %collective-permute-start.3 = (f32[2,3,64,128]{3,2,1,0:T(8,128)S(1)}, f32[2,3,64,128]{3,2,1,0:T(8,128)S(1)}, u32[]{:S(2)}, u32[]{:S(2)}) collective-permute-start(f32[2,3,64,128]{3,2,1,0:T(8,128)S(1)} %get-tuple-element.20), channel_id=1, source_target_pairs={{0,22},{1,23},{2,20},{3,21},{4,18},{5,19},{6,16},{7,17},{8,30},{9,... | collective-permute-start | bytes 589832 | tf_op jit(solution)/shard_map/ppermute | solution.py:387
  15.4 3.2 %shard_map.67 = f32[16,3,64,128]{3,2,1,0:T(8,128)} custom-call(s32[2]{0:T(128)S(1)} %pad_add_fusion.1.numbers_ref, bf16[64,4,4096]{2,1,0:T(4,128)(2,1)S(1)} %bitcast.34), custom_call_target="tpu_custom_call" | custom-call | tf_op jit(solution)/shard_map/pallas_call | solution.py:228
  18.6 0.0 copy-start.8
  18.6 4.5 %all-to-all-start = ((f32[16,3,64,128]{3,2,1,0:T(8,128)}), f32[16,3,64,128]{3,2,1,0:T(8,128)}, u32[]{:S(2)}, u32[]{:S(2)}) async-start(f32[16,3,64,128]{3,2,1,0:T(8,128)} %shard_map.67), calls=%async_computation | async-start | bytes 3145728 | tf_op jit(solution)/shard_map/all_to_all | solution.py:431
  23.2 0.1 mul.44
  23.3 0.9 select_reduce_fusion
  24.2 0.1 reshape.87
  24.3 0.1 convert_element_type.8
  24.4 0.2 fusion
  24.7 0.1 pad_add_fusion
  24.8 0.1 broadcast_add_fusion
  24.8 6.8 %collective-permute-done.refs_0_.refs_1_ = f32[2,3,64,128]{3,2,1,0:T(8,128)S(1)} collective-permute-done((f32[2,3,64,128]{3,2,1,0:T(8,128)S(1)}, f32[2,3,64,128]{3,2,1,0:T(8,128)S(1)}, u32[]{:S(2)}, u32[]{:S(2)}) %collective-permute-start) | collective-permute-done | bytes 196640 | tf_op jit(solution)/shard_map/ppermute | solution.py:387
  31.6 3.8 %collective-permute-start.5 = (f32[3,64,128]{2,1,0:T(8,128)S(1)}, f32[3,64,128]{2,1,0:T(8,128)S(1)}, u32[]{:S(2)}, u32[]{:S(2)}) collective-permute-start(f32[3,64,128]{2,1,0:T(8,128)S(1)} %get-tuple-element.22), channel_id=1, source_target_pairs={{0,25},{1,24},{2,27},{3,26},{4,29},{5,28},{6,31},{7,30},{8,17},{9,... | collective-permute-start | bytes 294920 | tf_op jit(solution)/shard_map/ppermute | solution.py:387
  35.4 0.0 collective-permute-done.1.refs_1_.refs_2_
  35.4 2.7 %collective-permute-start.6 = (f32[3,64,128]{2,1,0:T(8,128)S(1)}, f32[3,64,128]{2,1,0:T(8,128)S(1)}, u32[]{:S(2)}, u32[]{:S(2)}) collective-permute-start(f32[3,64,128]{2,1,0:T(8,128)S(1)} %get-tuple-element.23), channel_id=1, source_target_pairs={{0,26},{1,27},{2,24},{3,25},{4,30},{5,31},{6,28},{7,29},{8,18},{9,... | collective-permute-start | bytes 294920 | tf_op jit(solution)/shard_map/ppermute | solution.py:387
  38.1 5.2 %collective-permute-done.2.refs_2_.refs_3_ = f32[2,3,64,128]{3,2,1,0:T(8,128)S(1)} collective-permute-done((f32[2,3,64,128]{3,2,1,0:T(8,128)S(1)}, f32[2,3,64,128]{3,2,1,0:T(8,128)S(1)}, u32[]{:S(2)}, u32[]{:S(2)}) %collective-permute-start.2) | collective-permute-done | bytes 196640 | tf_op jit(solution)/shard_map/ppermute | solution.py:387
  43.4 3.1 %collective-permute-start.7 = (f32[3,64,128]{2,1,0:T(8,128)S(1)}, f32[3,64,128]{2,1,0:T(8,128)S(1)}, u32[]{:S(2)}, u32[]{:S(2)}) collective-permute-start(f32[3,64,128]{2,1,0:T(8,128)S(1)} %get-tuple-element.24), channel_id=1, source_target_pairs={{0,27},{1,26},{2,25},{3,24},{4,31},{5,30},{6,29},{7,28},{8,19},{9,... | collective-permute-start | bytes 294920 | tf_op jit(solution)/shard_map/ppermute | solution.py:387
  46.5 0.0 collective-permute-done.3.refs_3_.refs_4_
  46.5 1.3 %collective-permute-start.12 = (f32[4,3,64,128]{3,2,1,0:T(8,128)S(1)}, f32[4,3,64,128]{3,2,1,0:T(8,128)S(1)}, u32[]{:S(2)}, u32[]{:S(2)}) collective-permute-start(f32[4,3,64,128]{3,2,1,0:T(8,128)S(1)} %pad_maximum_fusion), channel_id=1, source_target_pairs={{0,1},{1,0},{2,3},{3,2},{4,5},{5,4},{6,7},{7,6},{8,9},{9,8},{10,11... | collective-permute-start | bytes 1179656 | tf_op jit(solution)/shard_map/ppermute | solution.py:387
  47.8 0.1 iota_compare_fusion.3
  47.9 0.1 copy.15
  47.9 0.6 select_reduce_fusion.1
  48.5 0.0 collective-permute-done.4.refs_4_.refs_5_
  48.6 10.1 %collective-permute-start.8 = (f32[3,64,128]{2,1,0:T(8,128)S(1)}, f32[3,64,128]{2,1,0:T(8,128)S(1)}, u32[]{:S(2)}, u32[]{:S(2)}) collective-permute-start(f32[3,64,128]{2,1,0:T(8,128)S(1)} %get-tuple-element.25), channel_id=1, source_target_pairs={{0,28},{1,29},{2,30},{3,31},{4,24},{5,25},{6,26},{7,27},{8,20},{9,... | collective-permute-start | bytes 294920 | tf_op jit(solution)/shard_map/ppermute | solution.py:387
  58.7 0.0 collective-permute-done.5.refs_5_.refs_6_
  58.7 0.0 collective-permute-start.9
  58.7 0.0 collective-permute-done.6.refs_6_.refs_7_
  58.7 3.5 %collective-permute-start.10 = (f32[3,64,128]{2,1,0:T(8,128)S(1)}, f32[3,64,128]{2,1,0:T(8,128)S(1)}, u32[]{:S(2)}, u32[]{:S(2)}) collective-permute-start(f32[3,64,128]{2,1,0:T(8,128)S(1)} %get-tuple-element.27), channel_id=1, source_target_pairs={{0,30},{1,31},{2,28},{3,29},{4,26},{5,27},{6,24},{7,25},{8,22},{9,... | collective-permute-start | bytes 294920 | tf_op jit(solution)/shard_map/ppermute | solution.py:387
  62.2 0.0 collective-permute-done.7.refs_7_.refs_8_
  62.2 1.9 %collective-permute-start.11 = (f32[3,64,128]{2,1,0:T(8,128)S(1)}, f32[3,64,128]{2,1,0:T(8,128)S(1)}, u32[]{:S(2)}, u32[]{:S(2)}) collective-permute-start(f32[3,64,128]{2,1,0:T(8,128)S(1)} %get-tuple-element.28), channel_id=1, source_target_pairs={{0,31},{1,30},{2,29},{3,28},{4,27},{5,26},{6,25},{7,24},{8,23},{9,... | collective-permute-start | bytes 294920 | tf_op jit(solution)/shard_map/ppermute | solution.py:387
  64.1 0.1 mul.47.places_ref
  64.2 0.1 reshape.88.slots_ref
  64.4 0.0 collective-permute-done.8.refs_8_.refs_9_
  64.4 3.8 %collective-permute-done.9.refs_9_.refs_10_ = f32[3,64,128]{2,1,0:T(8,128)S(1)} collective-permute-done((f32[3,64,128]{2,1,0:T(8,128)S(1)}, f32[3,64,128]{2,1,0:T(8,128)S(1)}, u32[]{:S(2)}, u32[]{:S(2)}) %collective-permute-start.9) | collective-permute-done | bytes 98336 | tf_op jit(solution)/shard_map/ppermute | solution.py:387
  68.2 2.2 %collective-permute-done.11.refs_11_.refs_12_ = f32[3,64,128]{2,1,0:T(8,128)S(1)} collective-permute-done((f32[3,64,128]{2,1,0:T(8,128)S(1)}, f32[3,64,128]{2,1,0:T(8,128)S(1)}, u32[]{:S(2)}, u32[]{:S(2)}) %collective-permute-start.11) | collective-permute-done | bytes 98336 | tf_op jit(solution)/shard_map/ppermute | solution.py:387
  70.3 0.0 collective-permute-done.12.refs_12_.refs_13_
  70.4 5.0 %all-to-all-done.refs_0_ = f32[16,3,64,128]{3,2,1,0:T(8,128)} async-done(((f32[16,3,64,128]{3,2,1,0:T(8,128)}), f32[16,3,64,128]{3,2,1,0:T(8,128)}, u32[]{:S(2)}, u32[]{:S(2)}) %all-to-all-start) | async-done | bytes 1572896 | tf_op jit(solution)/shard_map/all_to_all | solution.py:431
  75.4 4.0 %shard_map.68 = f32[16,3,8,128]{3,2,1,0:T(8,128)S(1)} custom-call(s32[256]{0:T(256)S(1)} %mul.47.places_ref, f32[1,2048]{1,0:T(1,128)S(1)} %shard_map.66.slots_ref, f32[16,3,64,128]{3,2,1,0:T(8,128)} %all-to-all-done.refs_0_, f32[2,3,64,128]{3,2,1,0:T(8,128)} %copy-done.1, f32[2,3,64,128]{3,2,1,0:T(8,128)} %copy-done.2, f32[2,3,64,128]{3,2,1,0:T(8,128)} %copy-done.3, ...), custom_call_target="tpu_custom_call" | custom-call | tf_op jit(solution)/shard_map/pallas_call | solution.py:329
  79.4 14.0 %all_to_all.10 = f32[16,3,8,128]{3,2,1,0:T(8,128)S(1)} all-to-all(f32[16,3,8,128]{3,2,1,0:T(8,128)S(1)} %shard_map.68), channel_id=1, replica_groups={{0,8,16,24,2,10,18,26,4,12,20,28,6,14,22,30},{1,9,17,25,3,11,19,27,5,13..., dimensions={0} | all-to-all | bytes 393216 | tf_op jit(solution)/shard_map/all_to_all | solution.py:453
  93.5 0.9 copy.19
  (34 shorter events, 0.2 us)
Async XLA Ops:
  0.1 1.6 %copy-start = (bf16[1,1,64,4,4096]{4,3,2,1,0:T(4,128)(2,1)S(1)}, bf16[1,1,64,4,4096]{4,3,2,1,0:T(4,128)(2,1)}, u32[]{:S(2)}) copy-start(bf16[1,1,64,4,4096]{4,3,2,1,0:T(4,128)(2,1)} %param.6) | copy-start | bytes 6291460
  2.7 28.9 %collective-permute-start = (f32[2,3,64,128]{3,2,1,0:T(8,128)S(1)}, f32[2,3,64,128]{3,2,1,0:T(8,128)S(1)}, u32[]{:S(2)}, u32[]{:S(2)}) collective-permute-start(f32[2,3,64,128]{3,2,1,0:T(8,128)S(1)} %get-tuple-element.17), channel_id=1, source_target_pairs={{0,16},{1,17},{2,18},{3,19},{4,20},{5,21},{6,22},{7,23},{8,24},{9,... | collective-permute-start | bytes 589832 | tf_op jit(solution)/shard_map/ppermute | solution.py:387
  6.8 28.6 %collective-permute-start.1 = (f32[2,3,64,128]{3,2,1,0:T(8,128)S(1)}, f32[2,3,64,128]{3,2,1,0:T(8,128)S(1)}, u32[]{:S(2)}, u32[]{:S(2)}) collective-permute-start(f32[2,3,64,128]{3,2,1,0:T(8,128)S(1)} %get-tuple-element.18), channel_id=1, source_target_pairs={{0,18},{1,19},{2,16},{3,17},{4,22},{5,23},{6,20},{7,21},{8,26},{9,... | collective-permute-start | bytes 589832 | tf_op jit(solution)/shard_map/ppermute | solution.py:387
  8.4 40.1 %collective-permute-start.4 = (f32[3,64,128]{2,1,0:T(8,128)S(1)}, f32[3,64,128]{2,1,0:T(8,128)S(1)}, u32[]{:S(2)}, u32[]{:S(2)}) collective-permute-start(f32[3,64,128]{2,1,0:T(8,128)S(1)} %get-tuple-element.21), channel_id=1, source_target_pairs={{0,24},{1,25},{2,26},{3,27},{4,28},{5,29},{6,30},{7,31},{8,16},{9,... | collective-permute-start | bytes 294920 | tf_op jit(solution)/shard_map/ppermute | solution.py:387
  11.6 31.7 %collective-permute-start.2 = (f32[2,3,64,128]{3,2,1,0:T(8,128)S(1)}, f32[2,3,64,128]{3,2,1,0:T(8,128)S(1)}, u32[]{:S(2)}, u32[]{:S(2)}) collective-permute-start(f32[2,3,64,128]{3,2,1,0:T(8,128)S(1)} %get-tuple-element.19), channel_id=1, source_target_pairs={{0,20},{1,21},{2,22},{3,23},{4,16},{5,17},{6,18},{7,19},{8,28},{9,... | collective-permute-start | bytes 589832 | tf_op jit(solution)/shard_map/ppermute | solution.py:387
  12.5 34.0 %collective-permute-start.3 = (f32[2,3,64,128]{3,2,1,0:T(8,128)S(1)}, f32[2,3,64,128]{3,2,1,0:T(8,128)S(1)}, u32[]{:S(2)}, u32[]{:S(2)}) collective-permute-start(f32[2,3,64,128]{3,2,1,0:T(8,128)S(1)} %get-tuple-element.20), channel_id=1, source_target_pairs={{0,22},{1,23},{2,20},{3,21},{4,18},{5,19},{6,16},{7,17},{8,30},{9,... | collective-permute-start | bytes 589832 | tf_op jit(solution)/shard_map/ppermute | solution.py:387
  18.6 4.6 %copy-start.9 = (s32[128]{0:T(128)S(1)}, s32[128]{0:T(128)}, u32[]{:S(2)}) copy-start(s32[128]{0:T(128)} %param.8) | copy-start | bytes 1540
  18.6 4.7 %copy-start.5 = (s32[2,16,64]{2,1,0:T(8,128)S(1)}, s32[2,16,64]{2,1,0:T(8,128)}, u32[]{:S(2)}) copy-start(s32[2,16,64]{2,1,0:T(8,128)} %param.7) | copy-start | bytes 24580
  18.6 5.6 %copy-start.6 = (s32[2,128]{1,0:T(2,128)S(1)}, s32[2,128]{1,0:T(2,128)}, u32[]{:S(2)}) copy-start(s32[2,128]{1,0:T(2,128)} %param.9) | copy-start | bytes 3076
  18.6 6.1 %copy-start.7 = (s32[16]{0:T(128)S(1)}, s32[16]{0:T(128)}, u32[]{:S(2)}) copy-start(s32[16]{0:T(128)} %constant.102.clone) | copy-start | bytes 196
  18.6 6.1 %copy-start.8 = (s32[16]{0:T(128)S(1)}, s32[16]{0:T(128)}, u32[]{:S(2)}) copy-start(s32[16]{0:T(128)} %constant.101.clone) | copy-start | bytes 196
  18.6 56.8 %all-to-all-start = ((f32[16,3,64,128]{3,2,1,0:T(8,128)}), f32[16,3,64,128]{3,2,1,0:T(8,128)}, u32[]{:S(2)}, u32[]{:S(2)}) async-start(f32[16,3,64,128]{3,2,1,0:T(8,128)} %shard_map.67), calls=%async_computation | async-start | bytes 3145728 | tf_op jit(solution)/shard_map/all_to_all | solution.py:431
  31.6 38.8 %copy-start.1 = (f32[2,3,64,128]{3,2,1,0:T(8,128)}, f32[2,3,64,128]{3,2,1,0:T(8,128)S(1)}, u32[]{:S(2)}) copy-start(f32[2,3,64,128]{3,2,1,0:T(8,128)S(1)} %collective-permute-done.refs_0_.refs_1_) | copy-start | bytes 589828
  31.6 27.1 %collective-permute-start.5 = (f32[3,64,128]{2,1,0:T(8,128)S(1)}, f32[3,64,128]{2,1,0:T(8,128)S(1)}, u32[]{:S(2)}, u32[]{:S(2)}) collective-permute-start(f32[3,64,128]{2,1,0:T(8,128)S(1)} %get-tuple-element.22), channel_id=1, source_target_pairs={{0,25},{1,24},{2,27},{3,26},{4,29},{5,28},{6,31},{7,30},{8,17},{9,... | collective-permute-start | bytes 294920 | tf_op jit(solution)/shard_map/ppermute | solution.py:387
  35.4 35.0 %copy-start.2 = (f32[2,3,64,128]{3,2,1,0:T(8,128)}, f32[2,3,64,128]{3,2,1,0:T(8,128)S(1)}, u32[]{:S(2)}) copy-start(f32[2,3,64,128]{3,2,1,0:T(8,128)S(1)} %collective-permute-done.1.refs_1_.refs_2_) | copy-start | bytes 589828
  35.4 23.4 %collective-permute-start.6 = (f32[3,64,128]{2,1,0:T(8,128)S(1)}, f32[3,64,128]{2,1,0:T(8,128)S(1)}, u32[]{:S(2)}, u32[]{:S(2)}) collective-permute-start(f32[3,64,128]{2,1,0:T(8,128)S(1)} %get-tuple-element.23), channel_id=1, source_target_pairs={{0,26},{1,27},{2,24},{3,25},{4,30},{5,31},{6,28},{7,29},{8,18},{9,... | collective-permute-start | bytes 294920 | tf_op jit(solution)/shard_map/ppermute | solution.py:387
  43.4 27.0 %copy-start.3 = (f32[2,3,64,128]{3,2,1,0:T(8,128)}, f32[2,3,64,128]{3,2,1,0:T(8,128)S(1)}, u32[]{:S(2)}) copy-start(f32[2,3,64,128]{3,2,1,0:T(8,128)S(1)} %collective-permute-done.2.refs_2_.refs_3_) | copy-start | bytes 589828
  43.4 18.9 %collective-permute-start.7 = (f32[3,64,128]{2,1,0:T(8,128)S(1)}, f32[3,64,128]{2,1,0:T(8,128)S(1)}, u32[]{:S(2)}, u32[]{:S(2)}) collective-permute-start(f32[3,64,128]{2,1,0:T(8,128)S(1)} %get-tuple-element.24), channel_id=1, source_target_pairs={{0,27},{1,26},{2,25},{3,24},{4,31},{5,30},{6,29},{7,28},{8,19},{9,... | collective-permute-start | bytes 294920 | tf_op jit(solution)/shard_map/ppermute | solution.py:387
  46.5 23.9 %copy-start.4 = (f32[2,3,64,128]{3,2,1,0:T(8,128)}, f32[2,3,64,128]{3,2,1,0:T(8,128)S(1)}, u32[]{:S(2)}) copy-start(f32[2,3,64,128]{3,2,1,0:T(8,128)S(1)} %collective-permute-done.3.refs_3_.refs_4_) | copy-start | bytes 589828
  46.5 23.8 %collective-permute-start.12 = (f32[4,3,64,128]{3,2,1,0:T(8,128)S(1)}, f32[4,3,64,128]{3,2,1,0:T(8,128)S(1)}, u32[]{:S(2)}, u32[]{:S(2)}) collective-permute-start(f32[4,3,64,128]{3,2,1,0:T(8,128)S(1)} %pad_maximum_fusion), channel_id=1, source_target_pairs={{0,1},{1,0},{2,3},{3,2},{4,5},{5,4},{6,7},{7,6},{8,9},{9,8},{10,11... | collective-permute-start | bytes 1179656 | tf_op jit(solution)/shard_map/ppermute | solution.py:387
  48.6 15.8 %collective-permute-start.8 = (f32[3,64,128]{2,1,0:T(8,128)S(1)}, f32[3,64,128]{2,1,0:T(8,128)S(1)}, u32[]{:S(2)}, u32[]{:S(2)}) collective-permute-start(f32[3,64,128]{2,1,0:T(8,128)S(1)} %get-tuple-element.25), channel_id=1, source_target_pairs={{0,28},{1,29},{2,30},{3,31},{4,24},{5,25},{6,26},{7,27},{8,20},{9,... | collective-permute-start | bytes 294920 | tf_op jit(solution)/shard_map/ppermute | solution.py:387
  58.7 9.5 %collective-permute-start.9 = (f32[3,64,128]{2,1,0:T(8,128)S(1)}, f32[3,64,128]{2,1,0:T(8,128)S(1)}, u32[]{:S(2)}, u32[]{:S(2)}) collective-permute-start(f32[3,64,128]{2,1,0:T(8,128)S(1)} %get-tuple-element.26), channel_id=1, source_target_pairs={{0,29},{1,28},{2,31},{3,30},{4,25},{5,24},{6,27},{7,26},{8,21},{9,... | collective-permute-start | bytes 294920 | tf_op jit(solution)/shard_map/ppermute | solution.py:387
  58.7 9.4 %collective-permute-start.10 = (f32[3,64,128]{2,1,0:T(8,128)S(1)}, f32[3,64,128]{2,1,0:T(8,128)S(1)}, u32[]{:S(2)}, u32[]{:S(2)}) collective-permute-start(f32[3,64,128]{2,1,0:T(8,128)S(1)} %get-tuple-element.27), channel_id=1, source_target_pairs={{0,30},{1,31},{2,28},{3,29},{4,26},{5,27},{6,24},{7,25},{8,22},{9,... | collective-permute-start | bytes 294920 | tf_op jit(solution)/shard_map/ppermute | solution.py:387
  62.2 8.1 %collective-permute-start.11 = (f32[3,64,128]{2,1,0:T(8,128)S(1)}, f32[3,64,128]{2,1,0:T(8,128)S(1)}, u32[]{:S(2)}, u32[]{:S(2)}) collective-permute-start(f32[3,64,128]{2,1,0:T(8,128)S(1)} %get-tuple-element.28), channel_id=1, source_target_pairs={{0,31},{1,30},{2,29},{3,28},{4,27},{5,26},{6,25},{7,24},{8,23},{9,... | collective-permute-start | bytes 294920 | tf_op jit(solution)/shard_map/ppermute | solution.py:387

commit v8 on v7

--- a/solution.py
+++ b/solution.py
@@ -415,7 +415,7 @@
     singles = [(offset, flip) for offset in direct for flip in range(2)]
     for partner, array in zip(singles, leaving[len(relayed) :]):
         keep(send(array, *partner), [(None, partner)])
-    late = set(range(len(relayed) + 1, len(arrays) + 1))
+    late = set(range(1, len(arrays) + 1))
     for first, last in ((0, 4),):
         group = jnp.stack([got[1] for got in passing[first:last]])
         keep(

time: 94.7 us -> 94.5 us (level)
  no operation moved by 1% of the time
where the time goes in v8:
time: 94.5 us; the launch traced here: 94.2 us
  starting transfers between devices  42 us (44%)
  waiting for transfers between devices  23 us (24%)
  blocking collectives  14 us (15%)
  Pallas kernels  9.68 us (10%)
  local copies, waits for them, and re-layouts  3.08 us (3%)
  other arithmetic  1.93 us (2%)
    ppermute x13, starting transfers between devices, send(): return lax.ppermute(array, ('grp', 'swap'), pairs)  37.5 us
    ppermute x13, waiting for transfers between devices, send(): return lax.ppermute(array, ('grp', 'swap'), pairs)  18 us
    all_to_all x1, blocking collectives, chunk_shards(): lax.all_to_all(tiles, 'grp', split_axis=0, concat_axis=0, tiled=True, axi...  14 us
    pallas_call x3, Pallas kernels, on_device(): pl.pallas_call(kernel, in_specs=[pl.BlockSpec(memory_space=pltpu.SMEM)] +...  5.81 us
    all_to_all x1, waiting for transfers between devices, chunk_shards(): lax.all_to_all(near_chunks, ('grp', 'swap'), split_axis=0, concat_axis=0,...  5.04 us
    all_to_all x1, starting transfers between devices, chunk_shards(): lax.all_to_all(near_chunks, ('grp', 'swap'), split_axis=0, concat_axis=0,...  4.55 us
    pallas_call x1, Pallas kernels, composite(): pl.pallas_call(functools.partial(composite_kernel, picks, late), in_specs...  3.86 us
  transfers between devices with their start and end apart: 14, of which 5 were waited for; matrix products, arithmetic and copies ran while one was open for 3% of the time, Pallas kernels for 5%

profile of v8, /device:TPU:0, one launch (start us, length us, event | category | flops | bytes accessed | tf_op | source)
XLA Modules:
  0.0 94.2 jit_solution(8879154426224453811)
XLA Ops:
  0.0 0.1 pad_add_fusion.1.numbers_ref
  0.1 1.6 %copy-done = bf16[1,1,64,4,4096]{4,3,2,1,0:T(4,128)(2,1)S(1)} copy-done((bf16[1,1,64,4,4096]{4,3,2,1,0:T(4,128)(2,1)S(1)}, bf16[1,1,64,4,4096]{4,3,2,1,0:T(4,128)(2,1)}, u32[]{:S(2)}) %copy-start) | copy-done | bytes 2097176
  1.7 1.0 %shard_map.64 = (f32[2,3,64,128]{3,2,1,0:T(8,128)S(1)}, f32[2,3,64,128]{3,2,1,0:T(8,128)S(1)}) custom-call(s32[2]{0:T(128)S(1)} %pad_add_fusion.1.numbers_ref, bf16[64,4,4096]{2,1,0:T(4,128)(2,1)S(1)} %bitcast.32), custom_call_target="tpu_custom_call" | custom-call | tf_op jit(solution)/shard_map/pallas_call | solution.py:228
  2.7 4.1 %collective-permute-start = (f32[2,3,64,128]{3,2,1,0:T(8,128)S(1)}, f32[2,3,64,128]{3,2,1,0:T(8,128)S(1)}, u32[]{:S(2)}, u32[]{:S(2)}) collective-permute-start(f32[2,3,64,128]{3,2,1,0:T(8,128)S(1)} %get-tuple-element.17), channel_id=1, source_target_pairs={{0,16},{1,17},{2,18},{3,19},{4,20},{5,21},{6,22},{7,23},{8,24},{9,... | collective-permute-start | bytes 589832 | tf_op jit(solution)/shard_map/ppermute | solution.py:387
  6.8 0.0 collective-permute-start.1
  6.8 1.6 %shard_map.65 = (f32[2,3,64,128]{3,2,1,0:T(8,128)S(1)}, f32[2,3,64,128]{3,2,1,0:T(8,128)S(1)}, f32[3,64,128]{2,1,0:T(8,128)S(1)}, f32[3,64,128]{2,1,0:T(8,128)S(...) custom-call(s32[2]{0:T(128)S(1)} %pad_add_fusion.1.numbers_ref, ...), custom_call_target="tpu_custom_call" | custom-call | tf_op jit(solution)/shard_map/pallas_call | solution.py:228
  8.4 3.2 %collective-permute-start.4 = (f32[3,64,128]{2,1,0:T(8,128)S(1)}, f32[3,64,128]{2,1,0:T(8,128)S(1)}, u32[]{:S(2)}, u32[]{:S(2)}) collective-permute-start(f32[3,64,128]{2,1,0:T(8,128)S(1)} %get-tuple-element.21), channel_id=1, source_target_pairs={{0,24},{1,25},{2,26},{3,27},{4,28},{5,29},{6,30},{7,31},{8,16},{9,... | collective-permute-start | bytes 294920 | tf_op jit(solution)/shard_map/ppermute | solution.py:387
  11.6 0.9 collective-permute-start.2
  12.5 3.0 %collective-permute-start.3 = (f32[2,3,64,128]{3,2,1,0:T(8,128)S(1)}, f32[2,3,64,128]{3,2,1,0:T(8,128)S(1)}, u32[]{:S(2)}, u32[]{:S(2)}) collective-permute-start(f32[2,3,64,128]{3,2,1,0:T(8,128)S(1)} %get-tuple-element.20), channel_id=1, source_target_pairs={{0,22},{1,23},{2,20},{3,21},{4,18},{5,19},{6,16},{7,17},{8,30},{9,... | collective-permute-start | bytes 589832 | tf_op jit(solution)/shard_map/ppermute | solution.py:387
  15.4 3.2 %shard_map.67 = f32[16,3,64,128]{3,2,1,0:T(8,128)} custom-call(s32[2]{0:T(128)S(1)} %pad_add_fusion.1.numbers_ref, bf16[64,4,4096]{2,1,0:T(4,128)(2,1)S(1)} %bitcast.34), custom_call_target="tpu_custom_call" | custom-call | tf_op jit(solution)/shard_map/pallas_call | solution.py:228
  18.6 0.0 copy-start.4
  18.6 4.5 %all-to-all-start = ((f32[16,3,64,128]{3,2,1,0:T(8,128)}), f32[16,3,64,128]{3,2,1,0:T(8,128)}, u32[]{:S(2)}, u32[]{:S(2)}) async-start(f32[16,3,64,128]{3,2,1,0:T(8,128)} %shard_map.67), calls=%async_computation | async-start | bytes 3145728 | tf_op jit(solution)/shard_map/all_to_all | solution.py:431
  23.2 0.1 mul.44
  23.3 0.9 select_reduce_fusion
  24.2 0.1 reshape.87
  24.3 0.1 convert_element_type.8
  24.4 0.2 fusion
  24.7 0.1 pad_add_fusion
  24.8 0.1 broadcast_add_fusion
  24.8 6.8 %collective-permute-done.refs_0_.refs_1_ = f32[2,3,64,128]{3,2,1,0:T(8,128)S(1)} collective-permute-done((f32[2,3,64,128]{3,2,1,0:T(8,128)S(1)}, f32[2,3,64,128]{3,2,1,0:T(8,128)S(1)}, u32[]{:S(2)}, u32[]{:S(2)}) %collective-permute-start) | collective-permute-done | bytes 196640 | tf_op jit(solution)/shard_map/ppermute | solution.py:387
  31.6 3.8 %collective-permute-start.5 = (f32[3,64,128]{2,1,0:T(8,128)S(1)}, f32[3,64,128]{2,1,0:T(8,128)S(1)}, u32[]{:S(2)}, u32[]{:S(2)}) collective-permute-start(f32[3,64,128]{2,1,0:T(8,128)S(1)} %get-tuple-element.22), channel_id=1, source_target_pairs={{0,25},{1,24},{2,27},{3,26},{4,29},{5,28},{6,31},{7,30},{8,17},{9,... | collective-permute-start | bytes 294920 | tf_op jit(solution)/shard_map/ppermute | solution.py:387
  35.4 0.0 collective-permute-done.1.refs_1_.refs_2_
  35.4 2.7 %collective-permute-start.6 = (f32[3,64,128]{2,1,0:T(8,128)S(1)}, f32[3,64,128]{2,1,0:T(8,128)S(1)}, u32[]{:S(2)}, u32[]{:S(2)}) collective-permute-start(f32[3,64,128]{2,1,0:T(8,128)S(1)} %get-tuple-element.23), channel_id=1, source_target_pairs={{0,26},{1,27},{2,24},{3,25},{4,30},{5,31},{6,28},{7,29},{8,18},{9,... | collective-permute-start | bytes 294920 | tf_op jit(solution)/shard_map/ppermute | solution.py:387
  38.1 5.2 %collective-permute-done.2.refs_2_.refs_3_ = f32[2,3,64,128]{3,2,1,0:T(8,128)S(1)} collective-permute-done((f32[2,3,64,128]{3,2,1,0:T(8,128)S(1)}, f32[2,3,64,128]{3,2,1,0:T(8,128)S(1)}, u32[]{:S(2)}, u32[]{:S(2)}) %collective-permute-start.2) | collective-permute-done | bytes 196640 | tf_op jit(solution)/shard_map/ppermute | solution.py:387
  43.3 3.1 %collective-permute-start.7 = (f32[3,64,128]{2,1,0:T(8,128)S(1)}, f32[3,64,128]{2,1,0:T(8,128)S(1)}, u32[]{:S(2)}, u32[]{:S(2)}) collective-permute-start(f32[3,64,128]{2,1,0:T(8,128)S(1)} %get-tuple-element.24), channel_id=1, source_target_pairs={{0,27},{1,26},{2,25},{3,24},{4,31},{5,30},{6,29},{7,28},{8,19},{9,... | collective-permute-start | bytes 294920 | tf_op jit(solution)/shard_map/ppermute | solution.py:387
  46.4 0.0 collective-permute-done.3.refs_3_.refs_4_
  46.5 1.3 %collective-permute-start.12 = (f32[4,3,64,128]{3,2,1,0:T(8,128)S(1)}, f32[4,3,64,128]{3,2,1,0:T(8,128)S(1)}, u32[]{:S(2)}, u32[]{:S(2)}) collective-permute-start(f32[4,3,64,128]{3,2,1,0:T(8,128)S(1)} %pad_maximum_fusion), channel_id=1, source_target_pairs={{0,1},{1,0},{2,3},{3,2},{4,5},{5,4},{6,7},{7,6},{8,9},{9,8},{10,11... | collective-permute-start | bytes 1179656 | tf_op jit(solution)/shard_map/ppermute | solution.py:387
  47.8 0.1 iota_compare_fusion.3
  47.8 0.1 copy.15
  47.9 0.6 select_reduce_fusion.1
  48.5 0.0 collective-permute-done.4.refs_4_.refs_5_
  48.6 10.1 %collective-permute-start.8 = (f32[3,64,128]{2,1,0:T(8,128)S(1)}, f32[3,64,128]{2,1,0:T(8,128)S(1)}, u32[]{:S(2)}, u32[]{:S(2)}) collective-permute-start(f32[3,64,128]{2,1,0:T(8,128)S(1)} %get-tuple-element.25), channel_id=1, source_target_pairs={{0,28},{1,29},{2,30},{3,31},{4,24},{5,25},{6,26},{7,27},{8,20},{9,... | collective-permute-start | bytes 294920 | tf_op jit(solution)/shard_map/ppermute | solution.py:387
  58.7 0.0 collective-permute-done.5.refs_5_.refs_6_
  58.7 0.0 collective-permute-start.9
  58.7 0.0 collective-permute-done.6.refs_6_.refs_7_
  58.7 3.5 %collective-permute-start.10 = (f32[3,64,128]{2,1,0:T(8,128)S(1)}, f32[3,64,128]{2,1,0:T(8,128)S(1)}, u32[]{:S(2)}, u32[]{:S(2)}) collective-permute-start(f32[3,64,128]{2,1,0:T(8,128)S(1)} %get-tuple-element.27), channel_id=1, source_target_pairs={{0,30},{1,31},{2,28},{3,29},{4,26},{5,27},{6,24},{7,25},{8,22},{9,... | collective-permute-start | bytes 294920 | tf_op jit(solution)/shard_map/ppermute | solution.py:387
  62.2 0.0 collective-permute-done.7.refs_7_.refs_8_
  62.2 1.9 %collective-permute-start.11 = (f32[3,64,128]{2,1,0:T(8,128)S(1)}, f32[3,64,128]{2,1,0:T(8,128)S(1)}, u32[]{:S(2)}, u32[]{:S(2)}) collective-permute-start(f32[3,64,128]{2,1,0:T(8,128)S(1)} %get-tuple-element.28), channel_id=1, source_target_pairs={{0,31},{1,30},{2,29},{3,28},{4,27},{5,26},{6,25},{7,24},{8,23},{9,... | collective-permute-start | bytes 294920 | tf_op jit(solution)/shard_map/ppermute | solution.py:387
  64.1 0.1 mul.47.places_ref
  64.2 0.1 reshape.88.slots_ref
  64.4 0.0 collective-permute-done.8.refs_8_.refs_9_
  64.4 3.8 %collective-permute-done.9.refs_9_.refs_10_ = f32[3,64,128]{2,1,0:T(8,128)S(1)} collective-permute-done((f32[3,64,128]{2,1,0:T(8,128)S(1)}, f32[3,64,128]{2,1,0:T(8,128)S(1)}, u32[]{:S(2)}, u32[]{:S(2)}) %collective-permute-start.9) | collective-permute-done | bytes 98336 | tf_op jit(solution)/shard_map/ppermute | solution.py:387
  68.2 0.0 collective-permute-done.10.refs_10_.refs_11_
  68.2 2.2 %collective-permute-done.11.refs_11_.refs_12_ = f32[3,64,128]{2,1,0:T(8,128)S(1)} collective-permute-done((f32[3,64,128]{2,1,0:T(8,128)S(1)}, f32[3,64,128]{2,1,0:T(8,128)S(1)}, u32[]{:S(2)}, u32[]{:S(2)}) %collective-permute-start.11) | collective-permute-done | bytes 98336 | tf_op jit(solution)/shard_map/ppermute | solution.py:387
  70.3 5.0 %all-to-all-done.refs_0_ = f32[16,3,64,128]{3,2,1,0:T(8,128)} async-done(((f32[16,3,64,128]{3,2,1,0:T(8,128)}), f32[16,3,64,128]{3,2,1,0:T(8,128)}, u32[]{:S(2)}, u32[]{:S(2)}) %all-to-all-start) | async-done | bytes 1572896 | tf_op jit(solution)/shard_map/all_to_all | solution.py:431
  75.4 3.9 %shard_map.68 = f32[16,3,8,128]{3,2,1,0:T(8,128)S(1)} custom-call(s32[256]{0:T(256)S(1)} %mul.47.places_ref, f32[1,2048]{1,0:T(1,128)S(1)} %shard_map.66.slots_ref, f32[16,3,64,128]{3,2,1,0:T(8,128)} %all-to-all-done.refs_0_, f32[2,3,64,128]{3,2,1,0:T(8,128)S(1)} %collective-permute-done.refs_0_.refs_1_, ...), custom_call_target="tpu_custom_call" | custom-call | tf_op jit(solution)/shard_map/pallas_call | solution.py:329
  79.2 14.0 %all_to_all.10 = f32[16,3,8,128]{3,2,1,0:T(8,128)S(1)} all-to-all(f32[16,3,8,128]{3,2,1,0:T(8,128)S(1)} %shard_map.68), channel_id=1, replica_groups={{0,8,16,24,2,10,18,26,4,12,20,28,6,14,22,30},{1,9,17,25,3,11,19,27,5,13..., dimensions={0} | all-to-all | bytes 393216 | tf_op jit(solution)/shard_map/all_to_all | solution.py:453
  93.3 0.9 copy.19
  (26 shorter events, 0.2 us)
Async XLA Ops:
  0.1 1.6 %copy-start = (bf16[1,1,64,4,4096]{4,3,2,1,0:T(4,128)(2,1)S(1)}, bf16[1,1,64,4,4096]{4,3,2,1,0:T(4,128)(2,1)}, u32[]{:S(2)}) copy-start(bf16[1,1,64,4,4096]{4,3,2,1,0:T(4,128)(2,1)} %param.6) | copy-start | bytes 6291460
  2.7 28.9 %collective-permute-start = (f32[2,3,64,128]{3,2,1,0:T(8,128)S(1)}, f32[2,3,64,128]{3,2,1,0:T(8,128)S(1)}, u32[]{:S(2)}, u32[]{:S(2)}) collective-permute-start(f32[2,3,64,128]{3,2,1,0:T(8,128)S(1)} %get-tuple-element.17), channel_id=1, source_target_pairs={{0,16},{1,17},{2,18},{3,19},{4,20},{5,21},{6,22},{7,23},{8,24},{9,... | collective-permute-start | bytes 589832 | tf_op jit(solution)/shard_map/ppermute | solution.py:387
  6.8 28.6 %collective-permute-start.1 = (f32[2,3,64,128]{3,2,1,0:T(8,128)S(1)}, f32[2,3,64,128]{3,2,1,0:T(8,128)S(1)}, u32[]{:S(2)}, u32[]{:S(2)}) collective-permute-start(f32[2,3,64,128]{3,2,1,0:T(8,128)S(1)} %get-tuple-element.18), channel_id=1, source_target_pairs={{0,18},{1,19},{2,16},{3,17},{4,22},{5,23},{6,20},{7,21},{8,26},{9,... | collective-permute-start | bytes 589832 | tf_op jit(solution)/shard_map/ppermute | solution.py:387
  8.4 40.1 %collective-permute-start.4 = (f32[3,64,128]{2,1,0:T(8,128)S(1)}, f32[3,64,128]{2,1,0:T(8,128)S(1)}, u32[]{:S(2)}, u32[]{:S(2)}) collective-permute-start(f32[3,64,128]{2,1,0:T(8,128)S(1)} %get-tuple-element.21), channel_id=1, source_target_pairs={{0,24},{1,25},{2,26},{3,27},{4,28},{5,29},{6,30},{7,31},{8,16},{9,... | collective-permute-start | bytes 294920 | tf_op jit(solution)/shard_map/ppermute | solution.py:387
  11.6 31.7 %collective-permute-start.2 = (f32[2,3,64,128]{3,2,1,0:T(8,128)S(1)}, f32[2,3,64,128]{3,2,1,0:T(8,128)S(1)}, u32[]{:S(2)}, u32[]{:S(2)}) collective-permute-start(f32[2,3,64,128]{3,2,1,0:T(8,128)S(1)} %get-tuple-element.19), channel_id=1, source_target_pairs={{0,20},{1,21},{2,22},{3,23},{4,16},{5,17},{6,18},{7,19},{8,28},{9,... | collective-permute-start | bytes 589832 | tf_op jit(solution)/shard_map/ppermute | solution.py:387
  12.5 34.0 %collective-permute-start.3 = (f32[2,3,64,128]{3,2,1,0:T(8,128)S(1)}, f32[2,3,64,128]{3,2,1,0:T(8,128)S(1)}, u32[]{:S(2)}, u32[]{:S(2)}) collective-permute-start(f32[2,3,64,128]{3,2,1,0:T(8,128)S(1)} %get-tuple-element.20), channel_id=1, source_target_pairs={{0,22},{1,23},{2,20},{3,21},{4,18},{5,19},{6,16},{7,17},{8,30},{9,... | collective-permute-start | bytes 589832 | tf_op jit(solution)/shard_map/ppermute | solution.py:387
  18.6 4.6 %copy-start.5 = (s32[128]{0:T(128)S(1)}, s32[128]{0:T(128)}, u32[]{:S(2)}) copy-start(s32[128]{0:T(128)} %param.8) | copy-start | bytes 1540
  18.6 4.7 %copy-start.1 = (s32[2,16,64]{2,1,0:T(8,128)S(1)}, s32[2,16,64]{2,1,0:T(8,128)}, u32[]{:S(2)}) copy-start(s32[2,16,64]{2,1,0:T(8,128)} %param.7) | copy-start | bytes 24580
  18.6 5.6 %copy-start.2 = (s32[2,128]{1,0:T(2,128)S(1)}, s32[2,128]{1,0:T(2,128)}, u32[]{:S(2)}) copy-start(s32[2,128]{1,0:T(2,128)} %param.9) | copy-start | bytes 3076
  18.6 6.1 %copy-start.3 = (s32[16]{0:T(128)S(1)}, s32[16]{0:T(128)}, u32[]{:S(2)}) copy-start(s32[16]{0:T(128)} %constant.102.clone) | copy-start | bytes 196
  18.6 6.1 %copy-start.4 = (s32[16]{0:T(128)S(1)}, s32[16]{0:T(128)}, u32[]{:S(2)}) copy-start(s32[16]{0:T(128)} %constant.101.clone) | copy-start | bytes 196
  18.6 56.8 %all-to-all-start = ((f32[16,3,64,128]{3,2,1,0:T(8,128)}), f32[16,3,64,128]{3,2,1,0:T(8,128)}, u32[]{:S(2)}, u32[]{:S(2)}) async-start(f32[16,3,64,128]{3,2,1,0:T(8,128)} %shard_map.67), calls=%async_computation | async-start | bytes 3145728 | tf_op jit(solution)/shard_map/all_to_all | solution.py:431
  31.6 27.1 %collective-permute-start.5 = (f32[3,64,128]{2,1,0:T(8,128)S(1)}, f32[3,64,128]{2,1,0:T(8,128)S(1)}, u32[]{:S(2)}, u32[]{:S(2)}) collective-permute-start(f32[3,64,128]{2,1,0:T(8,128)S(1)} %get-tuple-element.22), channel_id=1, source_target_pairs={{0,25},{1,24},{2,27},{3,26},{4,29},{5,28},{6,31},{7,30},{8,17},{9,... | collective-permute-start | bytes 294920 | tf_op jit(solution)/shard_map/ppermute | solution.py:387
  35.4 23.4 %collective-permute-start.6 = (f32[3,64,128]{2,1,0:T(8,128)S(1)}, f32[3,64,128]{2,1,0:T(8,128)S(1)}, u32[]{:S(2)}, u32[]{:S(2)}) collective-permute-start(f32[3,64,128]{2,1,0:T(8,128)S(1)} %get-tuple-element.23), channel_id=1, source_target_pairs={{0,26},{1,27},{2,24},{3,25},{4,30},{5,31},{6,28},{7,29},{8,18},{9,... | collective-permute-start | bytes 294920 | tf_op jit(solution)/shard_map/ppermute | solution.py:387
  43.3 18.9 %collective-permute-start.7 = (f32[3,64,128]{2,1,0:T(8,128)S(1)}, f32[3,64,128]{2,1,0:T(8,128)S(1)}, u32[]{:S(2)}, u32[]{:S(2)}) collective-permute-start(f32[3,64,128]{2,1,0:T(8,128)S(1)} %get-tuple-element.24), channel_id=1, source_target_pairs={{0,27},{1,26},{2,25},{3,24},{4,31},{5,30},{6,29},{7,28},{8,19},{9,... | collective-permute-start | bytes 294920 | tf_op jit(solution)/shard_map/ppermute | solution.py:387
  46.5 23.8 %collective-permute-start.12 = (f32[4,3,64,128]{3,2,1,0:T(8,128)S(1)}, f32[4,3,64,128]{3,2,1,0:T(8,128)S(1)}, u32[]{:S(2)}, u32[]{:S(2)}) collective-permute-start(f32[4,3,64,128]{3,2,1,0:T(8,128)S(1)} %pad_maximum_fusion), channel_id=1, source_target_pairs={{0,1},{1,0},{2,3},{3,2},{4,5},{5,4},{6,7},{7,6},{8,9},{9,8},{10,11... | collective-permute-start | bytes 1179656 | tf_op jit(solution)/shard_map/ppermute | solution.py:387
  48.6 15.8 %collective-permute-start.8 = (f32[3,64,128]{2,1,0:T(8,128)S(1)}, f32[3,64,128]{2,1,0:T(8,128)S(1)}, u32[]{:S(2)}, u32[]{:S(2)}) collective-permute-start(f32[3,64,128]{2,1,0:T(8,128)S(1)} %get-tuple-element.25), channel_id=1, source_target_pairs={{0,28},{1,29},{2,30},{3,31},{4,24},{5,25},{6,26},{7,27},{8,20},{9,... | collective-permute-start | bytes 294920 | tf_op jit(solution)/shard_map/ppermute | solution.py:387
  58.7 9.5 %collective-permute-start.9 = (f32[3,64,128]{2,1,0:T(8,128)S(1)}, f32[3,64,128]{2,1,0:T(8,128)S(1)}, u32[]{:S(2)}, u32[]{:S(2)}) collective-permute-start(f32[3,64,128]{2,1,0:T(8,128)S(1)} %get-tuple-element.26), channel_id=1, source_target_pairs={{0,29},{1,28},{2,31},{3,30},{4,25},{5,24},{6,27},{7,26},{8,21},{9,... | collective-permute-start | bytes 294920 | tf_op jit(solution)/shard_map/ppermute | solution.py:387
  58.7 9.4 %collective-permute-start.10 = (f32[3,64,128]{2,1,0:T(8,128)S(1)}, f32[3,64,128]{2,1,0:T(8,128)S(1)}, u32[]{:S(2)}, u32[]{:S(2)}) collective-permute-start(f32[3,64,128]{2,1,0:T(8,128)S(1)} %get-tuple-element.27), channel_id=1, source_target_pairs={{0,30},{1,31},{2,28},{3,29},{4,26},{5,27},{6,24},{7,25},{8,22},{9,... | collective-permute-start | bytes 294920 | tf_op jit(solution)/shard_map/ppermute | solution.py:387
  62.2 8.1 %collective-permute-start.11 = (f32[3,64,128]{2,1,0:T(8,128)S(1)}, f32[3,64,128]{2,1,0:T(8,128)S(1)}, u32[]{:S(2)}, u32[]{:S(2)}) collective-permute-start(f32[3,64,128]{2,1,0:T(8,128)S(1)} %get-tuple-element.28), channel_id=1, source_target_pairs={{0,31},{1,30},{2,29},{3,28},{4,27},{5,26},{6,25},{7,24},{8,23},{9,... | collective-permute-start | bytes 294920 | tf_op jit(solution)/shard_map/ppermute | solution.py:387
